TPU v7x, 256 devices: a whole 4x4x8 slice. The times are simulated.
256 devices in a mesh: src: 16 (over x, y_lo, core), tgt: 16 (over z, y_hi).
Axes of the slice: x: 4, y: 4 (y_hi: 2, y_lo: 2; y = y_hi * 2 + y_lo), z: 8, core: 2. Of those that a mesh axis runs over, the one named last changes fastest.
Arguments:
- src_feat: bfloat16 [32768, 256], P(('src', 'tgt')), may hold values from -90 to 90
- tgt_feat: bfloat16 [32768, 256], P(('tgt', 'src')), may hold values from -30 to 30
- src_weight: float32 [32768], P('src'), may hold values from 0.2 to 5
- tgt_weight: float32 [32768], P('tgt'), may hold values from 0.2 to 5
- cand: int32 [256, 16, 6], P('src', 'tgt'), may hold values from 0 to 15, as said below
- counts: int32 [256, 16], P('src', 'tgt'), may hold values from 1 to 6, as said below
Outputs:
- src_potential: float32 [32768], P('src')
- tgt_potential: float32 [32768], P('tgt')
Inputs may be any that keep to these rules, and one draw needn't show every extreme that they name: For each source block b and target shard t the entries cand[b, t, k] with k < counts[b, t] name distinct blocks, and cand[b, t, 0] equals b modulo 16; slots from counts[b, t] on are not used. `counts`: 6 is reached in every draw.
All inputs are finite; a program needn't handle non-finite values.
Results may differ from a plain program's by a relative error of at most 0.0003.
Values may be sent and summed in bfloat16 or wider, within the bound.
No kernel may reach another device: no remote copies, remote signals or barrier semaphores. Data moves between devices by JAX's collectives and lax.ppermute only.
A program may use at most 64 MiB of HBM per device.

v0:
```python
import math

import jax
import jax.numpy as jnp
from jax import lax
from jax.sharding import PartitionSpec as P

ITERS = 3


def merged(value, axis, combine):
    everything = jax.tree.map(lambda part: lax.all_gather(part, axis), value)
    initial = jax.tree.map(lambda part: part[0], everything)

    def step(k, so_far):
        return combine(so_far, jax.tree.map(lambda part: part[k], everything))

    return lax.fori_loop(1, lax.axis_size(axis), step, initial)


def combine_lse(left_pair, right_pair):
    highest = jnp.maximum(left_pair[0], right_pair[0])
    totals = left_pair[1] * jnp.exp(left_pair[0] - highest) + right_pair[1] * jnp.exp(
        right_pair[0] - highest
    )
    return (highest, totals)


def finish_rows(highest, totals, weight):
    highest, totals = merged((highest, totals), "tgt", combine_lse)
    return jnp.log(weight) - (highest + jnp.log(totals))


def finish_cols(highest, totals, weight):
    highest, totals = merged((highest, totals), "src", combine_lse)
    return jnp.log(weight) - (highest + jnp.log(totals))


def on_device(src_feat, tgt_feat, src_weight, tgt_weight, cand, counts):
    source_rows = lax.all_gather(src_feat, "tgt", axis=0, tiled=True)
    target_rows = lax.all_gather(tgt_feat, "src", axis=0, tiled=True)
    block_count = cand.shape[0]
    slot_count = cand.shape[2]
    block_rows = source_rows.shape[0] // block_count
    feature_dim = source_rows.shape[1]
    target_count = target_rows.shape[0] // block_rows
    group_size = 4
    group_count = block_count // group_size
    scale = 1.0 / math.sqrt(feature_dim)
    local_ids = cand[:, 0, :]
    usable = jnp.arange(slot_count, dtype=jnp.int32)[None, :] < counts[:, 0][:, None]
    source_groups = source_rows.reshape(group_count, group_size, block_rows, feature_dim)
    target_tiles = target_rows.reshape(target_count, block_rows, feature_dim)
    cand_groups = local_ids.reshape(group_count, group_size, slot_count)
    usable_groups = usable.reshape(group_count, group_size, slot_count)
    group_ids = jnp.arange(group_count, dtype=jnp.int32)

    def make_scores(position):
        picked = target_tiles[cand_groups[position]]
        products = jnp.einsum(
            "grf,gkcf->grkc", source_groups[position], picked, preferred_element_type=jnp.float32
        )
        return products * scale

    def row_stats(scores, position, target_dual):
        shifts = target_dual[cand_groups[position]]
        allowed = usable_groups[position][:, None, :, None]
        shifted = jnp.where(allowed, scores + shifts[:, None, :, :], -jnp.inf)
        highest = jnp.max(shifted, axis=(2, 3))
        totals = jnp.sum(jnp.exp(shifted - highest[:, :, None, None]), axis=(2, 3))
        return (highest, totals)

    def col_stats(scores, position, source_dual):
        shifts = source_dual.reshape(group_count, group_size, block_rows)[position]
        allowed = usable_groups[position][:, None, :, None]
        shifted = jnp.where(allowed, scores + shifts[:, :, None, None], -jnp.inf)
        highest = jnp.max(shifted, axis=1)
        slot_usable = usable_groups[position][:, :, None]
        safe_high = jnp.where(slot_usable, highest, 0.0)
        totals = jnp.sum(jnp.exp(shifted - safe_high[:, None, :, :]), axis=1)
        return (jnp.where(slot_usable, highest, -jnp.inf), totals)

    def sweep(stat_fn, dual_values):

        def from_fresh(position):
            return stat_fn(make_scores(position), position, dual_values)

        return lax.map(from_fresh, group_ids)

    flat_ids = local_ids.reshape(-1)
    flat_usable = usable.reshape(-1)[:, None]
    one_hot = (
        flat_ids[:, None] == jnp.arange(target_count, dtype=jnp.int32)[None, :]
    ) & flat_usable
    one_hot_f = one_hot.astype(jnp.float32)
    target_dual = jnp.zeros((target_count * block_rows,), jnp.float32)
    source_dual = jnp.zeros((block_count * block_rows,), jnp.float32)
    for iteration in range(ITERS):
        highest, totals = sweep(row_stats, target_dual.reshape(target_count, block_rows))
        source_dual = finish_rows(highest.reshape(-1), totals.reshape(-1), src_weight)
        col_high, col_totals = sweep(col_stats, source_dual)
        col_high = col_high.reshape(block_count * slot_count, block_rows)
        col_totals = col_totals.reshape(block_count * slot_count, block_rows)
        highest_all = jnp.max(
            jnp.where(one_hot[:, :, None], col_high[:, None, :], -jnp.inf), axis=0
        )
        shifted_high = jnp.where(flat_usable, col_high, 0.0) - highest_all[flat_ids]
        terms = jnp.where(flat_usable, col_totals * jnp.exp(shifted_high), 0.0)
        summed = jnp.einsum(
            "nq,nc->qc",
            one_hot_f,
            terms,
            precision=lax.Precision.HIGHEST,
            preferred_element_type=jnp.float32,
        )
        target_dual = finish_cols(highest_all.reshape(-1), summed.reshape(-1), tgt_weight)
    return (source_dual, target_dual)


def solution(mesh):
    placed = (
        P(("src", "tgt"), None),
        P(("tgt", "src"), None),
        P("src"),
        P("tgt"),
        P("src", "tgt", None),
        P("src", "tgt"),
    )
    return jax.shard_map(
        on_device, mesh=mesh, in_specs=placed, out_specs=(P("src"), P("tgt")), check_vma=False
    )
```

profile of v0, /device:TPU:1, one launch (start us, length us, event | category | flops | bytes accessed | tf_op | source)
XLA Modules:
  0.0 621.1 jit_solution(2698581006033638543)
XLA Ops:
  12.6 77.0 %all-gather.15.cloned.1.call-done = bf16[2048,256]{1,0:T(8,128)(2,1)} async-done(((bf16[128,256]{1,0:T(8,128)(2,1)}), bf16[2048,256]{1,0:T(8,128)(2,1)}) %all-gather.15.cloned.1.call-update) | async-done | bytes 1048592 | tf_op jit(solution)/shard_map/all_gather | solution.py:40
  89.5 37.5 %all-gather.17.cloned.1.call-done = bf16[2048,256]{1,0:T(8,128)(2,1)} async-done(((bf16[128,256]{1,0:T(8,128)(2,1)}), bf16[2048,256]{1,0:T(8,128)(2,1)}) %all-gather.17.cloned.1.call-update) | async-done | bytes 1048592 | tf_op jit(solution)/shard_map/all_gather | solution.py:41
  127.0 27.7 %while.174 = (s32[]{:T(128)}, f32[4,4,128]{2,1,0:T(4,128)S(1)}, f32[4,4,128]{2,1,0:T(4,128)S(1)}, s32[4]{0:T(128)S(1)}, pred[4,4,6]{2,1,0:T(4,128)(4,1)S(1)}, /*...) while((s32[]{:T(128)}, f32[4,4,128]{2,1,0:T(4,128)S(1)}, ...), condition=%wide.region_3.4_spmd, body=%wide.region_0.3_spmd.sunk | while | flops 203685968 | bytes 8215455 | solution.py:88
  129.6 1.9 gather_fusion.1
  136.6 1.9 gather_fusion.1
  143.5 1.9 gather_fusion.1
  150.4 1.9 gather_fusion.1
  154.7 34.6 %all-gather = f32[16,1,2048]{2,1,0:T(1,128)S(1)} all-gather(f32[1,1,2048]{2,1,0:T(1,128)S(1)} %bitcast.399), channel_id=1, replica_groups=mesh['src'=16,'tgt'=16] {'tgt'}, dimensions={0}, use_global_device_ids=true | all-gather | bytes 139264 | tf_op jit(solution)/shard_map/all_gather | solution.py:12
  189.4 29.4 %all-gather.1 = f32[16,1,2048]{2,1,0:T(1,128)S(1)} all-gather(f32[1,1,2048]{2,1,0:T(1,128)S(1)} %bitcast.400), channel_id=1, replica_groups=mesh['src'=16,'tgt'=16] {'tgt'}, dimensions={0}, use_global_device_ids=true | all-gather | bytes 139264 | tf_op jit(solution)/shard_map/all_gather | solution.py:12
  219.9 22.5 %while.176 = (s32[]{:T(128)}, f32[4,4,6,128]{3,2,1,0:T(8,128)S(1)}, f32[4,4,6,128]{3,2,1,0:T(8,128)S(1)}, s32[4]{0:T(128)S(1)}, pred[4,4,6]{2,1,0:T(4,128)(4,1)S...) while((s32[]{:T(128)}, f32[4,4,6,128]{3,2,1,0:T(8,128)S(1)}, ...), condition=%wide.region_9.10_spmd, body=%wide.region_6.9_spmd.sunk | while | flops 203686992 | bytes 8265047 | solution.py:88
  243.6 31.9 %all-gather.3 = f32[16,1,2048]{2,1,0:T(1,128)S(1)} all-gather(f32[1,1,2048]{2,1,0:T(1,128)S(1)} %bitcast.406), channel_id=1, replica_groups=mesh['src'=16,'tgt'=16] {'src'}, dimensions={0}, use_global_device_ids=true | all-gather | bytes 139264 | tf_op jit(solution)/shard_map/all_gather | solution.py:12
  275.5 16.9 %all-gather.2 = f32[16,1,2048]{2,1,0:T(1,128)S(1)} all-gather(f32[1,1,2048]{2,1,0:T(1,128)S(1)} %bitcast.357), channel_id=1, replica_groups=mesh['src'=16,'tgt'=16] {'src'}, dimensions={0}, use_global_device_ids=true | all-gather | bytes 139264 | tf_op jit(solution)/shard_map/all_gather | solution.py:12
  293.6 23.7 %while.178 = (s32[]{:T(128)}, f32[4,4,128]{2,1,0:T(4,128)S(1)}, f32[4,4,128]{2,1,0:T(4,128)S(1)}, s32[4]{0:T(128)S(1)}, pred[4,4,6]{2,1,0:T(4,128)(4,1)S(1)}, /*...) while((s32[]{:T(128)}, f32[4,4,128]{2,1,0:T(4,128)S(1)}, ...), condition=%wide.region_16.17_spmd, body=%wide.region_13.16_spmd.sunk | while | flops 203685968 | bytes 8207259 | solution.py:88
  317.4 32.8 %all-gather.4 = f32[16,1,2048]{2,1,0:T(1,128)S(1)} all-gather(f32[1,1,2048]{2,1,0:T(1,128)S(1)} %bitcast.401), channel_id=1, replica_groups=mesh['src'=16,'tgt'=16] {'tgt'}, dimensions={0}, use_global_device_ids=true | all-gather | bytes 139264 | tf_op jit(solution)/shard_map/all_gather | solution.py:12
  350.2 29.3 %all-gather.5 = f32[16,1,2048]{2,1,0:T(1,128)S(1)} all-gather(f32[1,1,2048]{2,1,0:T(1,128)S(1)} %bitcast.402), channel_id=1, replica_groups=mesh['src'=16,'tgt'=16] {'tgt'}, dimensions={0}, use_global_device_ids=true | all-gather | bytes 139264 | tf_op jit(solution)/shard_map/all_gather | solution.py:12
  380.6 22.5 %while.180 = (s32[]{:T(128)}, f32[4,4,6,128]{3,2,1,0:T(8,128)S(1)}, f32[4,4,6,128]{3,2,1,0:T(8,128)S(1)}, s32[4]{0:T(128)S(1)}, pred[4,4,6]{2,1,0:T(4,128)(4,1)S...) while((s32[]{:T(128)}, f32[4,4,6,128]{3,2,1,0:T(8,128)S(1)}, ...), condition=%wide.region_22.23_spmd, body=%wide.region_19.22_spmd.sunk | while | flops 203686992 | bytes 8265047 | solution.py:88
  404.3 31.5 %all-gather.7 = f32[16,1,2048]{2,1,0:T(1,128)S(1)} all-gather(f32[1,1,2048]{2,1,0:T(1,128)S(1)} %bitcast.407), channel_id=1, replica_groups=mesh['src'=16,'tgt'=16] {'src'}, dimensions={0}, use_global_device_ids=true | all-gather | bytes 139264 | tf_op jit(solution)/shard_map/all_gather | solution.py:12
  435.8 17.2 %all-gather.6 = f32[16,1,2048]{2,1,0:T(1,128)S(1)} all-gather(f32[1,1,2048]{2,1,0:T(1,128)S(1)} %bitcast.356), channel_id=1, replica_groups=mesh['src'=16,'tgt'=16] {'src'}, dimensions={0}, use_global_device_ids=true | all-gather | bytes 139264 | tf_op jit(solution)/shard_map/all_gather | solution.py:12
  454.2 23.7 %while.182 = (s32[]{:T(128)}, f32[4,4,128]{2,1,0:T(4,128)S(1)}, f32[4,4,128]{2,1,0:T(4,128)S(1)}, s32[4]{0:T(128)S(1)}, pred[4,4,6]{2,1,0:T(4,128)(4,1)S(1)}, /*...) while((s32[]{:T(128)}, f32[4,4,128]{2,1,0:T(4,128)S(1)}, ...), condition=%wide.region_29.30_spmd, body=%wide.region_26.29_spmd.sunk | while | flops 203685968 | bytes 8207259 | solution.py:88
  477.9 32.6 %all-gather.8 = f32[16,1,2048]{2,1,0:T(1,128)S(1)} all-gather(f32[1,1,2048]{2,1,0:T(1,128)S(1)} %bitcast.403), channel_id=1, replica_groups=mesh['src'=16,'tgt'=16] {'tgt'}, dimensions={0}, use_global_device_ids=true | all-gather | bytes 139264 | tf_op jit(solution)/shard_map/all_gather | solution.py:12
  510.6 29.4 %all-gather.9 = f32[16,1,2048]{2,1,0:T(1,128)S(1)} all-gather(f32[1,1,2048]{2,1,0:T(1,128)S(1)} %bitcast.404), channel_id=1, replica_groups=mesh['src'=16,'tgt'=16] {'tgt'}, dimensions={0}, use_global_device_ids=true | all-gather | bytes 139264 | tf_op jit(solution)/shard_map/all_gather | solution.py:12
  541.1 21.6 %while.184 = (s32[]{:T(128)}, f32[4,4,6,128]{3,2,1,0:T(8,128)S(1)}, f32[4,4,6,128]{3,2,1,0:T(8,128)S(1)}, s32[4]{0:T(128)S(1)}, pred[4,4,6]{2,1,0:T(4,128)(4,1)S...) while((s32[]{:T(128)}, f32[4,4,6,128]{3,2,1,0:T(8,128)S(1)}, ...), condition=%wide.region_35.36_spmd, body=%wide.region_32.35_spmd.sunk | while | flops 203686992 | bytes 8265047 | solution.py:88
  564.0 31.3 %all-gather.11 = f32[16,1,2048]{2,1,0:T(1,128)S(1)} all-gather(f32[1,1,2048]{2,1,0:T(1,128)S(1)} %bitcast.405), channel_id=1, replica_groups=mesh['src'=16,'tgt'=16] {'src'}, dimensions={0}, use_global_device_ids=true | all-gather | bytes 139264 | tf_op jit(solution)/shard_map/all_gather | solution.py:12
  595.3 17.2 %all-gather.10 = f32[16,1,2048]{2,1,0:T(1,128)S(1)} all-gather(f32[1,1,2048]{2,1,0:T(1,128)S(1)} %bitcast.355), channel_id=1, replica_groups=mesh['src'=16,'tgt'=16] {'src'}, dimensions={0}, use_global_device_ids=true | all-gather | bytes 139264 | tf_op jit(solution)/shard_map/all_gather | solution.py:12
  (537 shorter events, 103.8 us)
Async XLA Ops:
  7.2 82.4 %all-gather.15.cloned.1.call-start = ((), (), s32[]{:S(2)}) async-start(), calls=%async_computation | async-start | bytes 1114112 | tf_op jit(solution)/shard_map/all_gather | solution.py:40
  7.9 119.1 %all-gather.17.cloned.1.call-start = ((), (), s32[]{:S(2)}) async-start(), calls=%async_computation.1 | async-start | bytes 1114112 | tf_op jit(solution)/shard_map/all_gather | solution.py:41
  127.0 92.8 %copy-start.1 = (f32[2048]{0:T(1024)S(1)}, f32[2048]{0:T(1024)}, u32[]{:S(2)}) copy-start(f32[2048]{0:T(1024)} %param.32) | copy-start | bytes 24580
  154.7 65.2 %copy-start = (bf16[16,128,256]{2,1,0:T(8,128)(2,1)S(1)}, bf16[16,128,256]{2,1,0:T(8,128)(2,1)}, u32[]{:S(2)}) copy-start(bf16[16,128,256]{2,1,0:T(8,128)(2,1)} %get-tuple-element.2290) | copy-start | bytes 3145732
  242.4 51.1 %copy-start.2 = (f32[2048]{0:T(1024)S(1)}, f32[2048]{0:T(1024)}, u32[]{:S(2)}) copy-start(f32[2048]{0:T(1024)} %param.33) | copy-start | bytes 24580
  562.8 51.4 %copy-start.3 = (f32[2048]{0:T(1024)}, f32[2048]{0:T(1024)S(1)}, u32[]{:S(2)}) copy-start(f32[2048]{0:T(1024)S(1)} %get-tuple-element.2310) | copy-start | bytes 24580
Sparse Core Ops, SparseCore 0:
  10.6 78.8 all-gather.14
  91.4 35.5 all-gather.16
where the time goes:
time: 623 us; the launch traced here: 621 us
  blocking collectives  334 us (54%)
  waiting for transfers between devices  116 us (19%)
  loops' own time  52.8 us (8%)
  local copies, waits for them, and re-layouts  51.3 us (8%)
  matrix products  39 us (6%)
  between operations  14.5 us (2%)
  other arithmetic  13.5 us (2%)
    all_gather x12, blocking collectives, merged(): everything = jax.tree.map(lambda part: lax.all_gather(part, axis), value)  334 us
    all_gather x1, waiting for transfers between devices, on_device(): source_rows = lax.all_gather(src_feat, 'tgt', axis=0, tiled=True)  77 us
    another operation x6, loops' own time, sweep(): return lax.map(from_fresh, group_ids)  49.8 us
    dot_general x24, matrix products, make_scores(): jnp.einsum('grf,gkcf->grkc', source_groups[position], picked, preferred_e...  38.1 us
    all_gather x1, waiting for transfers between devices, on_device(): target_rows = lax.all_gather(tgt_feat, 'src', axis=0, tiled=True)  37.5 us
    gather x24, local copies, waits for them, and re-layouts, make_scores(): picked = target_tiles[cand_groups[position]]  20.4 us
    dynamic_slice x24, local copies, waits for them, and re-layouts, sweep(): return lax.map(from_fresh, group_ids)  15.5 us
  transfers between devices with their start and end apart: 2, of which 2 were waited for; matrix products, arithmetic and copies ran while one was open for 1% of the time, Pallas kernels for 0%

commit v1 on v0

v1 whole, which is shorter than its diff:
```python
import functools
import math

import jax
import jax.numpy as jnp
from jax import lax
from jax.experimental import pallas as pl
from jax.experimental.pallas import tpu as pltpu
from jax.sharding import PartitionSpec as P

ITERS = 3
UNROLL = 2
LOW = -1e30
LN2 = math.log(2.0)
LOG2E = math.log2(math.e)

VMEM = pl.BlockSpec(memory_space=pltpu.VMEM)
SMEM = pl.BlockSpec(memory_space=pltpu.SMEM)
PARAMS = pltpu.CompilerParams(vmem_limit_bytes=24 * 1024 * 1024)


def plan_kernel(blocks, slots, targets, room, cand_ref, counts_ref, plan_ref):
    spare = blocks * targets
    total = 0
    for block in range(blocks):

        def add(slot, at, block=block):
            target = cand_ref[block * slots + slot]
            plan_ref[at] = block
            plan_ref[room + at] = target
            plan_ref[2 * room + at] = target * blocks + block
            plan_ref[3 * room + at] = block * targets + target
            return at + 1

        total = lax.fori_loop(0, counts_ref[block], add, total)
    for extra in range(UNROLL):
        plan_ref[total + extra] = 0
        plan_ref[room + total + extra] = 0
        plan_ref[2 * room + total + extra] = spare
        plan_ref[3 * room + total + extra] = spare
    plan_ref[4 * room] = (total + UNROLL - 1) // UNROLL


def clear(high_ref, total_ref):
    high_ref[...] = jnp.full(high_ref.shape, LOW, jnp.float32)
    total_ref[...] = jnp.zeros(total_ref.shape, jnp.float32)


def keep_stats(shifted, row, high_ref, total_ref):
    highest = jnp.max(shifted, axis=0, keepdims=True)
    high_ref[pl.ds(row, 1), :] = highest
    total_ref[pl.ds(row, 1), :] = jnp.sum(jnp.exp2(shifted - highest), axis=0, keepdims=True)


def combine(high, total):
    highest = jnp.max(high, axis=0)
    return highest, jnp.sum(total * jnp.exp2(high - highest[None]), axis=0)


def send_out(high_ref, total_ref, kept, out_ref):
    outer = (high_ref.shape[0] - 8) // kept
    shape = (outer, kept, high_ref.shape[1])
    high = high_ref[: outer * kept, :].reshape(shape)
    total = total_ref[: outer * kept, :].reshape(shape)
    highest, totals = combine(high, total)
    local = highest + jnp.log2(totals)
    for part in range(out_ref.shape[0]):
        out_ref[part] = local


def potential(parts_ref, weight_ref):
    parts = parts_ref[...]
    highest = jnp.max(parts, axis=0)
    totals = jnp.sum(jnp.exp2(parts - highest[None]), axis=0)
    return jnp.log2(weight_ref[...]) - (highest + jnp.log2(totals))


def first_kernel(room, scale, plan_ref, src_ref, tgt_ref, scores_ref, flipped_ref, out_ref,
                 high_ref, total_ref):
    clear(high_ref, total_ref)
    contract = (((1,), (1,)), ((), ()))

    def group(step, carry):
        for lane in range(UNROLL):
            at = step * UNROLL + lane
            left = src_ref[plan_ref[at]]
            right = tgt_ref[plan_ref[room + at]]
            scores_ref[at] = scale * lax.dot_general(
                left, right, contract, preferred_element_type=jnp.float32)
            flipped = scale * lax.dot_general(
                right, left, contract, preferred_element_type=jnp.float32)
            flipped_ref[at] = flipped
            keep_stats(flipped, plan_ref[2 * room + at], high_ref, total_ref)
        return carry

    lax.fori_loop(0, plan_ref[4 * room], group, 0)
    send_out(high_ref, total_ref, src_ref.shape[0], out_ref)


def pass_kernel(room, own, row, kept, emit, plan_ref, parts_ref, weight_ref, scores_ref, out_ref,
                *refs):
    if emit:
        dual_ref, refs = refs[0], refs[1:]
    column_ref, high_ref, total_ref = refs
    dual = potential(parts_ref, weight_ref)
    if emit:
        dual_ref[...] = dual * LN2
    turned = dual.T
    for block in range(column_ref.shape[0]):
        column_ref[block] = jnp.broadcast_to(turned[:, block : block + 1], column_ref.shape[1:])
    clear(high_ref, total_ref)

    def group(step, carry):
        for lane in range(UNROLL):
            at = step * UNROLL + lane
            shifted = scores_ref[at] + column_ref[plan_ref[own * room + at]]
            keep_stats(shifted, plan_ref[row * room + at], high_ref, total_ref)
        return carry

    lax.fori_loop(0, plan_ref[4 * room], group, 0)
    send_out(high_ref, total_ref, kept, out_ref)


def last_kernel(parts_ref, weight_ref, dual_ref):
    dual_ref[...] = potential(parts_ref, weight_ref) * LN2


def spread(rows, axis):
    whole = jnp.broadcast_to(rows[None], (lax.axis_size(axis),) + rows.shape)
    return lax.all_to_all(whole, axis, 0, 0)


def on_device(src_feat, tgt_feat, src_weight, tgt_weight, cand, counts):
    blocks, _, slots = cand.shape
    size = src_feat.shape[0]
    targets = lax.axis_size("src")
    features = src_feat.shape[1]
    pairs = blocks * slots
    room = -(-(pairs + UNROLL) // 128) * 128
    held = -(-pairs // UNROLL) * UNROLL
    src_weight = src_weight.reshape(blocks, size)
    tgt_weight = tgt_weight.reshape(targets, size)

    plan = pl.pallas_call(
        functools.partial(plan_kernel, blocks, slots, targets, room),
        out_shape=jax.ShapeDtypeStruct((5 * room,), jnp.int32),
        in_specs=[SMEM, SMEM],
        out_specs=SMEM,
        name="plan",
    )(cand.reshape(-1), counts.reshape(-1))

    with jax.named_scope("gather_features"):
        source_rows = spread(src_feat, "tgt")
        target_rows = spread(tgt_feat, "src")

    tables = [pltpu.VMEM((blocks * targets + 8, size), jnp.float32)] * 2
    tile_shape = (held, size, size)
    to_tgt = jax.ShapeDtypeStruct((lax.axis_size("tgt"), blocks, size), jnp.float32)
    to_src = jax.ShapeDtypeStruct((lax.axis_size("src"), targets, size), jnp.float32)

    scores, flipped, parts = pl.pallas_call(
        functools.partial(first_kernel, room, LOG2E / math.sqrt(features)),
        out_shape=(pltpu.VMEM(tile_shape, jnp.float32), pltpu.VMEM(tile_shape, jnp.float32), to_tgt),
        in_specs=[SMEM, VMEM, VMEM],
        out_specs=(VMEM, VMEM, VMEM),
        scratch_shapes=tables,
        compiler_params=PARAMS,
        name="scores_and_rows",
    )(plan, source_rows, target_rows)

    def sweep(own, row, kept, emit, parts, weight, tiles, out, name):
        shapes = (out,) + ((jax.ShapeDtypeStruct(weight.shape, jnp.float32),) if emit else ())
        return pl.pallas_call(
            functools.partial(pass_kernel, room, own, row, kept, emit),
            out_shape=shapes,
            in_specs=[SMEM, VMEM, VMEM, VMEM],
            out_specs=(VMEM,) * len(shapes),
            scratch_shapes=[pltpu.VMEM((weight.shape[0], size, size), jnp.float32)] + tables,
            compiler_params=PARAMS,
            name=name,
        )(plan, parts, weight, pltpu.with_memory_space_constraint(tiles, pltpu.VMEM))

    for step in range(ITERS):
        if step:
            (parts,) = sweep(1, 2, blocks, False, parts, tgt_weight, flipped, to_tgt, "rows")
        with jax.named_scope("exchange_rows"):
            parts = lax.all_to_all(parts, "tgt", 0, 0)
        last = step == ITERS - 1
        parts, *source_dual = sweep(0, 3, targets, last, parts, src_weight, scores, to_src, "columns")
        with jax.named_scope("exchange_columns"):
            parts = lax.all_to_all(parts, "src", 0, 0)
    target_dual = pl.pallas_call(
        last_kernel,
        out_shape=jax.ShapeDtypeStruct((targets, size), jnp.float32),
        in_specs=[VMEM, VMEM],
        out_specs=VMEM,
        name="last",
    )(parts, tgt_weight)
    return (source_dual[0].reshape(-1), target_dual.reshape(-1))


def solution(mesh):
    placed = (
        P(("src", "tgt"), None),
        P(("tgt", "src"), None),
        P("src"),
        P("tgt"),
        P("src", "tgt", None),
        P("src", "tgt"),
    )
    return jax.shard_map(
        on_device, mesh=mesh, in_specs=placed, out_specs=(P("src"), P("tgt")), check_vma=False
    )
```

time: 623 us -> 163 us (0.26)
  blocking collectives: 334 us -> 101 us
  waiting for transfers between devices: 116 us -> 23.6 us
  loops' own time: 52.8 us -> 0 us
  local copies, waits for them, and re-layouts: 51.3 us -> 4.94 us
  matrix products: 39 us -> 0 us
  Pallas kernels: 0 us -> 21.8 us
  between operations: 14.5 us -> 0.72 us
  other arithmetic: 13.5 us -> 0 us
  starting transfers between devices: 0.08 us -> 10.6 us
    all_gather x12 -> x0, blocking collectives: 334 us -> none  [merged(): everything = jax.tree.map(lambda part: lax.all_gather(part, axis), value)]
    all_gather x2 -> x0, waiting for transfers between devices: 114 us -> none  [the longest x1 77 us: on_device(): source_rows = lax.all_gather(src_feat, 'tgt', axis=0, tiled=True)]
    all_to_all x0 -> x7, blocking collectives: none -> 101 us  [the longest x3 42.3 us: on_device(): parts = lax.all_to_all(parts, 'tgt', 0, 0)]
    another operation x12 -> x0, loops' own time: 52.8 us -> none  [the longest x6 49.8 us: sweep(): return lax.map(from_fresh, group_ids)]
    dot_general x27 -> x0, matrix products: 39 us -> none  [the longest x24 38.1 us: make_scores(): jnp.einsum('grf,gkcf->grkc', source_groups[position], picked, preferred_e...]
    gather x51 -> x0, local copies, waits for them, and re-layouts: 29.2 us -> none  [the longest x24 20.4 us: make_scores(): picked = target_tiles[cand_groups[position]]]
    all_to_all x0 -> x1, waiting for transfers between devices: none -> 23.6 us  [spread(): return lax.all_to_all(whole, axis, 0, 0)]
    pallas_call x0 -> x8, Pallas kernels: none -> 21.8 us  [the longest x5 12.2 us: sweep(): pl.pallas_call(functools.partial(pass_kernel, room, own, row, kept, emit)...]
  transfers between devices with their start and end apart: 2 -> 1, of which waited for: 2 -> 1; matrix products, arithmetic and copies ran while one was open for 1% -> 0% of each run, Pallas kernels for 0% -> 1%
where the time goes in v1:
time: 163 us; the launch traced here: 162 us
  blocking collectives  101 us (62%)
  waiting for transfers between devices  23.6 us (14%)
  Pallas kernels  21.8 us (13%)
  starting transfers between devices  10.6 us (7%)
  local copies, waits for them, and re-layouts  4.94 us (3%)
    all_to_all x3, blocking collectives, on_device(): parts = lax.all_to_all(parts, 'tgt', 0, 0)  42.3 us
    all_to_all x3, blocking collectives, on_device(): parts = lax.all_to_all(parts, 'src', 0, 0)  36.6 us
    all_to_all x1, waiting for transfers between devices, spread(): return lax.all_to_all(whole, axis, 0, 0)  23.6 us
    all_to_all x1, blocking collectives, spread(): return lax.all_to_all(whole, axis, 0, 0)  21.9 us
    pallas_call x5, Pallas kernels, sweep(): pl.pallas_call(functools.partial(pass_kernel, room, own, row, kept, emit)...  12.2 us
    all_to_all x1, starting transfers between devices, spread(): return lax.all_to_all(whole, axis, 0, 0)  10.6 us
    pallas_call x1, Pallas kernels, on_device(): pl.pallas_call(functools.partial(first_kernel, room, LOG2E / math.sqrt(fe...  6.3 us
  transfers between devices with their start and end apart: 1, of which 1 were waited for; matrix products, arithmetic and copies ran while one was open for 0% of the time, Pallas kernels for 1%

profile of v1, /device:TPU:1, one launch (start us, length us, event | category | flops | bytes accessed | tf_op | source)
XLA Modules:
  0.0 162.5 jit_solution(16823956947246542234)
XLA Ops:
  0.6 0.0 copy-start.4
  0.7 0.9 broadcast_in_dim.5
  1.6 21.9 %all_to_all.40.tgt_ref = bf16[16,128,256]{2,1,0:T(8,128)(2,1)S(1)} all-to-all(bf16[16,128,256]{2,1,0:T(8,128)(2,1)S(1)} %broadcast_in_dim.5), channel_id=1, replica_groups=mesh['src'=16,'tgt'=16] {'src'}, dimensions={0} | all-to-all | bytes 2097152 | tf_op jit(solution)/shard_map/gather_features/all_to_all | solution.py:130
  23.5 1.9 %broadcast_in_dim.4 = bf16[16,128,256]{2,1,0:T(8,128)(2,1)} broadcast(bf16[128,256]{1,0:T(8,128)(2,1)} %param.6), dimensions={1,2} | broadcast | bytes 1114112 | tf_op jit(solution)/shard_map/gather_features/broadcast_in_dim | solution.py:129
  25.4 10.6 %all-to-all-start = ((bf16[16,128,256]{2,1,0:T(8,128)(2,1)}), bf16[16,128,256]{2,1,0:T(8,128)(2,1)S(1)}, u32[]{:S(2)}, u32[]{:S(2)}) async-start(bf16[16,128,256]{2,1,0:T(8,128)(2,1)} %broadcast_in_dim.4), calls=%async_computation | async-start | bytes 2097152 | tf_op jit(solution)/shard_map/gather_features/all_to_all | solution.py:130
  36.0 0.1 copy.9
  36.1 0.6 reshape.24.cand_ref
  36.7 1.7 %plan.1.plan_ref = s32[640]{0:T(1024)} custom-call(s32[96]{0:T(128)} %reshape.24.cand_ref, s32[16]{0:T(128)} %bitcast.14), custom_call_target="tpu_custom_call" | custom-call | tf_op jit(solution)/shard_map/plan/pallas_call | solution.py:144
  38.4 23.6 %all-to-all-done.src_ref = bf16[16,128,256]{2,1,0:T(8,128)(2,1)S(1)} async-done(((bf16[16,128,256]{2,1,0:T(8,128)(2,1)}), bf16[16,128,256]{2,1,0:T(8,128)(2,1)S(1)}, u32[]{:S(2)}, u32[]{:S(2)}) %all-to-all-start) | async-done | bytes 1048608 | tf_op jit(solution)/shard_map/gather_features/all_to_all | solution.py:130
  62.0 0.7 copy-done
  62.7 6.3 %scores_and_rows.1 = (f32[96,128,128]{2,1,0:T(8,128)S(1)}, f32[96,128,128]{2,1,0:T(8,128)S(1)}, f32[16,16,128]{2,1,0:T(8,128)S(1)}) custom-call(s32[640]{0:T(1024)S(1)} %copy-done, bf16[16,128,256]{2,1,0:T(8,128)(2,1)S(1)} %all-to-all-done.src_ref, bf16[16,128,256]{2,1,0:T(8,128)(2,1)S(1)} %all_to_all.40.tgt_ref), custom_call_target="tpu_custom_call" | custom-call | tf_op jit(solution)/shard_map/scores_and_rows/pallas_call | solution.py:161
  69.0 16.8 %all_to_all.41.parts_ref = f32[16,16,128]{2,1,0:T(8,128)S(1)} all-to-all(f32[16,16,128]{2,1,0:T(8,128)S(1)} %get-tuple-element.7), channel_id=1, replica_groups=mesh['src'=16,'tgt'=16] {'tgt'}, dimensions={0} | all-to-all | bytes 262144 | tf_op jit(solution)/shard_map/exchange_rows/all_to_all | solution.py:187
  85.8 0.7 copy-done.1
  86.5 2.3 %columns.3 = f32[16,16,128]{2,1,0:T(8,128)S(1)} custom-call(s32[640]{0:T(1024)S(1)} %copy-done.1, f32[16,16,128]{2,1,0:T(8,128)S(1)} %all_to_all.41.parts_ref, f32[16,128]{1,0:T(8,128)S(1)} %bitcast.7, f32[96,128,128]{2,1,0:T(8,128)S(1)} %get-tuple-element.8.scores_ref), custom_call_target="tpu_custom_call" | custom-call | tf_op jit(solution)/shard_map/columns/pallas_call | solution.py:173
  88.8 13.6 %all_to_all.42.parts_ref = f32[16,16,128]{2,1,0:T(8,128)S(1)} all-to-all(f32[16,16,128]{2,1,0:T(8,128)S(1)} %columns.3), channel_id=1, replica_groups=mesh['src'=16,'tgt'=16] {'src'}, dimensions={0} | all-to-all | bytes 262144 | tf_op jit(solution)/shard_map/exchange_columns/all_to_all | solution.py:191
  102.4 2.3 %rows.2 = f32[16,16,128]{2,1,0:T(8,128)S(1)} custom-call(s32[640]{0:T(1024)S(1)} %copy-done.1, f32[16,16,128]{2,1,0:T(8,128)S(1)} %all_to_all.42.parts_ref, f32[16,128]{1,0:T(8,128)S(1)} %bitcast.11, f32[96,128,128]{2,1,0:T(8,128)S(1)} %get-tuple-element.9.scores_ref), custom_call_target="tpu_custom_call" | custom-call | tf_op jit(solution)/shard_map/rows/pallas_call | solution.py:173
  104.8 12.6 %all_to_all.43.parts_ref = f32[16,16,128]{2,1,0:T(8,128)S(1)} all-to-all(f32[16,16,128]{2,1,0:T(8,128)S(1)} %rows.2), channel_id=1, replica_groups=mesh['src'=16,'tgt'=16] {'tgt'}, dimensions={0} | all-to-all | bytes 262144 | tf_op jit(solution)/shard_map/exchange_rows/all_to_all | solution.py:187
  117.4 2.3 %columns.4 = f32[16,16,128]{2,1,0:T(8,128)S(1)} custom-call(s32[640]{0:T(1024)S(1)} %copy-done.1, f32[16,16,128]{2,1,0:T(8,128)S(1)} %all_to_all.43.parts_ref, f32[16,128]{1,0:T(8,128)S(1)} %bitcast.8, f32[96,128,128]{2,1,0:T(8,128)S(1)} %get-tuple-element.8.scores_ref), custom_call_target="tpu_custom_call" | custom-call | tf_op jit(solution)/shard_map/columns/pallas_call | solution.py:173
  119.8 11.6 %all_to_all.44.parts_ref = f32[16,16,128]{2,1,0:T(8,128)S(1)} all-to-all(f32[16,16,128]{2,1,0:T(8,128)S(1)} %columns.4), channel_id=1, replica_groups=mesh['src'=16,'tgt'=16] {'src'}, dimensions={0} | all-to-all | bytes 262144 | tf_op jit(solution)/shard_map/exchange_columns/all_to_all | solution.py:191
  131.4 2.3 %rows.3 = f32[16,16,128]{2,1,0:T(8,128)S(1)} custom-call(s32[640]{0:T(1024)S(1)} %copy-done.1, f32[16,16,128]{2,1,0:T(8,128)S(1)} %all_to_all.44.parts_ref, f32[16,128]{1,0:T(8,128)S(1)} %bitcast.12, f32[96,128,128]{2,1,0:T(8,128)S(1)} %get-tuple-element.9.scores_ref), custom_call_target="tpu_custom_call" | custom-call | tf_op jit(solution)/shard_map/rows/pallas_call | solution.py:173
  133.7 12.9 %all_to_all.45.parts_ref = f32[16,16,128]{2,1,0:T(8,128)S(1)} all-to-all(f32[16,16,128]{2,1,0:T(8,128)S(1)} %rows.3), channel_id=1, replica_groups=mesh['src'=16,'tgt'=16] {'tgt'}, dimensions={0} | all-to-all | bytes 262144 | tf_op jit(solution)/shard_map/exchange_rows/all_to_all | solution.py:187
  146.6 2.9 %columns.5 = (f32[16,16,128]{2,1,0:T(8,128)S(1)}, f32[16,128]{1,0:T(8,128)}) custom-call(s32[640]{0:T(1024)S(1)} %copy-done.1, f32[16,16,128]{2,1,0:T(8,128)S(1)} %all_to_all.45.parts_ref, f32[16,128]{1,0:T(8,128)S(1)} %bitcast.9, f32[96,128,128]{2,1,0:T(8,128)S(1)} %get-tuple-element.8.scores_ref), custom_call_target="tpu_custom_call" | custom-call | tf_op jit(solution)/shard_map/columns/pallas_call | solution.py:173
  149.5 11.4 %all_to_all.46.parts_ref = f32[16,16,128]{2,1,0:T(8,128)} all-to-all(f32[16,16,128]{2,1,0:T(8,128)S(1)} %get-tuple-element.11), channel_id=1, replica_groups=mesh['src'=16,'tgt'=16] {'src'}, dimensions={0} | all-to-all | bytes 262144 | tf_op jit(solution)/shard_map/exchange_columns/all_to_all | solution.py:191
  160.9 1.6 last.1
  (7 shorter events, 0.0 us)
Async XLA Ops:
  0.6 35.4 %copy-start.4 = (s32[16,1,6]{0,1,2:T(1,128)S(1)}, s32[16,1,6]{0,1,2:T(1,128)}, u32[]{:S(2)}) copy-start(s32[16,1,6]{0,1,2:T(1,128)} %param.10) | copy-start | bytes 1156
  0.6 85.1 %copy-start.2 = (f32[2048]{0:T(1024)S(1)}, f32[2048]{0:T(1024)}, u32[]{:S(2)}) copy-start(f32[2048]{0:T(1024)} %param.8) | copy-start | bytes 24580
  23.5 79.0 %copy-start.3 = (f32[2048]{0:T(1024)S(1)}, f32[2048]{0:T(1024)}, u32[]{:S(2)}) copy-start(f32[2048]{0:T(1024)} %param.9) | copy-start | bytes 24580
  25.4 36.6 %all-to-all-start = ((bf16[16,128,256]{2,1,0:T(8,128)(2,1)}), bf16[16,128,256]{2,1,0:T(8,128)(2,1)S(1)}, u32[]{:S(2)}, u32[]{:S(2)}) async-start(bf16[16,128,256]{2,1,0:T(8,128)(2,1)} %broadcast_in_dim.4), calls=%async_computation | async-start | bytes 2097152 | tf_op jit(solution)/shard_map/gather_features/all_to_all | solution.py:130
  62.0 0.7 copy-start
  85.8 0.7 copy-start.1

commit v2 on v1

v2 whole, which is shorter than its diff:
```python
import functools
import math

import jax
import jax.numpy as jnp
from jax import lax
from jax.experimental import pallas as pl
from jax.experimental.pallas import tpu as pltpu
from jax.sharding import PartitionSpec as P

ITERS = 3
UNROLL = 2
FIELDS = 5
LOW = -1e30
LN2 = math.log(2.0)
LOG2E = math.log2(math.e)

VMEM = pl.BlockSpec(memory_space=pltpu.VMEM)
SMEM = pl.BlockSpec(memory_space=pltpu.SMEM)
PARAMS = pltpu.CompilerParams(vmem_limit_bytes=8 * 1024 * 1024)


def plan_kernel(blocks, slots, targets, room, cand_ref, counts_ref, plan_ref):
    spare = blocks * targets
    here = lax.axis_index("tgt")
    deep, side = here // 2, here % 2
    stages = blocks // 2

    def put(at, block, target, row, column, place):
        for field, value in enumerate((block, target, row, column, place)):
            plan_ref[field * room + at] = value

    total = 0
    for chunk, offset in enumerate(arrival(stages)):
        plan_ref[FIELDS * room + chunk] = total // UNROLL
        for place in range(2):
            block = ((deep + offset + stages) % stages) * 2 + (side + place) % 2

            def add(slot, at, block=block, place=place):
                target = cand_ref[block * slots + slot]
                put(at, block, target, target * blocks + block, block * targets + target, place)
                return at + 1

            total = lax.fori_loop(0, counts_ref[block], add, total)
        for extra in range(UNROLL - 1):
            put(total + extra, 0, 0, spare, spare, 0)
        total = (total + UNROLL - 1) // UNROLL * UNROLL
    plan_ref[FIELDS * room + stages] = total // UNROLL


def arrival(stages):
    offsets = [0]
    for hop in range(1, stages // 2):
        offsets += [-hop, hop]
    return offsets + [stages // 2]


def clear(high_ref, total_ref):
    high_ref[...] = jnp.full(high_ref.shape, LOW, jnp.float32)
    total_ref[...] = jnp.zeros(total_ref.shape, jnp.float32)


def keep_stats(shifted, row, high_ref, total_ref):
    highest = jnp.max(shifted, axis=0, keepdims=True)
    high_ref[pl.ds(row, 1), :] = highest
    total_ref[pl.ds(row, 1), :] = jnp.sum(jnp.exp2(shifted - highest), axis=0, keepdims=True)


def combine(high, total):
    highest = jnp.max(high, axis=0)
    return highest, jnp.sum(total * jnp.exp2(high - highest[None]), axis=0)


def local_lse(high_ref, total_ref, kept):
    outer = (high_ref.shape[0] - 8) // kept
    shape = (outer, kept, high_ref.shape[1])
    high = high_ref[: outer * kept, :].reshape(shape)
    total = total_ref[: outer * kept, :].reshape(shape)
    highest, totals = combine(high, total)
    return highest + jnp.log2(totals)


def copies(local, out_ref):
    for part in range(out_ref.shape[0]):
        out_ref[part] = local


def potential(parts_ref, weight_ref):
    parts = parts_ref[...]
    highest = jnp.max(parts, axis=0)
    totals = jnp.sum(jnp.exp2(parts - highest[None]), axis=0)
    return jnp.log2(weight_ref[...]) - (highest + jnp.log2(totals))


def matmul(left, right, scale):
    return scale * lax.dot_general(
        left, right, (((1,), (1,)), ((), ())), preferred_element_type=jnp.float32)


def over_pairs(plan_ref, room, first, chunks, body):
    for chunk, ref in enumerate(chunks, first):

        def group(step, carry, ref=ref):
            for lane in range(UNROLL):
                body(ref, step * UNROLL + lane)
            return carry

        bounds = FIELDS * room + chunk
        lax.fori_loop(plan_ref[bounds], plan_ref[bounds + 1], group, 0)


def cost(pairs):
    return pl.CostEstimate(flops=pairs * 2 * 128 * 128 * 256, bytes_accessed=pairs * 65536, transcendentals=0)


def first_kernel(room, scale, first, count, plan_ref, tgt_ref, *refs):
    chunks, refs = refs[:count], refs[count:]
    if first:
        earlier_ref, refs = refs[0], refs[3:]
    flipped_ref, scores_ref, out_ref, high_ref, total_ref = refs
    clear(high_ref, total_ref)

    def body(ref, at):
        left, right = ref[plan_ref[4 * room + at]], tgt_ref[plan_ref[room + at]]
        flipped = matmul(right, left, scale)
        flipped_ref[at] = flipped
        scores_ref[at] = matmul(left, right, scale)
        keep_stats(flipped, plan_ref[2 * room + at], high_ref, total_ref)

    over_pairs(plan_ref, room, first, chunks, body)
    local = local_lse(high_ref, total_ref, out_ref.shape[-2])
    if first:
        local = jnp.maximum(local, earlier_ref[...])
    if len(out_ref.shape) == 3:
        copies(local, out_ref)
    else:
        out_ref[...] = local


def pass_kernel(room, column_chunks, own, row, kept, emit, plan_ref, parts_ref, weight_ref, scores_ref, out_ref,
                *refs):
    if emit:
        dual_ref, refs = refs[0], refs[1:]
    column_ref, high_ref, total_ref = refs
    dual = potential(parts_ref, weight_ref)
    if emit:
        dual_ref[...] = dual * LN2
    turned = dual.T
    for block in range(column_ref.shape[0]):
        column_ref[block] = jnp.broadcast_to(turned[:, block : block + 1], column_ref.shape[1:])
    clear(high_ref, total_ref)

    def group(step, carry):
        for lane in range(UNROLL):
            at = step * UNROLL + lane
            shifted = scores_ref[at] + column_ref[plan_ref[own * room + at]]
            keep_stats(shifted, plan_ref[row * room + at], high_ref, total_ref)
        return carry

    lax.fori_loop(0, plan_ref[FIELDS * room + column_chunks], group, 0)
    copies(local_lse(high_ref, total_ref, kept), out_ref)


def last_kernel(parts_ref, weight_ref, dual_ref):
    dual_ref[...] = potential(parts_ref, weight_ref) * LN2


def spread(rows, axis):
    whole = jnp.broadcast_to(rows[None], (lax.axis_size(axis),) + rows.shape)
    return lax.all_to_all(whole, axis, 0, 0)


def ring(rows, beside):
    size = lax.axis_size("tgt")
    stages = size // 2

    def along_z(value, by):
        return lax.ppermute(
            value, "tgt", [(k, (k // 2 + by) % stages * 2 + k % 2) for k in range(size)])

    other = lax.ppermute(rows, "tgt", [(k, k ^ 1) for k in range(size)])
    own = jnp.stack([rows, other])
    up, down, chunks = own, own, [own]
    for hop in range(1, stages // 2):
        if hop == stages // 2 - 1:
            up, down, beside = lax.optimization_barrier((up, down, beside))
        up, down = along_z(up, 1), along_z(down, -1)
        chunks += [up, down]

    def last(before):
        ends = lax.optimization_barrier((up[0], down[1], before))
        return jnp.stack([along_z(ends[0], 1), along_z(ends[1], -1)]), ends[2]

    return chunks, last, beside


def on_device(src_feat, tgt_feat, src_weight, tgt_weight, cand, counts):
    blocks, _, slots = cand.shape
    size, features = src_feat.shape
    targets = lax.axis_size("src")
    stages = blocks // 2
    held = blocks * slots + stages * UNROLL
    room = -(-held // 128) * 128
    src_weight = src_weight.reshape(blocks, size)
    tgt_weight = tgt_weight.reshape(targets, size)

    plan = pl.pallas_call(
        functools.partial(plan_kernel, blocks, slots, targets, room),
        out_shape=pltpu.SMEM(((FIELDS + 1) * room,), jnp.int32),
        in_specs=[SMEM, SMEM],
        out_specs=SMEM,
        compiler_params=PARAMS,
        name="plan",
    )(cand.reshape(-1), counts.reshape(-1))
    plan = pltpu.with_memory_space_constraint(plan, pltpu.SMEM)

    with jax.named_scope("gather_features"):
        target_rows = spread(tgt_feat, "src")
        chunks, last_chunk, target_rows = ring(src_feat, target_rows)

    tables = [pltpu.VMEM((blocks * targets + 8, size), jnp.float32)] * 2
    tiles = pltpu.VMEM((held, size, size), jnp.float32)
    to_tgt = jax.ShapeDtypeStruct((lax.axis_size("tgt"), blocks, size), jnp.float32)
    to_src = jax.ShapeDtypeStruct((lax.axis_size("src"), targets, size), jnp.float32)
    scale = LOG2E / math.sqrt(features)

    def first_rows(first, some, local, scored, out, pairs, name):
        kept = [pltpu.with_memory_space_constraint(part, pltpu.VMEM) for part in scored]
        more = [local] + kept if scored else []
        given = 2 + len(some)
        *scored, local = pl.pallas_call(
            functools.partial(first_kernel, room, scale, first, len(some)),
            out_shape=(tiles, tiles, out),
            in_specs=[SMEM] + [VMEM] * (1 + len(some) + len(more)),
            out_specs=(VMEM, VMEM, VMEM),
            scratch_shapes=tables,
            input_output_aliases={given + 1: 0, given + 2: 1} if more else {},
            compiler_params=PARAMS,
            cost_estimate=cost(pairs),
            name=name,
        )(plan, target_rows, *some, *more)
        return scored, local

    one = jax.ShapeDtypeStruct((blocks, size), jnp.float32)
    split = len(chunks) - 2
    scored, local = first_rows(0, chunks[:split], None, (), one, 26, "rows_early")
    end, local = last_chunk(local)
    scored, local = first_rows(split, chunks[split:], local, scored, one, 12, "rows_middle")
    (flipped, scores), parts = first_rows(split + 2, [end], local, scored, to_tgt, 6, "rows_late")

    def sweep(own, row, kept, emit, parts, weight, tiles, out, name):
        shapes = (out,) + ((jax.ShapeDtypeStruct(weight.shape, jnp.float32),) if emit else ())
        return pl.pallas_call(
            functools.partial(pass_kernel, room, stages, own, row, kept, emit),
            out_shape=shapes,
            in_specs=[SMEM, VMEM, VMEM, VMEM],
            out_specs=(VMEM,) * len(shapes),
            scratch_shapes=[pltpu.VMEM((weight.shape[0], size, size), jnp.float32)] + tables,
            compiler_params=PARAMS,
            name=name,
        )(plan, parts, weight, pltpu.with_memory_space_constraint(tiles, pltpu.VMEM))

    for step in range(ITERS):
        if step:
            (parts,) = sweep(1, 2, blocks, False, parts, tgt_weight, flipped, to_tgt, "rows")
        with jax.named_scope("exchange_rows"):
            parts = lax.all_to_all(parts, "tgt", 0, 0)
        last = step == ITERS - 1
        parts, *source_dual = sweep(0, 3, targets, last, parts, src_weight, scores, to_src, "columns")
        with jax.named_scope("exchange_columns"):
            parts = lax.all_to_all(parts, "src", 0, 0)
    target_dual = pl.pallas_call(
        last_kernel,
        out_shape=jax.ShapeDtypeStruct((targets, size), jnp.float32),
        in_specs=[VMEM, VMEM],
        out_specs=VMEM,
        compiler_params=PARAMS,
        name="last",
    )(parts, tgt_weight)
    return (source_dual[0].reshape(-1), target_dual.reshape(-1))


def solution(mesh):
    placed = (
        P(("src", "tgt"), None),
        P(("tgt", "src"), None),
        P("src"),
        P("tgt"),
        P("src", "tgt", None),
        P("src", "tgt"),
    )
    return jax.shard_map(
        on_device, mesh=mesh, in_specs=placed, out_specs=(P("src"), P("tgt")), check_vma=False
    )
```

time: 163 us -> 150 us (0.920)
  starting transfers between devices: 10.6 us -> 25.7 us
  blocking collectives: 101 us -> 89.8 us
  waiting for transfers between devices: 23.6 us -> 14.4 us
  Pallas kernels: 21.8 us -> 13.5 us
    all_to_all x1, waiting for transfers between devices: 23.6 us -> 0.01 us  [spread(): return lax.all_to_all(whole, axis, 0, 0)]
    all_to_all x1 -> x0, blocking collectives: 21.9 us -> none  [spread(): return lax.all_to_all(whole, axis, 0, 0)]
    ppermute x0 -> x9, starting transfers between devices: none -> 18.9 us  [the longest x8 16.3 us: along_z(): lax.ppermute(value, 'tgt', [(k, (k // 2 + by) % stages * 2 + k % 2) for k...]
    ppermute x0 -> x9, waiting for transfers between devices: none -> 14.4 us  [the longest x8 7.42 us: along_z(): lax.ppermute(value, 'tgt', [(k, (k // 2 + by) % stages * 2 + k % 2) for k...]
    all_to_all x3, blocking collectives: 36.6 us -> 48.7 us  [on_device(): parts = lax.all_to_all(parts, 'src', 0, 0)]
    pallas_call x6 -> x8, Pallas kernels: 18.5 us -> 11.8 us  [the longest x5 7.56 us: sweep(): pl.pallas_call(functools.partial(pass_kernel, room, stages, own, row, kep...]
    all_to_all x1, starting transfers between devices: 10.6 us -> 6.83 us  [spread(): return lax.all_to_all(whole, axis, 0, 0)]
  transfers between devices with their start and end apart: 1 -> 10, of which waited for: 1 -> 5; matrix products, arithmetic and copies ran while one was open for 0% -> 1% of each run, Pallas kernels for 1% -> 3%
where the time goes in v2:
time: 150 us; the launch traced here: 148 us
  blocking collectives  89.8 us (60%)
  starting transfers between devices  25.7 us (17%)
  waiting for transfers between devices  14.4 us (10%)
  Pallas kernels  13.5 us (9%)
  local copies, waits for them, and re-layouts  3.45 us (2%)
    all_to_all x3, blocking collectives, on_device(): parts = lax.all_to_all(parts, 'src', 0, 0)  48.7 us
    all_to_all x3, blocking collectives, on_device(): parts = lax.all_to_all(parts, 'tgt', 0, 0)  41.1 us
    ppermute x8, starting transfers between devices, along_z(): lax.ppermute(value, 'tgt', [(k, (k // 2 + by) % stages * 2 + k % 2) for k...  16.3 us
    pallas_call x5, Pallas kernels, sweep(): pl.pallas_call(functools.partial(pass_kernel, room, stages, own, row, kep...  7.56 us
    ppermute x8, waiting for transfers between devices, along_z(): lax.ppermute(value, 'tgt', [(k, (k // 2 + by) % stages * 2 + k % 2) for k...  7.42 us
    ppermute x1, waiting for transfers between devices, ring(): other = lax.ppermute(rows, 'tgt', [(k, k ^ 1) for k in range(size)])  6.98 us
    all_to_all x1, starting transfers between devices, spread(): return lax.all_to_all(whole, axis, 0, 0)  6.83 us
    pallas_call x3, Pallas kernels, first_rows(): pl.pallas_call(functools.partial(first_kernel, room, scale, first, len(so...  4.27 us
  transfers between devices with their start and end apart: 10, of which 5 were waited for; matrix products, arithmetic and copies ran while one was open for 1% of the time, Pallas kernels for 3%

profile of v2, /device:TPU:1, one launch (start us, length us, event | category | flops | bytes accessed | tf_op | source)
XLA Modules:
  0.0 148.5 jit_solution(2681066866007874829)
XLA Ops:
  0.6 1.9 %broadcast_in_dim.2 = bf16[16,128,256]{2,1,0:T(8,128)(2,1)} broadcast(bf16[128,256]{1,0:T(8,128)(2,1)} %param.7), dimensions={1,2} | broadcast | bytes 1114112 | tf_op jit(solution)/shard_map/gather_features/broadcast_in_dim | solution.py:169
  2.6 6.8 %all-to-all-start = ((bf16[16,128,256]{2,1,0:T(8,128)(2,1)}), bf16[16,128,256]{2,1,0:T(8,128)(2,1)S(1)}, u32[]{:S(2)}, u32[]{:S(2)}) async-start(bf16[16,128,256]{2,1,0:T(8,128)(2,1)} %broadcast_in_dim.2), calls=%async_computation | async-start | bytes 2097152 | tf_op jit(solution)/shard_map/gather_features/all_to_all | solution.py:170
  9.4 2.6 %collective-permute-start = (bf16[128,256]{1,0:T(8,128)(2,1)}, bf16[128,256]{1,0:T(8,128)(2,1)S(1)}, u32[]{:S(2)}, u32[]{:S(2)}) collective-permute-start(bf16[128,256]{1,0:T(8,128)(2,1)} %param.6), channel_id=1, source_target_pairs={{0,1},{1,0},{2,3},{3,2},{4,5},{5,4},{6,7},{7,6},{8,9},{9,8},{10,11... | collective-permute-start | bytes 196616 | tf_op jit(solution)/shard_map/gather_features/ppermute | solution.py:181
  12.0 7.0 %collective-permute-done = bf16[128,256]{1,0:T(8,128)(2,1)S(1)} collective-permute-done((bf16[128,256]{1,0:T(8,128)(2,1)}, bf16[128,256]{1,0:T(8,128)(2,1)S(1)}, u32[]{:S(2)}, u32[]{:S(2)}) %collective-permute-start) | collective-permute-done | bytes 65568 | tf_op jit(solution)/shard_map/gather_features/ppermute | solution.py:181
  19.8 1.7 %collective-permute-start.1 = (bf16[2,128,256]{2,1,0:T(8,128)(2,1)S(1)}, bf16[2,128,256]{2,1,0:T(8,128)(2,1)S(1)}, u32[]{:S(2)}, u32[]{:S(2)}) collective-permute-start(bf16[2,128,256]{2,1,0:T(8,128)(2,1)S(1)} %pad_maximum_fusion.refs_0_), channel_id=1, source_target_pairs={{0,2},{1,3},{2,4},{3,5},{4,6},{5,7},{6,8},{7,9},{8,10},{9,11},{10,... | collective-permute-start | bytes 393224 | tf_op jit(solution)/shard_map/gather_features/ppermute | solution.py:178
  21.6 4.0 %collective-permute-start.3 = (bf16[2,128,256]{2,1,0:T(8,128)(2,1)S(1)}, bf16[2,128,256]{2,1,0:T(8,128)(2,1)S(1)}, u32[]{:S(2)}, u32[]{:S(2)}) collective-permute-start(bf16[2,128,256]{2,1,0:T(8,128)(2,1)S(1)} %pad_maximum_fusion.refs_0_), channel_id=1, source_target_pairs={{0,14},{1,15},{2,0},{3,1},{4,2},{5,3},{6,4},{7,5},{8,6},{9,7},{10,... | collective-permute-start | bytes 393224 | tf_op jit(solution)/shard_map/gather_features/ppermute | solution.py:178
  25.6 2.3 %collective-permute-done.1.refs_1_ = bf16[2,128,256]{2,1,0:T(8,128)(2,1)S(1)} collective-permute-done((bf16[2,128,256]{2,1,0:T(8,128)(2,1)S(1)}, bf16[2,128,256]{2,1,0:T(8,128)(2,1)S(1)}, u32[]{:S(2)}, u32[]{:S(2)}) %collective-permute-start.1) | collective-permute-done | bytes 131104 | tf_op jit(solution)/shard_map/gather_features/ppermute | solution.py:178
  27.9 3.0 %collective-permute-start.4 = (bf16[2,128,256]{2,1,0:T(8,128)(2,1)S(1)}, bf16[2,128,256]{2,1,0:T(8,128)(2,1)S(1)}, u32[]{:S(2)}, u32[]{:S(2)}) collective-permute-start(bf16[2,128,256]{2,1,0:T(8,128)(2,1)S(1)} %collective-permute-done.3.refs_2_), channel_id=1, source_target_pairs={{0,14},{1,15},{2,0},{3,1},{4,2},{5,3},{6,4},{7,5},{8,6},{9,7},{10,... | collective-permute-start | bytes 393224 | tf_op jit(solution)/shard_map/gather_features/ppermute | solution.py:178
  30.9 2.0 %collective-permute-done.2.refs_3_ = bf16[2,128,256]{2,1,0:T(8,128)(2,1)S(1)} collective-permute-done((bf16[2,128,256]{2,1,0:T(8,128)(2,1)S(1)}, bf16[2,128,256]{2,1,0:T(8,128)(2,1)S(1)}, u32[]{:S(2)}, u32[]{:S(2)}) %collective-permute-start.2) | collective-permute-done | bytes 131104 | tf_op jit(solution)/shard_map/gather_features/ppermute | solution.py:178
  35.4 3.5 %collective-permute-start.6 = (bf16[2,128,256]{2,1,0:T(8,128)(2,1)S(1)}, bf16[2,128,256]{2,1,0:T(8,128)(2,1)S(1)}, u32[]{:S(2)}, u32[]{:S(2)}) collective-permute-start(bf16[2,128,256]{2,1,0:T(8,128)(2,1)S(1)} %collective-permute-done.4.refs_4_), channel_id=1, source_target_pairs={{0,14},{1,15},{2,0},{3,1},{4,2},{5,3},{6,4},{7,5},{8,6},{9,7},{10,... | collective-permute-start | bytes 393224 | tf_op jit(solution)/shard_map/gather_features/ppermute | solution.py:178
  38.9 2.5 %rows_early.1 = (f32[112,128,128]{2,1,0:T(8,128)S(1)}, f32[112,128,128]{2,1,0:T(8,128)S(1)}, f32[16,128]{1,0:T(8,128)S(1)}) custom-call(s32[768]{0:T(1024)S(4)} %plan.1.plan_ref, bf16[16,128,256]{2,1,0:T(8,128)(2,1)S(1)} %all-to-all-done.tgt_ref, bf16[2,128,256]{2,1,0:T(8,128)(2,1)S(1)} %pad_maximum_fusion.refs_0_, ...), custom_call_target="tpu_custom_call" | custom-call | flops 218103808 | bytes 1703936 | tf_op jit(solution)/shard_map/rows_early/pallas_call | solution.py:231
  41.5 4.0 %collective-permute-start.8 = (bf16[128,256]{1,0:T(8,128)(2,1)S(1)}, bf16[128,256]{1,0:T(8,128)(2,1)S(1)}, u32[]{:S(2)}, u32[]{:S(2)}) collective-permute-start(bf16[128,256]{1,0:T(8,128)(2,1)S(1)} %slice_bitcast_fusion), channel_id=1, source_target_pairs={{0,14},{1,15},{2,0},{3,1},{4,2},{5,3},{6,4},{7,5},{8,6},{9,7},{10,... | collective-permute-start | bytes 196616 | tf_op jit(solution)/shard_map/ppermute | solution.py:178
  46.8 3.0 %collective-permute-done.7 = bf16[128,256]{1,0:T(8,128)(2,1)S(1)} collective-permute-done((bf16[128,256]{1,0:T(8,128)(2,1)S(1)}, bf16[128,256]{1,0:T(8,128)(2,1)S(1)}, u32[]{:S(2)}, u32[]{:S(2)}) %collective-permute-start.7) | collective-permute-done | bytes 65568 | tf_op jit(solution)/shard_map/ppermute | solution.py:178
  50.4 15.9 %all_to_all.35.parts_ref = f32[16,16,128]{2,1,0:T(8,128)S(1)} all-to-all(f32[16,16,128]{2,1,0:T(8,128)S(1)} %get-tuple-element.31), channel_id=1, replica_groups=mesh['src'=16,'tgt'=16] {'tgt'}, dimensions={0} | all-to-all | bytes 262144 | tf_op jit(solution)/shard_map/exchange_rows/all_to_all | solution.py:267
  66.3 1.4 columns.3
  67.7 24.8 %all_to_all.36.parts_ref = f32[16,16,128]{2,1,0:T(8,128)S(1)} all-to-all(f32[16,16,128]{2,1,0:T(8,128)S(1)} %columns.3), channel_id=1, replica_groups=mesh['src'=16,'tgt'=16] {'src'}, dimensions={0} | all-to-all | bytes 262144 | tf_op jit(solution)/shard_map/exchange_columns/all_to_all | solution.py:271
  92.5 1.4 rows.2
  93.9 12.6 %all_to_all.37.parts_ref = f32[16,16,128]{2,1,0:T(8,128)S(1)} all-to-all(f32[16,16,128]{2,1,0:T(8,128)S(1)} %rows.2), channel_id=1, replica_groups=mesh['src'=16,'tgt'=16] {'tgt'}, dimensions={0} | all-to-all | bytes 262144 | tf_op jit(solution)/shard_map/exchange_rows/all_to_all | solution.py:267
  106.5 1.4 columns.4
  107.9 12.0 %all_to_all.38.parts_ref = f32[16,16,128]{2,1,0:T(8,128)S(1)} all-to-all(f32[16,16,128]{2,1,0:T(8,128)S(1)} %columns.4), channel_id=1, replica_groups=mesh['src'=16,'tgt'=16] {'src'}, dimensions={0} | all-to-all | bytes 262144 | tf_op jit(solution)/shard_map/exchange_columns/all_to_all | solution.py:271
  119.9 1.4 rows.3
  121.3 12.7 %all_to_all.39.parts_ref = f32[16,16,128]{2,1,0:T(8,128)S(1)} all-to-all(f32[16,16,128]{2,1,0:T(8,128)S(1)} %rows.3), channel_id=1, replica_groups=mesh['src'=16,'tgt'=16] {'tgt'}, dimensions={0} | all-to-all | bytes 262144 | tf_op jit(solution)/shard_map/exchange_rows/all_to_all | solution.py:267
  133.9 2.0 %columns.5 = (f32[16,16,128]{2,1,0:T(8,128)S(1)}, f32[16,128]{1,0:T(8,128)}) custom-call(s32[768]{0:T(1024)S(4)} %plan.1.plan_ref, f32[16,16,128]{2,1,0:T(8,128)S(1)} %all_to_all.39.parts_ref, f32[16,128]{1,0:T(8,128)S(1)} %bitcast.20, f32[112,128,128]{2,1,0:T(8,128)S(1)} %get-tuple-element.32.scores_ref), custom_call_target="tpu_custom_call" | custom-call | tf_op jit(solution)/shard_map/columns/pallas_call | solution.py:253
  135.9 11.9 %all_to_all.40.parts_ref = f32[16,16,128]{2,1,0:T(8,128)S(1)} all-to-all(f32[16,16,128]{2,1,0:T(8,128)S(1)} %get-tuple-element.35), channel_id=1, replica_groups=mesh['src'=16,'tgt'=16] {'src'}, dimensions={0} | all-to-all | bytes 262144 | tf_op jit(solution)/shard_map/exchange_columns/all_to_all | solution.py:271
  (25 shorter events, 6.0 us)
Async XLA Ops:
  2.6 30.3 %all-to-all-start = ((bf16[16,128,256]{2,1,0:T(8,128)(2,1)}), bf16[16,128,256]{2,1,0:T(8,128)(2,1)S(1)}, u32[]{:S(2)}, u32[]{:S(2)}) async-start(bf16[16,128,256]{2,1,0:T(8,128)(2,1)} %broadcast_in_dim.2), calls=%async_computation | async-start | bytes 2097152 | tf_op jit(solution)/shard_map/gather_features/all_to_all | solution.py:170
  9.4 9.6 %collective-permute-start = (bf16[128,256]{1,0:T(8,128)(2,1)}, bf16[128,256]{1,0:T(8,128)(2,1)S(1)}, u32[]{:S(2)}, u32[]{:S(2)}) collective-permute-start(bf16[128,256]{1,0:T(8,128)(2,1)} %param.6), channel_id=1, source_target_pairs={{0,1},{1,0},{2,3},{3,2},{4,5},{5,4},{6,7},{7,6},{8,9},{9,8},{10,11... | collective-permute-start | bytes 196616 | tf_op jit(solution)/shard_map/gather_features/ppermute | solution.py:181
  19.8 8.0 %collective-permute-start.1 = (bf16[2,128,256]{2,1,0:T(8,128)(2,1)S(1)}, bf16[2,128,256]{2,1,0:T(8,128)(2,1)S(1)}, u32[]{:S(2)}, u32[]{:S(2)}) collective-permute-start(bf16[2,128,256]{2,1,0:T(8,128)(2,1)S(1)} %pad_maximum_fusion.refs_0_), channel_id=1, source_target_pairs={{0,2},{1,3},{2,4},{3,5},{4,6},{5,7},{6,8},{7,9},{8,10},{9,11},{10,... | collective-permute-start | bytes 393224 | tf_op jit(solution)/shard_map/gather_features/ppermute | solution.py:178
  21.6 6.3 %collective-permute-start.3 = (bf16[2,128,256]{2,1,0:T(8,128)(2,1)S(1)}, bf16[2,128,256]{2,1,0:T(8,128)(2,1)S(1)}, u32[]{:S(2)}, u32[]{:S(2)}) collective-permute-start(bf16[2,128,256]{2,1,0:T(8,128)(2,1)S(1)} %pad_maximum_fusion.refs_0_), channel_id=1, source_target_pairs={{0,14},{1,15},{2,0},{3,1},{4,2},{5,3},{6,4},{7,5},{8,6},{9,7},{10,... | collective-permute-start | bytes 393224 | tf_op jit(solution)/shard_map/gather_features/ppermute | solution.py:178
  27.9 5.0 %collective-permute-start.2 = (bf16[2,128,256]{2,1,0:T(8,128)(2,1)S(1)}, bf16[2,128,256]{2,1,0:T(8,128)(2,1)S(1)}, u32[]{:S(2)}, u32[]{:S(2)}) collective-permute-start(bf16[2,128,256]{2,1,0:T(8,128)(2,1)S(1)} %collective-permute-done.1.refs_1_), channel_id=1, source_target_pairs={{0,2},{1,3},{2,4},{3,5},{4,6},{5,7},{6,8},{7,9},{8,10},{9,11},{10,... | collective-permute-start | bytes 393224 | tf_op jit(solution)/shard_map/gather_features/ppermute | solution.py:178
  27.9 5.0 %collective-permute-start.4 = (bf16[2,128,256]{2,1,0:T(8,128)(2,1)S(1)}, bf16[2,128,256]{2,1,0:T(8,128)(2,1)S(1)}, u32[]{:S(2)}, u32[]{:S(2)}) collective-permute-start(bf16[2,128,256]{2,1,0:T(8,128)(2,1)S(1)} %collective-permute-done.3.refs_2_), channel_id=1, source_target_pairs={{0,14},{1,15},{2,0},{3,1},{4,2},{5,3},{6,4},{7,5},{8,6},{9,7},{10,... | collective-permute-start | bytes 393224 | tf_op jit(solution)/shard_map/gather_features/ppermute | solution.py:178
  32.9 8.5 %collective-permute-start.5 = (bf16[2,128,256]{2,1,0:T(8,128)(2,1)S(1)}, bf16[2,128,256]{2,1,0:T(8,128)(2,1)S(1)}, u32[]{:S(2)}, u32[]{:S(2)}) collective-permute-start(bf16[2,128,256]{2,1,0:T(8,128)(2,1)S(1)} %collective-permute-done.2.refs_3_), channel_id=1, source_target_pairs={{0,2},{1,3},{2,4},{3,5},{4,6},{5,7},{6,8},{7,9},{8,10},{9,11},{10,... | collective-permute-start | bytes 393224 | tf_op jit(solution)/shard_map/gather_features/ppermute | solution.py:178
  33.8 0.7 copy-start.2
  35.4 6.0 %collective-permute-start.6 = (bf16[2,128,256]{2,1,0:T(8,128)(2,1)S(1)}, bf16[2,128,256]{2,1,0:T(8,128)(2,1)S(1)}, u32[]{:S(2)}, u32[]{:S(2)}) collective-permute-start(bf16[2,128,256]{2,1,0:T(8,128)(2,1)S(1)} %collective-permute-done.4.refs_4_), channel_id=1, source_target_pairs={{0,14},{1,15},{2,0},{3,1},{4,2},{5,3},{6,4},{7,5},{8,6},{9,7},{10,... | collective-permute-start | bytes 393224 | tf_op jit(solution)/shard_map/gather_features/ppermute | solution.py:178
  41.5 5.3 %collective-permute-start.8 = (bf16[128,256]{1,0:T(8,128)(2,1)S(1)}, bf16[128,256]{1,0:T(8,128)(2,1)S(1)}, u32[]{:S(2)}, u32[]{:S(2)}) collective-permute-start(bf16[128,256]{1,0:T(8,128)(2,1)S(1)} %slice_bitcast_fusion), channel_id=1, source_target_pairs={{0,14},{1,15},{2,0},{3,1},{4,2},{5,3},{6,4},{7,5},{8,6},{9,7},{10,... | collective-permute-start | bytes 196616 | tf_op jit(solution)/shard_map/ppermute | solution.py:178
  45.4 4.3 %collective-permute-start.7 = (bf16[128,256]{1,0:T(8,128)(2,1)S(1)}, bf16[128,256]{1,0:T(8,128)(2,1)S(1)}, u32[]{:S(2)}, u32[]{:S(2)}) collective-permute-start(bf16[128,256]{1,0:T(8,128)(2,1)S(1)} %slice_bitcast_fusion.1), channel_id=1, source_target_pairs={{0,2},{1,3},{2,4},{3,5},{4,6},{5,7},{6,8},{7,9},{8,10},{9,11},{10,... | collective-permute-start | bytes 196616 | tf_op jit(solution)/shard_map/ppermute | solution.py:178
  49.8 16.5 %copy-start.1 = (f32[2048]{0:T(1024)S(1)}, f32[2048]{0:T(1024)}, u32[]{:S(2)}) copy-start(f32[2048]{0:T(1024)} %param.8) | copy-start | bytes 24580
  50.4 42.1 %copy-start = (f32[2048]{0:T(1024)S(1)}, f32[2048]{0:T(1024)}, u32[]{:S(2)}) copy-start(f32[2048]{0:T(1024)} %param.9) | copy-start | bytes 24580

commit v3 on v2

--- a/solution.py
+++ b/solution.py
@@ -9,7 +9,7 @@
 from jax.sharding import PartitionSpec as P
 
 ITERS = 3
-UNROLL = 2
+UNROLL = 4
 FIELDS = 5
 LOW = -1e30
 LN2 = math.log(2.0)
@@ -20,7 +20,10 @@
 PARAMS = pltpu.CompilerParams(vmem_limit_bytes=8 * 1024 * 1024)
 
 
-def plan_kernel(blocks, slots, targets, room, cand_ref, counts_ref, plan_ref):
+def plan_kernel(blocks, slots, targets, room, cand_ref, counts_ref, src_ref, tgt_ref, plan_ref,
+                src_log_ref, tgt_log_ref):
+    src_log_ref[...] = jnp.log2(src_ref[...])
+    tgt_log_ref[...] = jnp.log2(tgt_ref[...])
     spare = blocks * targets
     here = lax.axis_index("tgt")
     deep, side = here // 2, here % 2
@@ -89,7 +92,7 @@
     parts = parts_ref[...]
     highest = jnp.max(parts, axis=0)
     totals = jnp.sum(jnp.exp2(parts - highest[None]), axis=0)
-    return jnp.log2(weight_ref[...]) - (highest + jnp.log2(totals))
+    return weight_ref[...] - (highest + jnp.log2(totals))
 
 
 def matmul(left, right, scale):
@@ -165,11 +168,6 @@
     dual_ref[...] = potential(parts_ref, weight_ref) * LN2
 
 
-def spread(rows, axis):
-    whole = jnp.broadcast_to(rows[None], (lax.axis_size(axis),) + rows.shape)
-    return lax.all_to_all(whole, axis, 0, 0)
-
-
 def ring(rows, beside):
     size = lax.axis_size("tgt")
     stages = size // 2
@@ -179,6 +177,9 @@
             value, "tgt", [(k, (k // 2 + by) % stages * 2 + k % 2) for k in range(size)])
 
     other = lax.ppermute(rows, "tgt", [(k, k ^ 1) for k in range(size)])
+    whole = jnp.broadcast_to(beside[0][None], (lax.axis_size("src"),) + beside[0].shape)
+    whole, weight, other = lax.optimization_barrier((whole, beside[1], other))
+    beside = lax.all_to_all(whole, "src", 0, 0), weight
     own = jnp.stack([rows, other])
     up, down, chunks = own, own, [own]
     for hop in range(1, stages // 2):
@@ -204,19 +205,23 @@
     src_weight = src_weight.reshape(blocks, size)
     tgt_weight = tgt_weight.reshape(targets, size)
 
-    plan = pl.pallas_call(
+    plan, src_weight, tgt_weight = pl.pallas_call(
         functools.partial(plan_kernel, blocks, slots, targets, room),
-        out_shape=pltpu.SMEM(((FIELDS + 1) * room,), jnp.int32),
-        in_specs=[SMEM, SMEM],
-        out_specs=SMEM,
+        out_shape=(
+            pltpu.SMEM(((FIELDS + 1) * room,), jnp.int32),
+            jax.ShapeDtypeStruct(src_weight.shape, jnp.float32),
+            jax.ShapeDtypeStruct(tgt_weight.shape, jnp.float32),
+        ),
+        in_specs=[SMEM, SMEM, VMEM, VMEM],
+        out_specs=(SMEM, VMEM, VMEM),
         compiler_params=PARAMS,
         name="plan",
-    )(cand.reshape(-1), counts.reshape(-1))
+    )(cand.reshape(-1), counts.reshape(-1), src_weight, tgt_weight)
     plan = pltpu.with_memory_space_constraint(plan, pltpu.SMEM)
 
     with jax.named_scope("gather_features"):
-        target_rows = spread(tgt_feat, "src")
-        chunks, last_chunk, target_rows = ring(src_feat, target_rows)
+        chunks, last_chunk, target_rows = ring(src_feat, (tgt_feat, src_weight))
+        target_rows, src_weight = target_rows
 
     tables = [pltpu.VMEM((blocks * targets + 8, size), jnp.float32)] * 2
     tiles = pltpu.VMEM((held, size, size), jnp.float32)

time: 150 us -> 134 us (0.89)
  blocking collectives: 89.8 us -> 80.2 us
  waiting for transfers between devices: 14.4 us -> 8.77 us
    all_to_all x3, blocking collectives: 48.7 us -> 36 us  [on_device(): parts = lax.all_to_all(parts, 'src', 0, 0)]
    ppermute x1, waiting for transfers between devices: 6.98 us -> 0.01 us  [ring(): other = lax.ppermute(rows, 'tgt', [(k, k ^ 1) for k in range(size)])]
    all_to_all x3, blocking collectives: 41.1 us -> 44.2 us  [on_device(): parts = lax.all_to_all(parts, 'tgt', 0, 0)]
  transfers between devices with their start and end apart: 10 -> 10, of which waited for: 5 -> 4; matrix products, arithmetic and copies ran while one was open for 1% -> 1% of each run, Pallas kernels for 3% -> 3%
where the time goes in v3:
time: 134 us; the launch traced here: 133 us
  blocking collectives  80.2 us (60%)
  starting transfers between devices  24.4 us (18%)
  Pallas kernels  13.5 us (10%)
  waiting for transfers between devices  8.77 us (7%)
  local copies, waits for them, and re-layouts  4.83 us (4%)
    all_to_all x3, blocking collectives, on_device(): parts = lax.all_to_all(parts, 'tgt', 0, 0)  44.2 us
    all_to_all x3, blocking collectives, on_device(): parts = lax.all_to_all(parts, 'src', 0, 0)  36 us
    ppermute x8, starting transfers between devices, along_z(): lax.ppermute(value, 'tgt', [(k, (k // 2 + by) % stages * 2 + k % 2) for k...  15.2 us
    ppermute x8, waiting for transfers between devices, along_z(): lax.ppermute(value, 'tgt', [(k, (k // 2 + by) % stages * 2 + k % 2) for k...  8.77 us
    pallas_call x5, Pallas kernels, sweep(): pl.pallas_call(functools.partial(pass_kernel, room, stages, own, row, kep...  7.79 us
    all_to_all x1, starting transfers between devices, ring(): beside = (lax.all_to_all(whole, 'src', 0, 0), weight)  5.36 us
    pallas_call x3, Pallas kernels, first_rows(): pl.pallas_call(functools.partial(first_kernel, room, scale, first, len(so...  3.97 us
    ppermute x1, starting transfers between devices, ring(): other = lax.ppermute(rows, 'tgt', [(k, k ^ 1) for k in range(size)])  3.83 us
  transfers between devices with their start and end apart: 10, of which 4 were waited for; matrix products, arithmetic and copies ran while one was open for 1% of the time, Pallas kernels for 3%

profile of v3, /device:TPU:1, one launch (start us, length us, event | category | flops | bytes accessed | tf_op | source)
XLA Modules:
  0.0 133.3 jit_solution(7565360036841748980)
XLA Ops:
  0.6 3.8 %collective-permute-start = (bf16[128,256]{1,0:T(8,128)(2,1)}, bf16[128,256]{1,0:T(8,128)(2,1)S(1)}, u32[]{:S(2)}, u32[]{:S(2)}) collective-permute-start(bf16[128,256]{1,0:T(8,128)(2,1)} %param.6), channel_id=1, source_target_pairs={{0,1},{1,0},{2,3},{3,2},{4,5},{5,4},{6,7},{7,6},{8,9},{9,8},{10,11... | collective-permute-start | bytes 196616 | tf_op jit(solution)/shard_map/gather_features/ppermute | solution.py:179
  7.4 1.1 plan.1
  8.5 1.9 %broadcast_in_dim.2 = bf16[16,128,256]{2,1,0:T(8,128)(2,1)} broadcast(bf16[128,256]{1,0:T(8,128)(2,1)} %param.7), dimensions={1,2} | broadcast | bytes 1114112 | tf_op jit(solution)/shard_map/gather_features/broadcast_in_dim | solution.py:180
  10.4 5.4 %all-to-all-start = ((bf16[16,128,256]{2,1,0:T(8,128)(2,1)}), bf16[16,128,256]{2,1,0:T(8,128)(2,1)S(1)}, u32[]{:S(2)}, u32[]{:S(2)}) async-start(bf16[16,128,256]{2,1,0:T(8,128)(2,1)} %broadcast_in_dim.2), calls=%async_computation | async-start | bytes 2097152 | tf_op jit(solution)/shard_map/gather_features/all_to_all | solution.py:182
  16.7 5.6 %collective-permute-start.3 = (bf16[2,128,256]{2,1,0:T(8,128)(2,1)S(1)}, bf16[2,128,256]{2,1,0:T(8,128)(2,1)S(1)}, u32[]{:S(2)}, u32[]{:S(2)}) collective-permute-start(bf16[2,128,256]{2,1,0:T(8,128)(2,1)S(1)} %pad_maximum_fusion.refs_0_), channel_id=1, source_target_pairs={{0,14},{1,15},{2,0},{3,1},{4,2},{5,3},{6,4},{7,5},{8,6},{9,7},{10,... | collective-permute-start | bytes 393224 | tf_op jit(solution)/shard_map/gather_features/ppermute | solution.py:176
  22.2 2.8 %collective-permute-done.3.refs_2_ = bf16[2,128,256]{2,1,0:T(8,128)(2,1)S(1)} collective-permute-done((bf16[2,128,256]{2,1,0:T(8,128)(2,1)S(1)}, bf16[2,128,256]{2,1,0:T(8,128)(2,1)S(1)}, u32[]{:S(2)}, u32[]{:S(2)}) %collective-permute-start.3) | collective-permute-done | bytes 131104 | tf_op jit(solution)/shard_map/gather_features/ppermute | solution.py:176
  25.1 3.4 %collective-permute-start.4 = (bf16[2,128,256]{2,1,0:T(8,128)(2,1)S(1)}, bf16[2,128,256]{2,1,0:T(8,128)(2,1)S(1)}, u32[]{:S(2)}, u32[]{:S(2)}) collective-permute-start(bf16[2,128,256]{2,1,0:T(8,128)(2,1)S(1)} %collective-permute-done.3.refs_2_), channel_id=1, source_target_pairs={{0,14},{1,15},{2,0},{3,1},{4,2},{5,3},{6,4},{7,5},{8,6},{9,7},{10,... | collective-permute-start | bytes 393224 | tf_op jit(solution)/shard_map/gather_features/ppermute | solution.py:176
  28.5 1.9 %collective-permute-done.4.refs_4_ = bf16[2,128,256]{2,1,0:T(8,128)(2,1)S(1)} collective-permute-done((bf16[2,128,256]{2,1,0:T(8,128)(2,1)S(1)}, bf16[2,128,256]{2,1,0:T(8,128)(2,1)S(1)}, u32[]{:S(2)}, u32[]{:S(2)}) %collective-permute-start.4) | collective-permute-done | bytes 131104 | tf_op jit(solution)/shard_map/gather_features/ppermute | solution.py:176
  30.4 3.1 %collective-permute-done.2.refs_3_ = bf16[2,128,256]{2,1,0:T(8,128)(2,1)S(1)} collective-permute-done((bf16[2,128,256]{2,1,0:T(8,128)(2,1)S(1)}, bf16[2,128,256]{2,1,0:T(8,128)(2,1)S(1)}, u32[]{:S(2)}, u32[]{:S(2)}) %collective-permute-start.2) | collective-permute-done | bytes 131104 | tf_op jit(solution)/shard_map/gather_features/ppermute | solution.py:176
  33.5 3.5 %collective-permute-start.6 = (bf16[2,128,256]{2,1,0:T(8,128)(2,1)S(1)}, bf16[2,128,256]{2,1,0:T(8,128)(2,1)S(1)}, u32[]{:S(2)}, u32[]{:S(2)}) collective-permute-start(bf16[2,128,256]{2,1,0:T(8,128)(2,1)S(1)} %collective-permute-done.4.refs_4_), channel_id=1, source_target_pairs={{0,14},{1,15},{2,0},{3,1},{4,2},{5,3},{6,4},{7,5},{8,6},{9,7},{10,... | collective-permute-start | bytes 393224 | tf_op jit(solution)/shard_map/gather_features/ppermute | solution.py:176
  37.0 2.4 %rows_early.1 = (f32[128,128,128]{2,1,0:T(8,128)S(1)}, f32[128,128,128]{2,1,0:T(8,128)S(1)}, f32[16,128]{1,0:T(8,128)S(1)}) custom-call(s32[768]{0:T(1024)S(4)} %get-tuple-element.26.plan_ref, bf16[16,128,256]{2,1,0:T(8,128)(2,1)S(1)} %all-to-all-done.tgt_ref, bf16[2,128,256]{2,1,0:T(8,128)(2,1)S(1)} %pad_maximum_fusion.refs_0_, ...), custom_call_target="tpu_custom_call" | custom-call | flops 218103808 | bytes 1703936 | tf_op jit(solution)/shard_map/rows_early/pallas_call | solution.py:236
  39.6 2.7 %collective-permute-start.8 = (bf16[128,256]{1,0:T(8,128)(2,1)S(1)}, bf16[128,256]{1,0:T(8,128)(2,1)S(1)}, u32[]{:S(2)}, u32[]{:S(2)}) collective-permute-start(bf16[128,256]{1,0:T(8,128)(2,1)S(1)} %slice_bitcast_fusion), channel_id=1, source_target_pairs={{0,14},{1,15},{2,0},{3,1},{4,2},{5,3},{6,4},{7,5},{8,6},{9,7},{10,... | collective-permute-start | bytes 196616 | tf_op jit(solution)/shard_map/ppermute | solution.py:176
  43.0 0.9 collective-permute-done.7
  44.7 18.2 %all_to_all.35.parts_ref = f32[16,16,128]{2,1,0:T(8,128)S(1)} all-to-all(f32[16,16,128]{2,1,0:T(8,128)S(1)} %get-tuple-element.43), channel_id=1, replica_groups=mesh['src'=16,'tgt'=16] {'tgt'}, dimensions={0} | all-to-all | bytes 262144 | tf_op jit(solution)/shard_map/exchange_rows/all_to_all | solution.py:272
  62.9 1.5 %columns.3 = f32[16,16,128]{2,1,0:T(8,128)S(1)} custom-call(s32[768]{0:T(1024)S(4)} %get-tuple-element.26.plan_ref, f32[16,16,128]{2,1,0:T(8,128)S(1)} %all_to_all.35.parts_ref, f32[16,128]{1,0:T(8,128)S(1)} %get-tuple-element.44.weight_ref, f32[128,128,128]{2,1,0:T(8,128)S(1)} %get-tuple-element.45.scores_ref), custom_call_target="tpu_custom_call" | custom-call | tf_op jit(solution)/shard_map/columns/pallas_call | solution.py:258
  64.4 14.1 %all_to_all.36.parts_ref = f32[16,16,128]{2,1,0:T(8,128)S(1)} all-to-all(f32[16,16,128]{2,1,0:T(8,128)S(1)} %columns.3), channel_id=1, replica_groups=mesh['src'=16,'tgt'=16] {'src'}, dimensions={0} | all-to-all | bytes 262144 | tf_op jit(solution)/shard_map/exchange_columns/all_to_all | solution.py:276
  78.4 1.4 %rows.2 = f32[16,16,128]{2,1,0:T(8,128)S(1)} custom-call(s32[768]{0:T(1024)S(4)} %get-tuple-element.26.plan_ref, f32[16,16,128]{2,1,0:T(8,128)S(1)} %all_to_all.36.parts_ref, f32[16,128]{1,0:T(8,128)S(1)} %get-tuple-element.46.weight_ref, f32[128,128,128]{2,1,0:T(8,128)S(1)} %get-tuple-element.47.scores_ref), custom_call_target="tpu_custom_call" | custom-call | tf_op jit(solution)/shard_map/rows/pallas_call | solution.py:258
  79.9 13.0 %all_to_all.37.parts_ref = f32[16,16,128]{2,1,0:T(8,128)S(1)} all-to-all(f32[16,16,128]{2,1,0:T(8,128)S(1)} %rows.2), channel_id=1, replica_groups=mesh['src'=16,'tgt'=16] {'tgt'}, dimensions={0} | all-to-all | bytes 262144 | tf_op jit(solution)/shard_map/exchange_rows/all_to_all | solution.py:272
  92.8 1.5 %columns.4 = f32[16,16,128]{2,1,0:T(8,128)S(1)} custom-call(s32[768]{0:T(1024)S(4)} %get-tuple-element.26.plan_ref, f32[16,16,128]{2,1,0:T(8,128)S(1)} %all_to_all.37.parts_ref, f32[16,128]{1,0:T(8,128)S(1)} %get-tuple-element.44.weight_ref, f32[128,128,128]{2,1,0:T(8,128)S(1)} %get-tuple-element.45.scores_ref), custom_call_target="tpu_custom_call" | custom-call | tf_op jit(solution)/shard_map/columns/pallas_call | solution.py:258
  94.3 10.9 %all_to_all.38.parts_ref = f32[16,16,128]{2,1,0:T(8,128)S(1)} all-to-all(f32[16,16,128]{2,1,0:T(8,128)S(1)} %columns.4), channel_id=1, replica_groups=mesh['src'=16,'tgt'=16] {'src'}, dimensions={0} | all-to-all | bytes 262144 | tf_op jit(solution)/shard_map/exchange_columns/all_to_all | solution.py:276
  105.2 1.4 %rows.3 = f32[16,16,128]{2,1,0:T(8,128)S(1)} custom-call(s32[768]{0:T(1024)S(4)} %get-tuple-element.26.plan_ref, f32[16,16,128]{2,1,0:T(8,128)S(1)} %all_to_all.38.parts_ref, f32[16,128]{1,0:T(8,128)S(1)} %get-tuple-element.46.weight_ref, f32[128,128,128]{2,1,0:T(8,128)S(1)} %get-tuple-element.47.scores_ref), custom_call_target="tpu_custom_call" | custom-call | tf_op jit(solution)/shard_map/rows/pallas_call | solution.py:258
  106.7 13.0 %all_to_all.39.parts_ref = f32[16,16,128]{2,1,0:T(8,128)S(1)} all-to-all(f32[16,16,128]{2,1,0:T(8,128)S(1)} %rows.3), channel_id=1, replica_groups=mesh['src'=16,'tgt'=16] {'tgt'}, dimensions={0} | all-to-all | bytes 262144 | tf_op jit(solution)/shard_map/exchange_rows/all_to_all | solution.py:272
  119.7 2.0 %columns.5 = (f32[16,16,128]{2,1,0:T(8,128)S(1)}, f32[16,128]{1,0:T(8,128)}) custom-call(s32[768]{0:T(1024)S(4)} %get-tuple-element.26.plan_ref, f32[16,16,128]{2,1,0:T(8,128)S(1)} %all_to_all.39.parts_ref, f32[16,128]{1,0:T(8,128)S(1)} %get-tuple-element.44.weight_ref, f32[128,128,128]{2,1,0:T(8,128)S(1)} %get-tuple-element.45.scores_ref), custom_call_target="tpu_custom_call" | custom-call | tf_op jit(solution)/shard_map/columns/pallas_call | solution.py:258
  121.7 11.0 %all_to_all.40.parts_ref = f32[16,16,128]{2,1,0:T(8,128)S(1)} all-to-all(f32[16,16,128]{2,1,0:T(8,128)S(1)} %get-tuple-element.49), channel_id=1, replica_groups=mesh['src'=16,'tgt'=16] {'src'}, dimensions={0} | all-to-all | bytes 262144 | tf_op jit(solution)/shard_map/exchange_columns/all_to_all | solution.py:276
  (25 shorter events, 6.0 us)
Async XLA Ops:
  0.6 7.9 %collective-permute-start = (bf16[128,256]{1,0:T(8,128)(2,1)}, bf16[128,256]{1,0:T(8,128)(2,1)S(1)}, u32[]{:S(2)}, u32[]{:S(2)}) collective-permute-start(bf16[128,256]{1,0:T(8,128)(2,1)} %param.6), channel_id=1, source_target_pairs={{0,1},{1,0},{2,3},{3,2},{4,5},{5,4},{6,7},{7,6},{8,9},{9,8},{10,11... | collective-permute-start | bytes 196616 | tf_op jit(solution)/shard_map/gather_features/ppermute | solution.py:179
  5.3 0.7 copy-start
  6.0 0.7 copy-start.1
  6.7 0.7 copy-start.2
  10.4 23.1 %all-to-all-start = ((bf16[16,128,256]{2,1,0:T(8,128)(2,1)}), bf16[16,128,256]{2,1,0:T(8,128)(2,1)S(1)}, u32[]{:S(2)}, u32[]{:S(2)}) async-start(bf16[16,128,256]{2,1,0:T(8,128)(2,1)} %broadcast_in_dim.2), calls=%async_computation | async-start | bytes 2097152 | tf_op jit(solution)/shard_map/gather_features/all_to_all | solution.py:182
  16.7 8.4 %collective-permute-start.3 = (bf16[2,128,256]{2,1,0:T(8,128)(2,1)S(1)}, bf16[2,128,256]{2,1,0:T(8,128)(2,1)S(1)}, u32[]{:S(2)}, u32[]{:S(2)}) collective-permute-start(bf16[2,128,256]{2,1,0:T(8,128)(2,1)S(1)} %pad_maximum_fusion.refs_0_), channel_id=1, source_target_pairs={{0,14},{1,15},{2,0},{3,1},{4,2},{5,3},{6,4},{7,5},{8,6},{9,7},{10,... | collective-permute-start | bytes 393224 | tf_op jit(solution)/shard_map/gather_features/ppermute | solution.py:176
  22.2 6.3 %collective-permute-start.1 = (bf16[2,128,256]{2,1,0:T(8,128)(2,1)S(1)}, bf16[2,128,256]{2,1,0:T(8,128)(2,1)S(1)}, u32[]{:S(2)}, u32[]{:S(2)}) collective-permute-start(bf16[2,128,256]{2,1,0:T(8,128)(2,1)S(1)} %pad_maximum_fusion.refs_0_), channel_id=1, source_target_pairs={{0,2},{1,3},{2,4},{3,5},{4,6},{5,7},{6,8},{7,9},{8,10},{9,11},{10,... | collective-permute-start | bytes 393224 | tf_op jit(solution)/shard_map/gather_features/ppermute | solution.py:176
  25.1 5.4 %collective-permute-start.4 = (bf16[2,128,256]{2,1,0:T(8,128)(2,1)S(1)}, bf16[2,128,256]{2,1,0:T(8,128)(2,1)S(1)}, u32[]{:S(2)}, u32[]{:S(2)}) collective-permute-start(bf16[2,128,256]{2,1,0:T(8,128)(2,1)S(1)} %collective-permute-done.3.refs_2_), channel_id=1, source_target_pairs={{0,14},{1,15},{2,0},{3,1},{4,2},{5,3},{6,4},{7,5},{8,6},{9,7},{10,... | collective-permute-start | bytes 393224 | tf_op jit(solution)/shard_map/gather_features/ppermute | solution.py:176
  28.5 5.0 %collective-permute-start.2 = (bf16[2,128,256]{2,1,0:T(8,128)(2,1)S(1)}, bf16[2,128,256]{2,1,0:T(8,128)(2,1)S(1)}, u32[]{:S(2)}, u32[]{:S(2)}) collective-permute-start(bf16[2,128,256]{2,1,0:T(8,128)(2,1)S(1)} %collective-permute-done.1.refs_1_), channel_id=1, source_target_pairs={{0,2},{1,3},{2,4},{3,5},{4,6},{5,7},{6,8},{7,9},{8,10},{9,11},{10,... | collective-permute-start | bytes 393224 | tf_op jit(solution)/shard_map/gather_features/ppermute | solution.py:176
  33.5 5.9 %collective-permute-start.5 = (bf16[2,128,256]{2,1,0:T(8,128)(2,1)S(1)}, bf16[2,128,256]{2,1,0:T(8,128)(2,1)S(1)}, u32[]{:S(2)}, u32[]{:S(2)}) collective-permute-start(bf16[2,128,256]{2,1,0:T(8,128)(2,1)S(1)} %collective-permute-done.2.refs_3_), channel_id=1, source_target_pairs={{0,2},{1,3},{2,4},{3,5},{4,6},{5,7},{6,8},{7,9},{8,10},{9,11},{10,... | collective-permute-start | bytes 393224 | tf_op jit(solution)/shard_map/gather_features/ppermute | solution.py:176
  33.5 5.9 %collective-permute-start.6 = (bf16[2,128,256]{2,1,0:T(8,128)(2,1)S(1)}, bf16[2,128,256]{2,1,0:T(8,128)(2,1)S(1)}, u32[]{:S(2)}, u32[]{:S(2)}) collective-permute-start(bf16[2,128,256]{2,1,0:T(8,128)(2,1)S(1)} %collective-permute-done.4.refs_4_), channel_id=1, source_target_pairs={{0,14},{1,15},{2,0},{3,1},{4,2},{5,3},{6,4},{7,5},{8,6},{9,7},{10,... | collective-permute-start | bytes 393224 | tf_op jit(solution)/shard_map/gather_features/ppermute | solution.py:176
  39.5 4.4 %collective-permute-start.7 = (bf16[128,256]{1,0:T(8,128)(2,1)S(1)}, bf16[128,256]{1,0:T(8,128)(2,1)S(1)}, u32[]{:S(2)}, u32[]{:S(2)}) collective-permute-start(bf16[128,256]{1,0:T(8,128)(2,1)S(1)} %slice_bitcast_fusion.1), channel_id=1, source_target_pairs={{0,2},{1,3},{2,4},{3,5},{4,6},{5,7},{6,8},{7,9},{8,10},{9,11},{10,... | collective-permute-start | bytes 196616 | tf_op jit(solution)/shard_map/ppermute | solution.py:176
  39.6 4.3 %collective-permute-start.8 = (bf16[128,256]{1,0:T(8,128)(2,1)S(1)}, bf16[128,256]{1,0:T(8,128)(2,1)S(1)}, u32[]{:S(2)}, u32[]{:S(2)}) collective-permute-start(bf16[128,256]{1,0:T(8,128)(2,1)S(1)} %slice_bitcast_fusion), channel_id=1, source_target_pairs={{0,14},{1,15},{2,0},{3,1},{4,2},{5,3},{6,4},{7,5},{8,6},{9,7},{10,... | collective-permute-start | bytes 196616 | tf_op jit(solution)/shard_map/ppermute | solution.py:176

commit v4 on v1

v4 whole, which is shorter than its diff:
```python
import functools
import math

import jax
import jax.numpy as jnp
from jax import lax
from jax.experimental import pallas as pl
from jax.experimental.pallas import tpu as pltpu
from jax.sharding import Mesh
from jax.sharding import PartitionSpec as P

ITERS = 3
UNROLL = 8
FIELDS = 5
LOW = -1e30
LN2 = math.log(2.0)
LOG2E = math.log2(math.e)

SRC = {"x": 4, "l": 2, "c": 2}
TGT = {"z": 8, "h": 2}
ROW_GROUP = ("z", "c")
COLUMN_GROUP = ("x", "l", "h")
LAST_GROUP = ("x", "l", "c", "h")
PIECES = (8,)

VMEM = pl.BlockSpec(memory_space=pltpu.VMEM)
SMEM = pl.BlockSpec(memory_space=pltpu.SMEM)
ANY = pl.BlockSpec(memory_space=pl.ANY)
PARAMS = pltpu.CompilerParams(vmem_limit_bytes=8 * 1024 * 1024)


def arrival(stages):
    offsets = [0]
    for hop in range(1, stages // 2):
        offsets += [-hop, hop]
    return offsets + [stages // 2]


def prepare_kernel(slots, own_hbm, tgt_hbm, *refs):
    lists_hbm, whole_ref, held_ref, tgt_ref, info_ref, refs, sems = refs[:4], *refs[4:8], refs[8:-1], refs[-1]
    pairs = ((tgt_hbm, tgt_ref), (own_hbm, held_ref)) + tuple(zip(lists_hbm, refs))
    moves = [pltpu.make_async_copy(source, target, sems.at[n]) for n, (source, target) in enumerate(pairs)]
    for move in moves:
        move.start()
    info_ref[...] = jnp.zeros(info_ref.shape, jnp.float32)
    for move in moves:
        move.wait()
    for flip, (cand_ref, counts_ref) in enumerate((refs[:2], refs[2:])):
        blocks = cand_ref.shape[2]
        for slot in range(slots):
            info_ref[8 * flip + slot : 8 * flip + slot + 1, :blocks] = cand_ref[slot].astype(jnp.float32)
        info_ref[8 * flip + slots : 8 * flip + slots + 1, :blocks] = counts_ref[...].astype(jnp.float32)
    size = tgt_ref.shape[0]
    info = info_ref[...].astype(whole_ref.dtype)
    for part in range(whole_ref.shape[0]):
        whole_ref[part, :size, :] = tgt_ref[...]
        whole_ref[part, size:, :] = info


def plan_kernel(stages, slots, room, rows_ref, src_hbm, tgt_hbm, plan_ref, src_log_ref, tgt_log_ref, src_ref,
                tgt_ref, lists_ref, info_ref, sems):
    moves = (pltpu.make_async_copy(src_hbm, src_ref, sems.at[0]), pltpu.make_async_copy(tgt_hbm, tgt_ref, sems.at[1]))
    for move in moves:
        move.start()
    deep, side, core = lax.axis_index("z"), lax.axis_index("h"), lax.axis_index("c")
    pair = (lax.axis_index("x") * 2 + lax.axis_index("l")) * 2
    lanes = lists_ref.shape[1]
    size = rows_ref.shape[1] - 16
    for flip in range(2):
        rows = rows_ref[pair + (side + flip) % 2, size:, :lanes].astype(jnp.float32)
        lists_ref[16 * flip : 16 * flip + 16, :] = rows.astype(jnp.int32)
    fetch = pltpu.make_async_copy(lists_ref, info_ref, sems.at[2])
    fetch.start()
    fetch.wait()
    blocks = 2 * stages
    spare = blocks * blocks

    def put(at, block, target, row, column, place):
        for field, value in enumerate((block, target, row, column, place)):
            plan_ref[field * room + at] = value

    total = 0
    offsets = arrival(stages)
    chunk = 0
    for piece, length in enumerate(PIECES):
        plan_ref[FIELDS * room + piece] = total // UNROLL
        for place in range(2 * length):
            depth = (deep + offsets[chunk + place // 2] + stages) % stages
            first = 8 * (place % 2)
            block = depth * 2 + (core + place % 2) % 2
            row = depth * 2 + side
            for flip in range(2):

                def add(slot, at, first=first, flip=flip, row=row, block=block, place=place):
                    local = info_ref[16 * flip + first + slot, row]
                    target = local - local % 2 + (side + flip) % 2
                    put(at, block, target, target * blocks + block, block * blocks + target, place)
                    return at + jnp.where(local % 2 == core, 1, 0)

                total = lax.fori_loop(0, info_ref[16 * flip + first + slots, row], add, total)
        for extra in range(UNROLL - 1):
            put(total + extra, 0, 0, spare, spare, 0)
        total = (total + UNROLL - 1) // UNROLL * UNROLL
        chunk += length
    plan_ref[FIELDS * room + len(PIECES)] = total // UNROLL
    for move in moves:
        move.wait()
    for row in range(stages):
        src_log_ref[row : row + 1, :] = jnp.log2(src_ref[pl.ds(row * 2 + side, 1), :])
        tgt_log_ref[row : row + 1, :] = jnp.log2(tgt_ref[pl.ds(row * 2 + core, 1), :])


def clear(high_ref, total_ref):
    high_ref[...] = jnp.full(high_ref.shape, LOW, jnp.float32)
    total_ref[...] = jnp.zeros(total_ref.shape, jnp.float32)


def keep_stats(shifted, row, high_ref, total_ref):
    highest = jnp.max(shifted, axis=0, keepdims=True)
    high_ref[pl.ds(row, 1), :] = highest
    total_ref[pl.ds(row, 1), :] = jnp.sum(jnp.exp2(shifted - highest), axis=0, keepdims=True)


def local_lse(high_ref, total_ref, kept):
    outer = (high_ref.shape[0] - 8) // kept
    shape = (outer, kept, high_ref.shape[1])
    high = high_ref[: outer * kept, :].reshape(shape)
    total = total_ref[: outer * kept, :].reshape(shape)
    highest = jnp.max(high, axis=0)
    totals = jnp.sum(total * jnp.exp2(high - highest[None]), axis=0)
    return highest + jnp.log2(totals)


def copies(local, log_ref, out_ref):
    kept = local.shape[0]
    for part in range(out_ref.shape[0]):
        out_ref[part, :kept, :] = local
        if log_ref is not None:
            out_ref[part, kept:, :] = log_ref[...]


def potential(parts_ref, weight):
    parts = parts_ref[:, : weight.shape[0], :]
    highest = jnp.max(parts, axis=0)
    totals = jnp.sum(jnp.exp2(parts - highest[None]), axis=0)
    return weight - (highest + jnp.log2(totals))


def matmul(left, right, scale):
    return scale * lax.dot_general(
        left, right, (((1,), (1,)), ((), ())), preferred_element_type=jnp.float32)


def first_kernel(room, scale, piece, plan_ref, tgt_ref, *refs):
    count = 2 * PIECES[piece]
    features, refs = refs[:count], refs[count:]
    log_ref = earlier_ref = None
    if piece:
        earlier_ref, refs = refs[0], refs[3:]
    if piece == len(PIECES) - 1:
        log_ref, refs = refs[0], refs[1:]
    flipped_ref, scores_ref, out_ref, held_ref, high_ref, total_ref = refs
    for place, ref in enumerate(features):
        held_ref[place] = ref[...]
    clear(high_ref, total_ref)

    def group(step, carry):
        for lane in range(UNROLL):
            at = step * UNROLL + lane
            left, right = held_ref[plan_ref[4 * room + at]], tgt_ref[plan_ref[room + at], : held_ref.shape[1], :]
            flipped = matmul(right, left, scale)
            flipped_ref[at] = flipped
            scores_ref[at] = matmul(left, right, scale)
            keep_stats(flipped, plan_ref[2 * room + at], high_ref, total_ref)
        return carry

    bounds = FIELDS * room + piece
    lax.fori_loop(plan_ref[bounds], plan_ref[bounds + 1], group, 0)
    local = local_lse(high_ref, total_ref, out_ref.shape[0])
    if piece:
        local = jnp.maximum(local, earlier_ref[...])
    if log_ref is None:
        out_ref[...] = local
    else:
        copies(local, log_ref, out_ref)


def pass_kernel(room, own, row, fresh, first, emit, plan_ref, parts_ref, weight_ref, scores_ref, *refs):
    log_ref = weight_ref if first else None
    out_ref, refs = refs[0], refs[1:]
    if fresh:
        kept_ref, refs = refs[0], refs[1:]
        blocks = kept_ref.shape[0]
        for block in range(blocks):
            at = blocks + block // 2
            kept_ref[block : block + 1, :] = parts_ref[block % 2, at : at + 1, :]
        weight_ref = kept_ref
    if emit:
        dual_ref, refs = refs[0], refs[1:]
    column_ref, high_ref, total_ref = refs
    dual = potential(parts_ref, weight_ref[...])
    blocks = dual.shape[0]
    if emit:
        high_ref[:blocks, :] = dual * LN2
        for block in range(blocks // 2):
            dual_ref[block : block + 1, :] = high_ref[pl.ds(2 * block + lax.axis_index("c"), 1), :]
    turned = dual.T
    for block in range(blocks):
        column_ref[block] = jnp.broadcast_to(turned[:, block : block + 1], column_ref.shape[1:])
    clear(high_ref, total_ref)

    def group(step, carry):
        for lane in range(UNROLL):
            at = step * UNROLL + lane
            shifted = scores_ref[at] + column_ref[plan_ref[own * room + at]]
            keep_stats(shifted, plan_ref[row * room + at], high_ref, total_ref)
        return carry

    lax.fori_loop(0, plan_ref[FIELDS * room + len(PIECES)], group, 0)
    local = local_lse(high_ref, total_ref, blocks)
    if not emit:
        copies(local, log_ref, out_ref)
        return
    for block in range(blocks):
        at = block % 2 * (blocks // 2) + block // 2
        high_ref[at : at + 1, :] = local[block : block + 1, :]
    for part in range(out_ref.shape[0]):
        out_ref[part] = high_ref[pl.ds(part % 2 * (blocks // 2), blocks // 2), :]


def interleave(out_ref, axis, mine_ref, other_ref):
    side = lax.axis_index(axis)
    for block in range(mine_ref.shape[0]):
        out_ref[pl.ds(2 * block + side, 1), :] = mine_ref[block : block + 1, :]
        out_ref[pl.ds(2 * block + 1 - side, 1), :] = other_ref[block : block + 1, :]


def last_kernel(parts_ref, weight_ref, mine_ref, other_ref, src_ref, tgt_ref, lse_ref):
    interleave(src_ref, "h", mine_ref, other_ref)
    for core in range(2):
        parts = [parts_ref[part] for part in range(parts_ref.shape[0]) if part // 2 % 2 == core]
        highest = functools.reduce(jnp.maximum, parts)
        lse = highest + jnp.log2(sum(jnp.exp2(part - highest) for part in parts))
        for block in range(lse.shape[0]):
            at = 2 * block + core
            lse_ref[at : at + 1, :] = lse[block : block + 1, :]
    tgt_ref[...] = (jnp.log2(weight_ref[...]) - lse_ref[...]) * LN2


def cost(pairs):
    return pl.CostEstimate(flops=pairs * 2 * 128 * 128 * 256, bytes_accessed=pairs * 65536, transcendentals=0)


def in_hbm(value):
    return pltpu.with_memory_space_constraint(value, pltpu.HBM)


def swap(value, axis):
    return lax.ppermute(value, axis, [(0, 1), (1, 0)])


def along_z(value, by):
    stages = lax.axis_size("z")
    return lax.ppermute(value, "z", [(k, (k + by) % stages) for k in range(stages)])


def on_device(src_feat, tgt_feat, src_weight, tgt_weight, cand, counts):
    slots = cand.shape[2]
    size, features = src_feat.shape
    stages = lax.axis_size("z")
    blocks = 2 * stages
    held = -(-2 * blocks * slots // UNROLL) * UNROLL + len(PIECES) * UNROLL
    room = -(-held // 128) * 128
    scale = LOG2E / math.sqrt(features)

    lists = (cand.transpose(2, 1, 0), counts.T)
    across = tuple(swap(part, "c") for part in lists)
    whole, own = pl.pallas_call(
        functools.partial(prepare_kernel, slots),
        out_shape=(
            jax.ShapeDtypeStruct((blocks, size + 16, features), tgt_feat.dtype),
            pltpu.VMEM(src_feat.shape, src_feat.dtype),
        ),
        in_specs=[ANY] * 6,
        out_specs=(VMEM, VMEM),
        scratch_shapes=[pltpu.VMEM(tgt_feat.shape, tgt_feat.dtype), pltpu.VMEM((16, features), jnp.float32)]
        + [pltpu.VMEM((slots, 1, blocks), jnp.int32), pltpu.VMEM((1, blocks), jnp.int32)] * 2
        + [pltpu.SemaphoreType.DMA((6,))],
        compiler_params=PARAMS,
        name="prepare",
    )(in_hbm(src_feat), in_hbm(tgt_feat), *map(in_hbm, lists), *across)
    with jax.named_scope("gather_features"):
        gated = (swap(src_feat, "c"), along_z(src_feat, 1), along_z(src_feat, -1))
        whole, other, up, down = lax.optimization_barrier((whole, *gated))
        target_rows = lax.all_to_all(whole, COLUMN_GROUP, 0, 0)
        chunks = [src_feat, up, down]
        for _ in range(2, stages // 2):
            up, down = along_z(up, 1), along_z(down, -1)
            chunks += [up, down]
        chunks += [along_z(up, 1)]
        pairs = [own, other] + [part for chunk in chunks[1:] for part in (chunk, swap(chunk, "c"))]

    half = jax.ShapeDtypeStruct((stages, size), jnp.float32)
    plan, src_log, tgt_log = pl.pallas_call(
        functools.partial(plan_kernel, stages, slots, room),
        out_shape=(pltpu.SMEM(((FIELDS + 1) * room,), jnp.int32), half, half),
        in_specs=[VMEM] + [ANY] * 2,
        out_specs=(SMEM, VMEM, VMEM),
        scratch_shapes=[pltpu.VMEM((blocks, size), jnp.float32)] * 2
        + [pltpu.VMEM((32, size), jnp.int32), pltpu.SMEM((32, size), jnp.int32), pltpu.SemaphoreType.DMA((3,))],
        compiler_params=PARAMS,
        name="plan",
    )(target_rows, in_hbm(src_weight.reshape(blocks, size)), in_hbm(tgt_weight.reshape(blocks, size)))
    plan = pltpu.with_memory_space_constraint(plan, pltpu.SMEM)

    tables = [pltpu.VMEM((blocks * blocks + 8, size), jnp.float32)] * 2
    tiles = pltpu.VMEM((held, size, size), jnp.float32)
    whole_rows = jax.ShapeDtypeStruct((blocks, size), jnp.float32)
    parts_of = lambda kept: jax.ShapeDtypeStruct((blocks, kept, size), jnp.float32)

    def first_rows(piece, some, local, scored, out, log, name):
        kept = [pltpu.with_memory_space_constraint(part, pltpu.VMEM) for part in scored]
        more = ([local] + kept if scored else []) + log
        given = 2 + len(some)
        *scored, local = pl.pallas_call(
            functools.partial(first_kernel, room, scale, piece),
            out_shape=(tiles, tiles, out),
            in_specs=[SMEM] + [VMEM] * (1 + len(some) + len(more)),
            out_specs=(VMEM, VMEM, VMEM),
            scratch_shapes=[pltpu.VMEM((len(some), size, features), src_feat.dtype)] + tables,
            input_output_aliases={given + 1: 0, given + 2: 1} if scored else {},
            compiler_params=PARAMS,
            cost_estimate=cost(5 * PIECES[piece]),
            name=name,
        )(plan, target_rows, *some, *more)
        return scored, local

    (flipped, scores), parts = first_rows(0, pairs, None, (), parts_of(blocks + stages), [src_log], "scores_and_rows")

    def sweep(own, row, step, emit, parts, weight, tiles, name):
        first, fresh = name == "columns" and not step, weight is None
        shapes = (parts_of(blocks + stages if first else blocks),)
        if emit:
            shapes = (jax.ShapeDtypeStruct((2 * blocks, stages, size), jnp.float32),)
        shapes += (whole_rows,) * fresh + (half,) * emit
        weights = tgt_log if fresh else weight
        return pl.pallas_call(
            functools.partial(pass_kernel, room, own, row, fresh, first, emit),
            out_shape=shapes,
            in_specs=[SMEM, VMEM, VMEM, VMEM],
            out_specs=(VMEM,) * len(shapes),
            scratch_shapes=[pltpu.VMEM((blocks, size, size), jnp.float32)] + tables,
            compiler_params=PARAMS,
            name=name,
        )(plan, parts, weights, pltpu.with_memory_space_constraint(tiles, pltpu.VMEM))

    src_kept = tgt_kept = None
    for step in range(ITERS):
        if step:
            parts, *kept = sweep(1, 2, step, False, parts, tgt_kept, flipped, "rows")
            tgt_kept = kept[0] if kept else tgt_kept
        with jax.named_scope("exchange_rows"):
            parts = lax.all_to_all(parts, ROW_GROUP, 0, 0)
        last = step == ITERS - 1
        parts, *kept = sweep(0, 3, step, last, parts, src_kept, scores, "columns")
        if last:
            mine = kept.pop()
            other = swap(mine, "h")
        src_kept = kept[0] if kept else src_kept
        with jax.named_scope("exchange_columns"):
            parts = lax.all_to_all(parts, LAST_GROUP if last else COLUMN_GROUP, 0, 0)
    source_dual, target_dual = pl.pallas_call(
        last_kernel,
        out_shape=(whole_rows, whole_rows),
        in_specs=[VMEM] * 4,
        out_specs=(VMEM, VMEM),
        scratch_shapes=[pltpu.VMEM((blocks, size), jnp.float32)],
        compiler_params=PARAMS,
        name="last",
    )(parts, tgt_weight.reshape(blocks, size), mine, other)
    return (source_dual.reshape(-1), target_dual.reshape(-1))


def solution(mesh):
    fine = Mesh(mesh.devices.reshape(tuple(SRC.values()) + tuple(TGT.values())), tuple(SRC) + tuple(TGT))
    src, tgt = tuple(SRC), tuple(TGT)
    placed = (P(src + tgt, None), P(tgt + src, None), P(src), P(tgt), P(src, tgt, None), P(src, tgt))
    return jax.shard_map(
        on_device, mesh=fine, in_specs=placed, out_specs=(P(src), P(tgt)), check_vma=False
    )
```

time: 163 us -> 128 us (0.79)
  blocking collectives: 101 us -> 66.8 us
  starting transfers between devices: 10.6 us -> 36.1 us
  waiting for transfers between devices: 23.6 us -> 9.9 us
  Pallas kernels: 21.8 us -> 13.5 us
  local copies, waits for them, and re-layouts: 4.94 us -> 0.01 us
    all_to_all x7 -> x5, blocking collectives: 101 us -> 66.8 us  [the longest x3 46.4 us: on_device(): parts = lax.all_to_all(parts, ROW_GROUP, 0, 0)]
    ppermute x0 -> x18, starting transfers between devices: none -> 25.7 us  [the longest x11 16.2 us: swap(): return lax.ppermute(value, axis, [(0, 1), (1, 0)])]
    all_to_all x1 -> x2, waiting for transfers between devices: 23.6 us -> 3.48 us  [the longest x1 3.48 us: on_device(): parts = lax.all_to_all(parts, LAST_GROUP if last else COLUMN_GROUP, 0, 0)]
    pallas_call x8 -> x9, Pallas kernels: 21.8 us -> 13.5 us  [the longest x5 6.17 us: sweep(): pl.pallas_call(functools.partial(pass_kernel, room, own, row, fresh, firs...]
    ppermute x0 -> x18, waiting for transfers between devices: none -> 6.42 us  [the longest x7 4.01 us: along_z(): lax.ppermute(value, 'z', [(k, (k + by) % stages) for k in range(stages)])]
    broadcast_in_dim x2 -> x0, local copies, waits for them, and re-layouts: 2.86 us -> none  [spread(): whole = jnp.broadcast_to(rows[None], (lax.axis_size(axis),) + rows.shape)]
    all_to_all x1 -> x2, starting transfers between devices: 10.6 us -> 10.4 us  [the longest x1 6.76 us: on_device(): target_rows = lax.all_to_all(whole, COLUMN_GROUP, 0, 0)]
  transfers between devices with their start and end apart: 1 -> 20, of which waited for: 1 -> 6; matrix products, arithmetic and copies ran while one was open for 0% -> 0% of each run, Pallas kernels for 1% -> 3%
where the time goes in v4:
time: 128 us; the launch traced here: 127 us
  blocking collectives  66.8 us (52%)
  starting transfers between devices  36.1 us (28%)
  Pallas kernels  13.5 us (11%)
  waiting for transfers between devices  9.9 us (8%)
    all_to_all x3, blocking collectives, on_device(): parts = lax.all_to_all(parts, ROW_GROUP, 0, 0)  46.4 us
    all_to_all x2, blocking collectives, on_device(): parts = lax.all_to_all(parts, LAST_GROUP if last else COLUMN_GROUP, 0, 0)  20.5 us
    ppermute x11, starting transfers between devices, swap(): return lax.ppermute(value, axis, [(0, 1), (1, 0)])  16.2 us
    ppermute x7, starting transfers between devices, along_z(): lax.ppermute(value, 'z', [(k, (k + by) % stages) for k in range(stages)])  9.56 us
    all_to_all x1, starting transfers between devices, on_device(): target_rows = lax.all_to_all(whole, COLUMN_GROUP, 0, 0)  6.76 us
    pallas_call x5, Pallas kernels, sweep(): pl.pallas_call(functools.partial(pass_kernel, room, own, row, fresh, firs...  6.17 us
    ppermute x7, waiting for transfers between devices, along_z(): lax.ppermute(value, 'z', [(k, (k + by) % stages) for k in range(stages)])  4.01 us
    all_to_all x1, starting transfers between devices, on_device(): parts = lax.all_to_all(parts, LAST_GROUP if last else COLUMN_GROUP, 0, 0)  3.64 us
  transfers between devices with their start and end apart: 20, of which 6 were waited for; matrix products, arithmetic and copies ran while one was open for 0% of the time, Pallas kernels for 3%

profile of v4, /device:TPU:1, one launch (start us, length us, event | category | flops | bytes accessed | tf_op | source)
XLA Modules:
  0.0 127.2 jit_solution(2415217857542291715)
XLA Ops:
  0.6 3.3 %collective-permute-start.2 = (bf16[128,256]{1,0:T(8,128)(2,1)}, bf16[128,256]{1,0:T(8,128)(2,1)S(1)}, u32[]{:S(2)}, u32[]{:S(2)}) collective-permute-start(bf16[128,256]{1,0:T(8,128)(2,1)} %own_hbm.1), channel_id=1, source_target_pairs={{0,16},{16,0},{1,17},{17,1},{2,18},{18,2},{3,19},{19,3},{4,20},{20... | collective-permute-start | bytes 196616 | tf_op jit(solution)/shard_map/gather_features/ppermute | solution.py:259
  4.0 3.9 %collective-permute-start.4 = (bf16[128,256]{1,0:T(8,128)(2,1)}, bf16[128,256]{1,0:T(8,128)(2,1)S(1)}, u32[]{:S(2)}, u32[]{:S(2)}) collective-permute-start(bf16[128,256]{1,0:T(8,128)(2,1)} %own_hbm.1), channel_id=1, source_target_pairs={{0,14},{2,0},{4,2},{6,4},{8,6},{10,8},{12,10},{14,12},{1,15},{3,1}... | collective-permute-start | bytes 196616 | tf_op jit(solution)/shard_map/gather_features/ppermute | solution.py:264
  9.4 2.0 %prepare.1 = (bf16[16,144,256]{2,1,0:T(8,128)(2,1)}, bf16[128,256]{1,0:T(8,128)(2,1)S(1)}) custom-call(bf16[128,256]{1,0:T(8,128)(2,1)} %own_hbm.1, bf16[128,256]{1,0:T(8,128)(2,1)} %tgt_hbm.1, s32[6,1,16]{2,1,0:T(1,128)} %bitcast.10, s32[1,16]{1,0:T(1,128)} %bitcast.12, s32[6,1,16]{2,1,0:T(1,128)S(1)} %collective-permute-done.refs_2_, ...), custom_call_target="tpu_custom_call" | custom-call | tf_op jit(solution)/shard_map/prepare/pallas_call | solution.py:278
  12.4 6.8 %all-to-all-start = ((bf16[16,144,256]{2,1,0:T(8,128)(2,1)}), bf16[16,144,256]{2,1,0:T(8,128)(2,1)S(1)}, u32[]{:S(2)}, u32[]{:S(2)}) async-start(bf16[16,144,256]{2,1,0:T(8,128)(2,1)} %get-tuple-element.23), calls=%async_computation | async-start | bytes 2359296 | tf_op jit(solution)/shard_map/gather_features/all_to_all | solution.py:295
  19.2 2.7 %collective-permute-start.9 = (bf16[128,256]{1,0:T(8,128)(2,1)S(1)}, bf16[128,256]{1,0:T(8,128)(2,1)S(1)}, u32[]{:S(2)}, u32[]{:S(2)}) collective-permute-start(bf16[128,256]{1,0:T(8,128)(2,1)S(1)} %collective-permute-done.4.refs_4_), channel_id=1, source_target_pairs={{0,14},{2,0},{4,2},{6,4},{8,6},{10,8},{12,10},{14,12},{1,15},{3,1}... | collective-permute-start | bytes 196616 | tf_op jit(solution)/shard_map/gather_features/ppermute | solution.py:264
  21.9 1.6 %collective-permute-done.7.refs_6_ = bf16[128,256]{1,0:T(8,128)(2,1)S(1)} collective-permute-done((bf16[128,256]{1,0:T(8,128)(2,1)S(1)}, bf16[128,256]{1,0:T(8,128)(2,1)S(1)}, u32[]{:S(2)}, u32[]{:S(2)}) %collective-permute-start.7) | collective-permute-done | bytes 65568 | tf_op jit(solution)/shard_map/gather_features/ppermute | solution.py:264
  23.5 2.9 %collective-permute-start.5 = (bf16[128,256]{1,0:T(8,128)(2,1)S(1)}, bf16[128,256]{1,0:T(8,128)(2,1)S(1)}, u32[]{:S(2)}, u32[]{:S(2)}) collective-permute-start(bf16[128,256]{1,0:T(8,128)(2,1)S(1)} %collective-permute-done.3.refs_2_), channel_id=1, source_target_pairs={{0,16},{16,0},{1,17},{17,1},{2,18},{18,2},{3,19},{19,3},{4,20},{20... | collective-permute-start | bytes 196616 | tf_op jit(solution)/shard_map/gather_features/ppermute | solution.py:259
  26.5 3.0 %collective-permute-start.13 = (bf16[128,256]{1,0:T(8,128)(2,1)S(1)}, bf16[128,256]{1,0:T(8,128)(2,1)S(1)}, u32[]{:S(2)}, u32[]{:S(2)}) collective-permute-start(bf16[128,256]{1,0:T(8,128)(2,1)S(1)} %collective-permute-done.9.refs_8_), channel_id=1, source_target_pairs={{0,14},{2,0},{4,2},{6,4},{8,6},{10,8},{12,10},{14,12},{1,15},{3,1}... | collective-permute-start | bytes 196616 | tf_op jit(solution)/shard_map/gather_features/ppermute | solution.py:264
  29.4 2.5 %collective-permute-start.8 = (bf16[128,256]{1,0:T(8,128)(2,1)S(1)}, bf16[128,256]{1,0:T(8,128)(2,1)S(1)}, u32[]{:S(2)}, u32[]{:S(2)}) collective-permute-start(bf16[128,256]{1,0:T(8,128)(2,1)S(1)} %collective-permute-done.7.refs_6_), channel_id=1, source_target_pairs={{0,16},{16,0},{1,17},{17,1},{2,18},{18,2},{3,19},{19,3},{4,20},{20... | collective-permute-start | bytes 196616 | tf_op jit(solution)/shard_map/gather_features/ppermute | solution.py:259
  32.5 1.5 %collective-permute-done.15.refs_14_ = bf16[128,256]{1,0:T(8,128)(2,1)S(1)} collective-permute-done((bf16[128,256]{1,0:T(8,128)(2,1)S(1)}, bf16[128,256]{1,0:T(8,128)(2,1)S(1)}, u32[]{:S(2)}, u32[]{:S(2)}) %collective-permute-start.15) | collective-permute-done | bytes 65568 | tf_op jit(solution)/shard_map/gather_features/ppermute | solution.py:264
  34.0 3.4 %collective-permute-start.16 = (bf16[128,256]{1,0:T(8,128)(2,1)S(1)}, bf16[128,256]{1,0:T(8,128)(2,1)S(1)}, u32[]{:S(2)}, u32[]{:S(2)}) collective-permute-start(bf16[128,256]{1,0:T(8,128)(2,1)S(1)} %collective-permute-done.15.refs_14_), channel_id=1, source_target_pairs={{0,16},{16,0},{1,17},{17,1},{2,18},{18,2},{3,19},{19,3},{4,20},{20... | collective-permute-start | bytes 196616 | tf_op jit(solution)/shard_map/gather_features/ppermute | solution.py:259
  37.4 2.4 %plan.1 = (s32[1536]{0:T(1024)S(4)}, f32[8,128]{1,0:T(8,128)S(1)}, f32[8,128]{1,0:T(8,128)S(1)}) custom-call(bf16[16,144,256]{2,1,0:T(8,128)(2,1)S(1)} %all-to-all-done.rows_ref.tgt_ref, f32[16,128]{1,0:T(8,128)} %bitcast.8, f32[16,128]{1,0:T(8,128)} %bitcast.6), custom_call_target="tpu_custom_call" | custom-call | tf_op jit(solution)/shard_map/plan/pallas_call | solution.py:304
  39.9 2.3 %scores_and_rows.1 = (f32[200,128,128]{2,1,0:T(8,128)S(1)}, f32[200,128,128]{2,1,0:T(8,128)S(1)}, f32[16,24,128]{2,1,0:T(8,128)S(1)}) custom-call(s32[1536]{0:T(1024)S(4)} %get-tuple-element.24.plan_ref, bf16[16,144,256]{2,1,0:T(8,128)(2,1)S(1)} %all-to-all-done.rows_ref.tgt_ref, bf16[128,256]{1,0:T(8,128)(2,1)S(1)} %get-tuple-element.25.refs_0_, ...), custom_call_target="tpu_custom_call" | custom-call | flops 335544320 | bytes 2621440 | tf_op jit(solution)/shard_map/scores_and_rows/pallas_call | solution.py:325
  42.1 18.8 %all_to_all.35.parts_ref = f32[16,24,128]{2,1,0:T(8,128)S(1)} all-to-all(f32[16,24,128]{2,1,0:T(8,128)S(1)} %get-tuple-element.30), channel_id=1, replica_groups=mesh['x'=4,'l'=2,'c'=2,'z'=8,'h'=2] {'z','c'}, dimensions={0} | all-to-all | bytes 393216 | tf_op jit(solution)/shard_map/exchange_rows/all_to_all | solution.py:363
  61.0 1.1 columns.3
  62.1 10.8 %all_to_all.36.parts_ref = f32[16,24,128]{2,1,0:T(8,128)S(1)} all-to-all(f32[16,24,128]{2,1,0:T(8,128)S(1)} %get-tuple-element.33), channel_id=1, replica_groups=mesh['x'=4,'l'=2,'c'=2,'z'=8,'h'=2] {'x','l','h'}, dimensions={0} | all-to-all | bytes 393216 | tf_op jit(solution)/shard_map/exchange_columns/all_to_all | solution.py:371
  74.0 14.1 %all_to_all.37.parts_ref = f32[16,16,128]{2,1,0:T(8,128)S(1)} all-to-all(f32[16,16,128]{2,1,0:T(8,128)S(1)} %get-tuple-element.35), channel_id=1, replica_groups=mesh['x'=4,'l'=2,'c'=2,'z'=8,'h'=2] {'z','c'}, dimensions={0} | all-to-all | bytes 262144 | tf_op jit(solution)/shard_map/exchange_rows/all_to_all | solution.py:363
  89.2 9.7 %all_to_all.38.parts_ref = f32[16,16,128]{2,1,0:T(8,128)S(1)} all-to-all(f32[16,16,128]{2,1,0:T(8,128)S(1)} %columns.4), channel_id=1, replica_groups=mesh['x'=4,'l'=2,'c'=2,'z'=8,'h'=2] {'x','l','h'}, dimensions={0} | all-to-all | bytes 262144 | tf_op jit(solution)/shard_map/exchange_columns/all_to_all | solution.py:371
  100.0 13.5 %all_to_all.39.parts_ref = f32[16,16,128]{2,1,0:T(8,128)S(1)} all-to-all(f32[16,16,128]{2,1,0:T(8,128)S(1)} %rows.3), channel_id=1, replica_groups=mesh['x'=4,'l'=2,'c'=2,'z'=8,'h'=2] {'z','c'}, dimensions={0} | all-to-all | bytes 262144 | tf_op jit(solution)/shard_map/exchange_rows/all_to_all | solution.py:363
  113.4 1.8 %columns.5 = (f32[32,8,128]{2,1,0:T(8,128)}, f32[8,128]{1,0:T(8,128)S(1)}) custom-call(s32[1536]{0:T(1024)S(4)} %get-tuple-element.24.plan_ref, f32[16,16,128]{2,1,0:T(8,128)S(1)} %all_to_all.39.parts_ref, f32[16,128]{1,0:T(8,128)S(1)} %get-tuple-element.36.weight_ref, f32[200,128,128]{2,1,0:T(8,128)S(1)} %get-tuple-element.32.scores_ref), custom_call_target="tpu_custom_call" | custom-call | tf_op jit(solution)/shard_map/columns/pallas_call | solution.py:347
  115.2 3.6 %all-to-all-start.6 = ((f32[32,8,128]{2,1,0:T(8,128)}), f32[32,8,128]{2,1,0:T(8,128)S(1)}, u32[]{:S(2)}, u32[]{:S(2)}) async-start(f32[32,8,128]{2,1,0:T(8,128)} %get-tuple-element.38), calls=%async_computation.6 | async-start | bytes 262144 | tf_op jit(solution)/shard_map/exchange_columns/all_to_all | solution.py:371
  118.8 2.9 %collective-permute-start.17 = (f32[8,128]{1,0:T(8,128)S(1)}, f32[8,128]{1,0:T(8,128)S(1)}, u32[]{:S(2)}, u32[]{:S(2)}) collective-permute-start(f32[8,128]{1,0:T(8,128)S(1)} %get-tuple-element.39.mine_ref), channel_id=1, source_target_pairs={{0,1},{1,0},{2,3},{3,2},{4,5},{5,4},{6,7},{7,6},{8,9},{9,8},{10,11... | collective-permute-start | bytes 12296 | tf_op jit(solution)/shard_map/ppermute | solution.py:259
  121.7 1.3 %collective-permute-done.17.other_ref = f32[8,128]{1,0:T(8,128)S(1)} collective-permute-done((f32[8,128]{1,0:T(8,128)S(1)}, f32[8,128]{1,0:T(8,128)S(1)}, u32[]{:S(2)}, u32[]{:S(2)}) %collective-permute-start.17) | collective-permute-done | bytes 4128 | tf_op jit(solution)/shard_map/ppermute | solution.py:259
  123.0 3.5 %all-to-all-done.6.parts_ref = f32[32,8,128]{2,1,0:T(8,128)S(1)} async-done(((f32[32,8,128]{2,1,0:T(8,128)}), f32[32,8,128]{2,1,0:T(8,128)S(1)}, u32[]{:S(2)}, u32[]{:S(2)}) %all-to-all-start.6) | async-done | bytes 131104 | tf_op jit(solution)/shard_map/exchange_columns/all_to_all | solution.py:371
  (32 shorter events, 7.2 us)
Async XLA Ops:
  0.6 10.9 %collective-permute-start.2 = (bf16[128,256]{1,0:T(8,128)(2,1)}, bf16[128,256]{1,0:T(8,128)(2,1)S(1)}, u32[]{:S(2)}, u32[]{:S(2)}) collective-permute-start(bf16[128,256]{1,0:T(8,128)(2,1)} %own_hbm.1), channel_id=1, source_target_pairs={{0,16},{16,0},{1,17},{17,1},{2,18},{18,2},{3,19},{19,3},{4,20},{20... | collective-permute-start | bytes 196616 | tf_op jit(solution)/shard_map/gather_features/ppermute | solution.py:259
  4.0 7.5 %collective-permute-start.4 = (bf16[128,256]{1,0:T(8,128)(2,1)}, bf16[128,256]{1,0:T(8,128)(2,1)S(1)}, u32[]{:S(2)}, u32[]{:S(2)}) collective-permute-start(bf16[128,256]{1,0:T(8,128)(2,1)} %own_hbm.1), channel_id=1, source_target_pairs={{0,14},{2,0},{4,2},{6,4},{8,6},{10,8},{12,10},{14,12},{1,15},{3,1}... | collective-permute-start | bytes 196616 | tf_op jit(solution)/shard_map/gather_features/ppermute | solution.py:264
  7.8 4.5 %collective-permute-start.3 = (bf16[128,256]{1,0:T(8,128)(2,1)}, bf16[128,256]{1,0:T(8,128)(2,1)S(1)}, u32[]{:S(2)}, u32[]{:S(2)}) collective-permute-start(bf16[128,256]{1,0:T(8,128)(2,1)} %own_hbm.1), channel_id=1, source_target_pairs={{0,2},{2,4},{4,6},{6,8},{8,10},{10,12},{12,14},{14,0},{1,3},{3,5},... | collective-permute-start | bytes 196616 | tf_op jit(solution)/shard_map/gather_features/ppermute | solution.py:264
  7.8 1.6 %collective-permute-start = (s32[6,1,16]{2,1,0:T(1,128)}, s32[6,1,16]{2,1,0:T(1,128)S(1)}, u32[]{:S(2)}, u32[]{:S(2)}) collective-permute-start(s32[6,1,16]{2,1,0:T(1,128)} %bitcast.9), channel_id=1, source_target_pairs={{0,16},{16,0},{1,17},{17,1},{2,18},{18,2},{3,19},{19,3},{4,20},{20... | collective-permute-start | bytes 1160 | tf_op jit(solution)/shard_map/ppermute | solution.py:259
  8.2 1.3 collective-permute-start.1
  12.4 25.1 %all-to-all-start = ((bf16[16,144,256]{2,1,0:T(8,128)(2,1)}), bf16[16,144,256]{2,1,0:T(8,128)(2,1)S(1)}, u32[]{:S(2)}, u32[]{:S(2)}) async-start(bf16[16,144,256]{2,1,0:T(8,128)(2,1)} %get-tuple-element.23), calls=%async_computation | async-start | bytes 2359296 | tf_op jit(solution)/shard_map/gather_features/all_to_all | solution.py:295
  19.1 4.4 %collective-permute-start.7 = (bf16[128,256]{1,0:T(8,128)(2,1)S(1)}, bf16[128,256]{1,0:T(8,128)(2,1)S(1)}, u32[]{:S(2)}, u32[]{:S(2)}) collective-permute-start(bf16[128,256]{1,0:T(8,128)(2,1)S(1)} %collective-permute-done.3.refs_2_), channel_id=1, source_target_pairs={{0,2},{2,4},{4,6},{6,8},{8,10},{10,12},{12,14},{14,0},{1,3},{3,5},... | collective-permute-start | bytes 196616 | tf_op jit(solution)/shard_map/gather_features/ppermute | solution.py:264
  19.2 7.3 %collective-permute-start.9 = (bf16[128,256]{1,0:T(8,128)(2,1)S(1)}, bf16[128,256]{1,0:T(8,128)(2,1)S(1)}, u32[]{:S(2)}, u32[]{:S(2)}) collective-permute-start(bf16[128,256]{1,0:T(8,128)(2,1)S(1)} %collective-permute-done.4.refs_4_), channel_id=1, source_target_pairs={{0,14},{2,0},{4,2},{6,4},{8,6},{10,8},{12,10},{14,12},{1,15},{3,1}... | collective-permute-start | bytes 196616 | tf_op jit(solution)/shard_map/gather_features/ppermute | solution.py:264
  23.5 5.9 %collective-permute-start.11 = (bf16[128,256]{1,0:T(8,128)(2,1)S(1)}, bf16[128,256]{1,0:T(8,128)(2,1)S(1)}, u32[]{:S(2)}, u32[]{:S(2)}) collective-permute-start(bf16[128,256]{1,0:T(8,128)(2,1)S(1)} %collective-permute-done.7.refs_6_), channel_id=1, source_target_pairs={{0,2},{2,4},{4,6},{6,8},{8,10},{10,12},{12,14},{14,0},{1,3},{3,5},... | collective-permute-start | bytes 196616 | tf_op jit(solution)/shard_map/gather_features/ppermute | solution.py:264
  23.5 8.4 %collective-permute-start.5 = (bf16[128,256]{1,0:T(8,128)(2,1)S(1)}, bf16[128,256]{1,0:T(8,128)(2,1)S(1)}, u32[]{:S(2)}, u32[]{:S(2)}) collective-permute-start(bf16[128,256]{1,0:T(8,128)(2,1)S(1)} %collective-permute-done.3.refs_2_), channel_id=1, source_target_pairs={{0,16},{16,0},{1,17},{17,1},{2,18},{18,2},{3,19},{19,3},{4,20},{20... | collective-permute-start | bytes 196616 | tf_op jit(solution)/shard_map/gather_features/ppermute | solution.py:259
  26.5 5.6 %collective-permute-start.6 = (bf16[128,256]{1,0:T(8,128)(2,1)S(1)}, bf16[128,256]{1,0:T(8,128)(2,1)S(1)}, u32[]{:S(2)}, u32[]{:S(2)}) collective-permute-start(bf16[128,256]{1,0:T(8,128)(2,1)S(1)} %collective-permute-done.4.refs_4_), channel_id=1, source_target_pairs={{0,16},{16,0},{1,17},{17,1},{2,18},{18,2},{3,19},{19,3},{4,20},{20... | collective-permute-start | bytes 196616 | tf_op jit(solution)/shard_map/gather_features/ppermute | solution.py:259
  26.5 6.0 %collective-permute-start.13 = (bf16[128,256]{1,0:T(8,128)(2,1)S(1)}, bf16[128,256]{1,0:T(8,128)(2,1)S(1)}, u32[]{:S(2)}, u32[]{:S(2)}) collective-permute-start(bf16[128,256]{1,0:T(8,128)(2,1)S(1)} %collective-permute-done.9.refs_8_), channel_id=1, source_target_pairs={{0,14},{2,0},{4,2},{6,4},{8,6},{10,8},{12,10},{14,12},{1,15},{3,1}... | collective-permute-start | bytes 196616 | tf_op jit(solution)/shard_map/gather_features/ppermute | solution.py:264
  29.4 4.6 %collective-permute-start.15 = (bf16[128,256]{1,0:T(8,128)(2,1)S(1)}, bf16[128,256]{1,0:T(8,128)(2,1)S(1)}, u32[]{:S(2)}, u32[]{:S(2)}) collective-permute-start(bf16[128,256]{1,0:T(8,128)(2,1)S(1)} %collective-permute-done.11.refs_10_), channel_id=1, source_target_pairs={{0,2},{2,4},{4,6},{6,8},{8,10},{10,12},{12,14},{14,0},{1,3},{3,5},... | collective-permute-start | bytes 196616 | tf_op jit(solution)/shard_map/gather_features/ppermute | solution.py:264
  29.4 10.4 %collective-permute-start.8 = (bf16[128,256]{1,0:T(8,128)(2,1)S(1)}, bf16[128,256]{1,0:T(8,128)(2,1)S(1)}, u32[]{:S(2)}, u32[]{:S(2)}) collective-permute-start(bf16[128,256]{1,0:T(8,128)(2,1)S(1)} %collective-permute-done.7.refs_6_), channel_id=1, source_target_pairs={{0,16},{16,0},{1,17},{17,1},{2,18},{18,2},{3,19},{19,3},{4,20},{20... | collective-permute-start | bytes 196616 | tf_op jit(solution)/shard_map/gather_features/ppermute | solution.py:259
  31.9 7.9 %collective-permute-start.10 = (bf16[128,256]{1,0:T(8,128)(2,1)S(1)}, bf16[128,256]{1,0:T(8,128)(2,1)S(1)}, u32[]{:S(2)}, u32[]{:S(2)}) collective-permute-start(bf16[128,256]{1,0:T(8,128)(2,1)S(1)} %collective-permute-done.9.refs_8_), channel_id=1, source_target_pairs={{0,16},{16,0},{1,17},{17,1},{2,18},{18,2},{3,19},{19,3},{4,20},{20... | collective-permute-start | bytes 196616 | tf_op jit(solution)/shard_map/gather_features/ppermute | solution.py:259
  32.0 7.8 %collective-permute-start.12 = (bf16[128,256]{1,0:T(8,128)(2,1)S(1)}, bf16[128,256]{1,0:T(8,128)(2,1)S(1)}, u32[]{:S(2)}, u32[]{:S(2)}) collective-permute-start(bf16[128,256]{1,0:T(8,128)(2,1)S(1)} %collective-permute-done.11.refs_10_), channel_id=1, source_target_pairs={{0,16},{16,0},{1,17},{17,1},{2,18},{18,2},{3,19},{19,3},{4,20},{20... | collective-permute-start | bytes 196616 | tf_op jit(solution)/shard_map/gather_features/ppermute | solution.py:259
  32.5 7.4 %collective-permute-start.14 = (bf16[128,256]{1,0:T(8,128)(2,1)S(1)}, bf16[128,256]{1,0:T(8,128)(2,1)S(1)}, u32[]{:S(2)}, u32[]{:S(2)}) collective-permute-start(bf16[128,256]{1,0:T(8,128)(2,1)S(1)} %collective-permute-done.13.refs_12_), channel_id=1, source_target_pairs={{0,16},{16,0},{1,17},{17,1},{2,18},{18,2},{3,19},{19,3},{4,20},{20... | collective-permute-start | bytes 196616 | tf_op jit(solution)/shard_map/gather_features/ppermute | solution.py:259
  34.0 5.8 %collective-permute-start.16 = (bf16[128,256]{1,0:T(8,128)(2,1)S(1)}, bf16[128,256]{1,0:T(8,128)(2,1)S(1)}, u32[]{:S(2)}, u32[]{:S(2)}) collective-permute-start(bf16[128,256]{1,0:T(8,128)(2,1)S(1)} %collective-permute-done.15.refs_14_), channel_id=1, source_target_pairs={{0,16},{16,0},{1,17},{17,1},{2,18},{18,2},{3,19},{19,3},{4,20},{20... | collective-permute-start | bytes 196616 | tf_op jit(solution)/shard_map/gather_features/ppermute | solution.py:259
  98.8 27.7 %copy-start = (f32[2048]{0:T(1024)S(1)}, f32[2048]{0:T(1024)}, u32[]{:S(2)}) copy-start(f32[2048]{0:T(1024)} %param.9) | copy-start | bytes 24580
  115.2 11.3 %all-to-all-start.6 = ((f32[32,8,128]{2,1,0:T(8,128)}), f32[32,8,128]{2,1,0:T(8,128)S(1)}, u32[]{:S(2)}, u32[]{:S(2)}) async-start(f32[32,8,128]{2,1,0:T(8,128)} %get-tuple-element.38), calls=%async_computation.6 | async-start | bytes 262144 | tf_op jit(solution)/shard_map/exchange_columns/all_to_all | solution.py:371
  118.8 4.2 %collective-permute-start.17 = (f32[8,128]{1,0:T(8,128)S(1)}, f32[8,128]{1,0:T(8,128)S(1)}, u32[]{:S(2)}, u32[]{:S(2)}) collective-permute-start(f32[8,128]{1,0:T(8,128)S(1)} %get-tuple-element.39.mine_ref), channel_id=1, source_target_pairs={{0,1},{1,0},{2,3},{3,2},{4,5},{5,4},{6,7},{7,6},{8,9},{9,8},{10,11... | collective-permute-start | bytes 12296 | tf_op jit(solution)/shard_map/ppermute | solution.py:259

commit v5 on v4

--- a/solution.py
+++ b/solution.py
@@ -170,7 +170,7 @@
             left, right = held_ref[plan_ref[4 * room + at]], tgt_ref[plan_ref[room + at], : held_ref.shape[1], :]
             flipped = matmul(right, left, scale)
             flipped_ref[at] = flipped
-            scores_ref[at] = matmul(left, right, scale)
+            scores_ref[at] = flipped.T
             keep_stats(flipped, plan_ref[2 * room + at], high_ref, total_ref)
         return carry
 
@@ -195,9 +195,9 @@
             at = blocks + block // 2
             kept_ref[block : block + 1, :] = parts_ref[block % 2, at : at + 1, :]
         weight_ref = kept_ref
+    column_ref, high_ref, total_ref = refs[:3]
     if emit:
-        dual_ref, refs = refs[0], refs[1:]
-    column_ref, high_ref, total_ref = refs
+        dual_ref = refs[3]
     dual = potential(parts_ref, weight_ref[...])
     blocks = dual.shape[0]
     if emit:
@@ -225,23 +225,22 @@
         at = block % 2 * (blocks // 2) + block // 2
         high_ref[at : at + 1, :] = local[block : block + 1, :]
     for part in range(out_ref.shape[0]):
-        out_ref[part] = high_ref[pl.ds(part % 2 * (blocks // 2), blocks // 2), :]
-
-
-def interleave(out_ref, axis, mine_ref, other_ref):
-    side = lax.axis_index(axis)
-    for block in range(mine_ref.shape[0]):
-        out_ref[pl.ds(2 * block + side, 1), :] = mine_ref[block : block + 1, :]
-        out_ref[pl.ds(2 * block + 1 - side, 1), :] = other_ref[block : block + 1, :]
-
-
-def last_kernel(parts_ref, weight_ref, mine_ref, other_ref, src_ref, tgt_ref, lse_ref):
-    interleave(src_ref, "h", mine_ref, other_ref)
+        out_ref[part, : blocks // 2, :] = high_ref[pl.ds(part % 2 * (blocks // 2), blocks // 2), :]
+        out_ref[part, blocks // 2 :, :] = dual_ref[...]
+
+
+def last_kernel(parts_ref, weight_ref, src_ref, tgt_ref, lse_ref):
+    half = parts_ref.shape[1] // 2
+    place = (lax.axis_index("x") * 2 + lax.axis_index("l")) * 2 + lax.axis_index("c")
+    for side in range(2):
+        for block in range(half):
+            src_ref[2 * block + side : 2 * block + side + 1, :] = (
+                parts_ref[2 * place + side, half + block : half + block + 1, :])
     for core in range(2):
-        parts = [parts_ref[part] for part in range(parts_ref.shape[0]) if part // 2 % 2 == core]
+        parts = [parts_ref[part, :half, :] for part in range(parts_ref.shape[0]) if part // 2 % 2 == core]
         highest = functools.reduce(jnp.maximum, parts)
         lse = highest + jnp.log2(sum(jnp.exp2(part - highest) for part in parts))
-        for block in range(lse.shape[0]):
+        for block in range(half):
             at = 2 * block + core
             lse_ref[at : at + 1, :] = lse[block : block + 1, :]
     tgt_ref[...] = (jnp.log2(weight_ref[...]) - lse_ref[...]) * LN2
@@ -297,8 +296,8 @@
         for _ in range(2, stages // 2):
             up, down = along_z(up, 1), along_z(down, -1)
             chunks += [up, down]
-        chunks += [along_z(up, 1)]
         pairs = [own, other] + [part for chunk in chunks[1:] for part in (chunk, swap(chunk, "c"))]
+        pairs += [along_z(up, 1), along_z(pairs[-1], -1)]
 
     half = jax.ShapeDtypeStruct((stages, size), jnp.float32)
     plan, src_log, tgt_log = pl.pallas_call(
@@ -341,15 +340,16 @@
         first, fresh = name == "columns" and not step, weight is None
         shapes = (parts_of(blocks + stages if first else blocks),)
         if emit:
-            shapes = (jax.ShapeDtypeStruct((2 * blocks, stages, size), jnp.float32),)
-        shapes += (whole_rows,) * fresh + (half,) * emit
+            shapes = (jax.ShapeDtypeStruct((2 * blocks, blocks, size), jnp.float32),)
+        shapes += (whole_rows,) * fresh
         weights = tgt_log if fresh else weight
         return pl.pallas_call(
             functools.partial(pass_kernel, room, own, row, fresh, first, emit),
             out_shape=shapes,
             in_specs=[SMEM, VMEM, VMEM, VMEM],
             out_specs=(VMEM,) * len(shapes),
-            scratch_shapes=[pltpu.VMEM((blocks, size, size), jnp.float32)] + tables,
+            scratch_shapes=[pltpu.VMEM((blocks, size, size), jnp.float32)] + tables
+            + [pltpu.VMEM((stages, size), jnp.float32)] * emit,
             compiler_params=PARAMS,
             name=name,
         )(plan, parts, weights, pltpu.with_memory_space_constraint(tiles, pltpu.VMEM))
@@ -363,21 +363,18 @@
             parts = lax.all_to_all(parts, ROW_GROUP, 0, 0)
         last = step == ITERS - 1
         parts, *kept = sweep(0, 3, step, last, parts, src_kept, scores, "columns")
-        if last:
-            mine = kept.pop()
-            other = swap(mine, "h")
         src_kept = kept[0] if kept else src_kept
         with jax.named_scope("exchange_columns"):
             parts = lax.all_to_all(parts, LAST_GROUP if last else COLUMN_GROUP, 0, 0)
     source_dual, target_dual = pl.pallas_call(
         last_kernel,
         out_shape=(whole_rows, whole_rows),
-        in_specs=[VMEM] * 4,
+        in_specs=[VMEM] * 2,
         out_specs=(VMEM, VMEM),
         scratch_shapes=[pltpu.VMEM((blocks, size), jnp.float32)],
         compiler_params=PARAMS,
         name="last",
-    )(parts, tgt_weight.reshape(blocks, size), mine, other)
+    )(parts, tgt_weight.reshape(blocks, size))
     return (source_dual.reshape(-1), target_dual.reshape(-1))
 
 

time: 128 us -> 127 us (level)
  blocking collectives: 66.8 us -> 80.7 us
  starting transfers between devices: 36.1 us -> 27.8 us
  waiting for transfers between devices: 9.9 us -> 5.79 us
  Pallas kernels: 13.5 us -> 11.3 us
    all_to_all x2 -> x3, blocking collectives: 20.5 us -> 31.9 us  [on_device(): parts = lax.all_to_all(parts, LAST_GROUP if last else COLUMN_GROUP, 0, 0)]
    ppermute x11 -> x9, starting transfers between devices: 16.2 us -> 8.98 us  [swap(): return lax.ppermute(value, axis, [(0, 1), (1, 0)])]
    all_to_all x1 -> x0, starting transfers between devices: 3.64 us -> none  [on_device(): parts = lax.all_to_all(parts, LAST_GROUP if last else COLUMN_GROUP, 0, 0)]
    all_to_all x1 -> x0, waiting for transfers between devices: 3.48 us -> none  [on_device(): parts = lax.all_to_all(parts, LAST_GROUP if last else COLUMN_GROUP, 0, 0)]
    ppermute x7 -> x8, starting transfers between devices: 9.56 us -> 12 us  [along_z(): lax.ppermute(value, 'z', [(k, (k + by) % stages) for k in range(stages)])]
    all_to_all x3, blocking collectives: 46.4 us -> 48.7 us  [on_device(): parts = lax.all_to_all(parts, ROW_GROUP, 0, 0)]
    pallas_call x5, Pallas kernels: 6.17 us -> 4.85 us  [sweep(): pl.pallas_call(functools.partial(pass_kernel, room, own, row, fresh, firs...]
    ppermute x11 -> x9, waiting for transfers between devices: 2.42 us -> 1.12 us  [swap(): return lax.ppermute(value, axis, [(0, 1), (1, 0)])]
  transfers between devices with their start and end apart: 20 -> 18, of which waited for: 6 -> 4; matrix products, arithmetic and copies ran while one was open for 0% -> 0% of each run, Pallas kernels for 3% -> 4%
where the time goes in v5:
time: 127 us; the launch traced here: 126 us
  blocking collectives  80.7 us (64%)
  starting transfers between devices  27.8 us (22%)
  Pallas kernels  11.3 us (9%)
  waiting for transfers between devices  5.79 us (5%)
    all_to_all x3, blocking collectives, on_device(): parts = lax.all_to_all(parts, ROW_GROUP, 0, 0)  48.7 us
    all_to_all x3, blocking collectives, on_device(): parts = lax.all_to_all(parts, LAST_GROUP if last else COLUMN_GROUP, 0, 0)  31.9 us
    ppermute x8, starting transfers between devices, along_z(): lax.ppermute(value, 'z', [(k, (k + by) % stages) for k in range(stages)])  12 us
    ppermute x9, starting transfers between devices, swap(): return lax.ppermute(value, axis, [(0, 1), (1, 0)])  8.98 us
    all_to_all x1, starting transfers between devices, on_device(): target_rows = lax.all_to_all(whole, COLUMN_GROUP, 0, 0)  6.76 us
    pallas_call x5, Pallas kernels, sweep(): pl.pallas_call(functools.partial(pass_kernel, room, own, row, fresh, firs...  4.85 us
    ppermute x8, waiting for transfers between devices, along_z(): lax.ppermute(value, 'z', [(k, (k + by) % stages) for k in range(stages)])  4.67 us
  transfers between devices with their start and end apart: 18, of which 4 were waited for; matrix products, arithmetic and copies ran while one was open for 0% of the time, Pallas kernels for 4%

profile of v5, /device:TPU:1, one launch (start us, length us, event | category | flops | bytes accessed | tf_op | source)
XLA Modules:
  0.0 126.3 jit_solution(5880567421937214197)
XLA Ops:
  0.6 3.3 %collective-permute-start.2 = (bf16[128,256]{1,0:T(8,128)(2,1)}, bf16[128,256]{1,0:T(8,128)(2,1)S(1)}, u32[]{:S(2)}, u32[]{:S(2)}) collective-permute-start(bf16[128,256]{1,0:T(8,128)(2,1)} %own_hbm.1), channel_id=1, source_target_pairs={{0,16},{16,0},{1,17},{17,1},{2,18},{18,2},{3,19},{19,3},{4,20},{20... | collective-permute-start | bytes 196616 | tf_op jit(solution)/shard_map/gather_features/ppermute | solution.py:258
  4.0 3.9 %collective-permute-start.4 = (bf16[128,256]{1,0:T(8,128)(2,1)}, bf16[128,256]{1,0:T(8,128)(2,1)S(1)}, u32[]{:S(2)}, u32[]{:S(2)}) collective-permute-start(bf16[128,256]{1,0:T(8,128)(2,1)} %own_hbm.1), channel_id=1, source_target_pairs={{0,14},{2,0},{4,2},{6,4},{8,6},{10,8},{12,10},{14,12},{1,15},{3,1}... | collective-permute-start | bytes 196616 | tf_op jit(solution)/shard_map/gather_features/ppermute | solution.py:263
  8.3 1.1 collective-permute-done.1.refs_3_
  9.4 2.1 %prepare.1 = (bf16[16,144,256]{2,1,0:T(8,128)(2,1)}, bf16[128,256]{1,0:T(8,128)(2,1)S(1)}) custom-call(bf16[128,256]{1,0:T(8,128)(2,1)} %own_hbm.1, bf16[128,256]{1,0:T(8,128)(2,1)} %tgt_hbm.1, s32[6,1,16]{2,1,0:T(1,128)} %bitcast.10, s32[1,16]{1,0:T(1,128)} %bitcast.12, s32[6,1,16]{2,1,0:T(1,128)S(1)} %collective-permute-done.refs_2_, ...), custom_call_target="tpu_custom_call" | custom-call | tf_op jit(solution)/shard_map/prepare/pallas_call | solution.py:277
  12.4 6.8 %all-to-all-start = ((bf16[16,144,256]{2,1,0:T(8,128)(2,1)}), bf16[16,144,256]{2,1,0:T(8,128)(2,1)S(1)}, u32[]{:S(2)}, u32[]{:S(2)}) async-start(bf16[16,144,256]{2,1,0:T(8,128)(2,1)} %get-tuple-element.21), calls=%async_computation | async-start | bytes 2359296 | tf_op jit(solution)/shard_map/gather_features/all_to_all | solution.py:294
  19.1 2.2 %collective-permute-start.9 = (bf16[128,256]{1,0:T(8,128)(2,1)S(1)}, bf16[128,256]{1,0:T(8,128)(2,1)S(1)}, u32[]{:S(2)}, u32[]{:S(2)}) collective-permute-start(bf16[128,256]{1,0:T(8,128)(2,1)S(1)} %collective-permute-done.4.refs_4_), channel_id=1, source_target_pairs={{0,14},{2,0},{4,2},{6,4},{8,6},{10,8},{12,10},{14,12},{1,15},{3,1}... | collective-permute-start | bytes 196616 | tf_op jit(solution)/shard_map/gather_features/ppermute | solution.py:263
  21.3 1.3 %collective-permute-done.9.refs_8_ = bf16[128,256]{1,0:T(8,128)(2,1)S(1)} collective-permute-done((bf16[128,256]{1,0:T(8,128)(2,1)S(1)}, bf16[128,256]{1,0:T(8,128)(2,1)S(1)}, u32[]{:S(2)}, u32[]{:S(2)}) %collective-permute-start.9) | collective-permute-done | bytes 65568 | tf_op jit(solution)/shard_map/gather_features/ppermute | solution.py:263
  22.7 3.0 %collective-permute-start.13 = (bf16[128,256]{1,0:T(8,128)(2,1)S(1)}, bf16[128,256]{1,0:T(8,128)(2,1)S(1)}, u32[]{:S(2)}, u32[]{:S(2)}) collective-permute-start(bf16[128,256]{1,0:T(8,128)(2,1)S(1)} %collective-permute-done.9.refs_8_), channel_id=1, source_target_pairs={{0,14},{2,0},{4,2},{6,4},{8,6},{10,8},{12,10},{14,12},{1,15},{3,1}... | collective-permute-start | bytes 196616 | tf_op jit(solution)/shard_map/gather_features/ppermute | solution.py:263
  25.7 1.9 %collective-permute-start.5 = (bf16[128,256]{1,0:T(8,128)(2,1)S(1)}, bf16[128,256]{1,0:T(8,128)(2,1)S(1)}, u32[]{:S(2)}, u32[]{:S(2)}) collective-permute-start(bf16[128,256]{1,0:T(8,128)(2,1)S(1)} %collective-permute-done.3.refs_2_), channel_id=1, source_target_pairs={{0,16},{16,0},{1,17},{17,1},{2,18},{18,2},{3,19},{19,3},{4,20},{20... | collective-permute-start | bytes 196616 | tf_op jit(solution)/shard_map/gather_features/ppermute | solution.py:258
  27.7 1.8 %collective-permute-start.14 = (bf16[128,256]{1,0:T(8,128)(2,1)S(1)}, bf16[128,256]{1,0:T(8,128)(2,1)S(1)}, u32[]{:S(2)}, u32[]{:S(2)}) collective-permute-start(bf16[128,256]{1,0:T(8,128)(2,1)S(1)} %collective-permute-done.13.refs_12_), channel_id=1, source_target_pairs={{0,16},{16,0},{1,17},{17,1},{2,18},{18,2},{3,19},{19,3},{4,20},{20... | collective-permute-start | bytes 196616 | tf_op jit(solution)/shard_map/gather_features/ppermute | solution.py:258
  30.0 2.5 %collective-permute-done.11.refs_10_ = bf16[128,256]{1,0:T(8,128)(2,1)S(1)} collective-permute-done((bf16[128,256]{1,0:T(8,128)(2,1)S(1)}, bf16[128,256]{1,0:T(8,128)(2,1)S(1)}, u32[]{:S(2)}, u32[]{:S(2)}) %collective-permute-start.11) | collective-permute-done | bytes 65568 | tf_op jit(solution)/shard_map/gather_features/ppermute | solution.py:263
  33.3 3.0 %collective-permute-start.16 = (bf16[128,256]{1,0:T(8,128)(2,1)S(1)}, bf16[128,256]{1,0:T(8,128)(2,1)S(1)}, u32[]{:S(2)}, u32[]{:S(2)}) collective-permute-start(bf16[128,256]{1,0:T(8,128)(2,1)S(1)} %collective-permute-done.14.refs_13_), channel_id=1, source_target_pairs={{0,14},{2,0},{4,2},{6,4},{8,6},{10,8},{12,10},{14,12},{1,15},{3,1}... | collective-permute-start | bytes 196616 | tf_op jit(solution)/shard_map/gather_features/ppermute | solution.py:263
  36.3 2.4 %plan.1 = (s32[1536]{0:T(1024)S(4)}, f32[8,128]{1,0:T(8,128)S(1)}, f32[8,128]{1,0:T(8,128)S(1)}) custom-call(bf16[16,144,256]{2,1,0:T(8,128)(2,1)S(1)} %all-to-all-done.rows_ref.tgt_ref, f32[16,128]{1,0:T(8,128)} %bitcast.8, f32[16,128]{1,0:T(8,128)} %bitcast.6), custom_call_target="tpu_custom_call" | custom-call | tf_op jit(solution)/shard_map/plan/pallas_call | solution.py:303
  38.8 1.3 %scores_and_rows.1 = (f32[200,128,128]{2,1,0:T(8,128)S(1)}, f32[200,128,128]{2,1,0:T(8,128)S(1)}, f32[16,24,128]{2,1,0:T(8,128)S(1)}) custom-call(s32[1536]{0:T(1024)S(4)} %get-tuple-element.22.plan_ref, bf16[16,144,256]{2,1,0:T(8,128)(2,1)S(1)} %all-to-all-done.rows_ref.tgt_ref, bf16[128,256]{1,0:T(8,128)(2,1)S(1)} %get-tuple-element.23.refs_0_, ...), custom_call_target="tpu_custom_call" | custom-call | flops 335544320 | bytes 2621440 | tf_op jit(solution)/shard_map/scores_and_rows/pallas_call | solution.py:324
  40.1 20.6 %all_to_all.35.parts_ref = f32[16,24,128]{2,1,0:T(8,128)S(1)} all-to-all(f32[16,24,128]{2,1,0:T(8,128)S(1)} %get-tuple-element.28), channel_id=1, replica_groups=mesh['x'=4,'l'=2,'c'=2,'z'=8,'h'=2] {'z','c'}, dimensions={0} | all-to-all | bytes 393216 | tf_op jit(solution)/shard_map/exchange_rows/all_to_all | solution.py:363
  60.6 1.0 columns.3
  61.6 10.3 %all_to_all.36.parts_ref = f32[16,24,128]{2,1,0:T(8,128)S(1)} all-to-all(f32[16,24,128]{2,1,0:T(8,128)S(1)} %get-tuple-element.31), channel_id=1, replica_groups=mesh['x'=4,'l'=2,'c'=2,'z'=8,'h'=2] {'x','l','h'}, dimensions={0} | all-to-all | bytes 393216 | tf_op jit(solution)/shard_map/exchange_columns/all_to_all | solution.py:368
  71.9 1.0 rows.2
  72.8 14.2 %all_to_all.37.parts_ref = f32[16,16,128]{2,1,0:T(8,128)S(1)} all-to-all(f32[16,16,128]{2,1,0:T(8,128)S(1)} %get-tuple-element.33), channel_id=1, replica_groups=mesh['x'=4,'l'=2,'c'=2,'z'=8,'h'=2] {'z','c'}, dimensions={0} | all-to-all | bytes 262144 | tf_op jit(solution)/shard_map/exchange_rows/all_to_all | solution.py:363
  87.0 1.0 columns.4
  88.0 9.8 %all_to_all.38.parts_ref = f32[16,16,128]{2,1,0:T(8,128)S(1)} all-to-all(f32[16,16,128]{2,1,0:T(8,128)S(1)} %columns.4), channel_id=1, replica_groups=mesh['x'=4,'l'=2,'c'=2,'z'=8,'h'=2] {'x','l','h'}, dimensions={0} | all-to-all | bytes 262144 | tf_op jit(solution)/shard_map/exchange_columns/all_to_all | solution.py:368
  98.8 13.9 %all_to_all.39.parts_ref = f32[16,16,128]{2,1,0:T(8,128)S(1)} all-to-all(f32[16,16,128]{2,1,0:T(8,128)S(1)} %rows.3), channel_id=1, replica_groups=mesh['x'=4,'l'=2,'c'=2,'z'=8,'h'=2] {'z','c'}, dimensions={0} | all-to-all | bytes 262144 | tf_op jit(solution)/shard_map/exchange_rows/all_to_all | solution.py:363
  112.7 1.0 columns.5
  113.7 11.9 %all_to_all.40.parts_ref = f32[32,16,128]{2,1,0:T(8,128)S(1)} all-to-all(f32[32,16,128]{2,1,0:T(8,128)S(1)} %columns.5), channel_id=1, replica_groups=mesh['x'=4,'l'=2,'c'=2,'z'=8,'h'=2] {'x','l','c','h'}, dimensions={0} | all-to-all | bytes 524288 | tf_op jit(solution)/shard_map/exchange_columns/all_to_all | solution.py:368
  (29 shorter events, 4.4 us)
Async XLA Ops:
  0.6 10.9 %collective-permute-start.2 = (bf16[128,256]{1,0:T(8,128)(2,1)}, bf16[128,256]{1,0:T(8,128)(2,1)S(1)}, u32[]{:S(2)}, u32[]{:S(2)}) collective-permute-start(bf16[128,256]{1,0:T(8,128)(2,1)} %own_hbm.1), channel_id=1, source_target_pairs={{0,16},{16,0},{1,17},{17,1},{2,18},{18,2},{3,19},{19,3},{4,20},{20... | collective-permute-start | bytes 196616 | tf_op jit(solution)/shard_map/gather_features/ppermute | solution.py:258
  4.0 7.5 %collective-permute-start.4 = (bf16[128,256]{1,0:T(8,128)(2,1)}, bf16[128,256]{1,0:T(8,128)(2,1)S(1)}, u32[]{:S(2)}, u32[]{:S(2)}) collective-permute-start(bf16[128,256]{1,0:T(8,128)(2,1)} %own_hbm.1), channel_id=1, source_target_pairs={{0,14},{2,0},{4,2},{6,4},{8,6},{10,8},{12,10},{14,12},{1,15},{3,1}... | collective-permute-start | bytes 196616 | tf_op jit(solution)/shard_map/gather_features/ppermute | solution.py:263
  7.8 4.5 %collective-permute-start.3 = (bf16[128,256]{1,0:T(8,128)(2,1)}, bf16[128,256]{1,0:T(8,128)(2,1)S(1)}, u32[]{:S(2)}, u32[]{:S(2)}) collective-permute-start(bf16[128,256]{1,0:T(8,128)(2,1)} %own_hbm.1), channel_id=1, source_target_pairs={{0,2},{2,4},{4,6},{6,8},{8,10},{10,12},{12,14},{14,0},{1,3},{3,5},... | collective-permute-start | bytes 196616 | tf_op jit(solution)/shard_map/gather_features/ppermute | solution.py:263
  7.8 1.6 %collective-permute-start = (s32[6,1,16]{2,1,0:T(1,128)}, s32[6,1,16]{2,1,0:T(1,128)S(1)}, u32[]{:S(2)}, u32[]{:S(2)}) collective-permute-start(s32[6,1,16]{2,1,0:T(1,128)} %bitcast.9), channel_id=1, source_target_pairs={{0,16},{16,0},{1,17},{17,1},{2,18},{18,2},{3,19},{19,3},{4,20},{20... | collective-permute-start | bytes 1160 | tf_op jit(solution)/shard_map/ppermute | solution.py:258
  8.2 1.3 collective-permute-start.1
  12.4 23.9 %all-to-all-start = ((bf16[16,144,256]{2,1,0:T(8,128)(2,1)}), bf16[16,144,256]{2,1,0:T(8,128)(2,1)S(1)}, u32[]{:S(2)}, u32[]{:S(2)}) async-start(bf16[16,144,256]{2,1,0:T(8,128)(2,1)} %get-tuple-element.21), calls=%async_computation | async-start | bytes 2359296 | tf_op jit(solution)/shard_map/gather_features/all_to_all | solution.py:294
  19.1 3.5 %collective-permute-start.9 = (bf16[128,256]{1,0:T(8,128)(2,1)S(1)}, bf16[128,256]{1,0:T(8,128)(2,1)S(1)}, u32[]{:S(2)}, u32[]{:S(2)}) collective-permute-start(bf16[128,256]{1,0:T(8,128)(2,1)S(1)} %collective-permute-done.4.refs_4_), channel_id=1, source_target_pairs={{0,14},{2,0},{4,2},{6,4},{8,6},{10,8},{12,10},{14,12},{1,15},{3,1}... | collective-permute-start | bytes 196616 | tf_op jit(solution)/shard_map/gather_features/ppermute | solution.py:263
  21.3 6.2 %collective-permute-start.7 = (bf16[128,256]{1,0:T(8,128)(2,1)S(1)}, bf16[128,256]{1,0:T(8,128)(2,1)S(1)}, u32[]{:S(2)}, u32[]{:S(2)}) collective-permute-start(bf16[128,256]{1,0:T(8,128)(2,1)S(1)} %collective-permute-done.3.refs_2_), channel_id=1, source_target_pairs={{0,2},{2,4},{4,6},{6,8},{8,10},{10,12},{12,14},{14,0},{1,3},{3,5},... | collective-permute-start | bytes 196616 | tf_op jit(solution)/shard_map/gather_features/ppermute | solution.py:263
  22.7 5.0 %collective-permute-start.13 = (bf16[128,256]{1,0:T(8,128)(2,1)S(1)}, bf16[128,256]{1,0:T(8,128)(2,1)S(1)}, u32[]{:S(2)}, u32[]{:S(2)}) collective-permute-start(bf16[128,256]{1,0:T(8,128)(2,1)S(1)} %collective-permute-done.9.refs_8_), channel_id=1, source_target_pairs={{0,14},{2,0},{4,2},{6,4},{8,6},{10,8},{12,10},{14,12},{1,15},{3,1}... | collective-permute-start | bytes 196616 | tf_op jit(solution)/shard_map/gather_features/ppermute | solution.py:263
  25.7 3.9 %collective-permute-start.5 = (bf16[128,256]{1,0:T(8,128)(2,1)S(1)}, bf16[128,256]{1,0:T(8,128)(2,1)S(1)}, u32[]{:S(2)}, u32[]{:S(2)}) collective-permute-start(bf16[128,256]{1,0:T(8,128)(2,1)S(1)} %collective-permute-done.3.refs_2_), channel_id=1, source_target_pairs={{0,16},{16,0},{1,17},{17,1},{2,18},{18,2},{3,19},{19,3},{4,20},{20... | collective-permute-start | bytes 196616 | tf_op jit(solution)/shard_map/gather_features/ppermute | solution.py:258
  27.6 4.9 %collective-permute-start.11 = (bf16[128,256]{1,0:T(8,128)(2,1)S(1)}, bf16[128,256]{1,0:T(8,128)(2,1)S(1)}, u32[]{:S(2)}, u32[]{:S(2)}) collective-permute-start(bf16[128,256]{1,0:T(8,128)(2,1)S(1)} %collective-permute-done.7.refs_6_), channel_id=1, source_target_pairs={{0,2},{2,4},{4,6},{6,8},{8,10},{10,12},{12,14},{14,0},{1,3},{3,5},... | collective-permute-start | bytes 196616 | tf_op jit(solution)/shard_map/gather_features/ppermute | solution.py:263
  27.6 4.9 %collective-permute-start.6 = (bf16[128,256]{1,0:T(8,128)(2,1)S(1)}, bf16[128,256]{1,0:T(8,128)(2,1)S(1)}, u32[]{:S(2)}, u32[]{:S(2)}) collective-permute-start(bf16[128,256]{1,0:T(8,128)(2,1)S(1)} %collective-permute-done.4.refs_4_), channel_id=1, source_target_pairs={{0,16},{16,0},{1,17},{17,1},{2,18},{18,2},{3,19},{19,3},{4,20},{20... | collective-permute-start | bytes 196616 | tf_op jit(solution)/shard_map/gather_features/ppermute | solution.py:258
  27.7 5.6 %collective-permute-start.14 = (bf16[128,256]{1,0:T(8,128)(2,1)S(1)}, bf16[128,256]{1,0:T(8,128)(2,1)S(1)}, u32[]{:S(2)}, u32[]{:S(2)}) collective-permute-start(bf16[128,256]{1,0:T(8,128)(2,1)S(1)} %collective-permute-done.13.refs_12_), channel_id=1, source_target_pairs={{0,16},{16,0},{1,17},{17,1},{2,18},{18,2},{3,19},{19,3},{4,20},{20... | collective-permute-start | bytes 196616 | tf_op jit(solution)/shard_map/gather_features/ppermute | solution.py:258
  29.5 9.2 %collective-permute-start.8 = (bf16[128,256]{1,0:T(8,128)(2,1)S(1)}, bf16[128,256]{1,0:T(8,128)(2,1)S(1)}, u32[]{:S(2)}, u32[]{:S(2)}) collective-permute-start(bf16[128,256]{1,0:T(8,128)(2,1)S(1)} %collective-permute-done.7.refs_6_), channel_id=1, source_target_pairs={{0,16},{16,0},{1,17},{17,1},{2,18},{18,2},{3,19},{19,3},{4,20},{20... | collective-permute-start | bytes 196616 | tf_op jit(solution)/shard_map/gather_features/ppermute | solution.py:258
  29.5 9.2 %collective-permute-start.10 = (bf16[128,256]{1,0:T(8,128)(2,1)S(1)}, bf16[128,256]{1,0:T(8,128)(2,1)S(1)}, u32[]{:S(2)}, u32[]{:S(2)}) collective-permute-start(bf16[128,256]{1,0:T(8,128)(2,1)S(1)} %collective-permute-done.9.refs_8_), channel_id=1, source_target_pairs={{0,16},{16,0},{1,17},{17,1},{2,18},{18,2},{3,19},{19,3},{4,20},{20... | collective-permute-start | bytes 196616 | tf_op jit(solution)/shard_map/gather_features/ppermute | solution.py:258
  32.5 6.2 %collective-permute-start.15 = (bf16[128,256]{1,0:T(8,128)(2,1)S(1)}, bf16[128,256]{1,0:T(8,128)(2,1)S(1)}, u32[]{:S(2)}, u32[]{:S(2)}) collective-permute-start(bf16[128,256]{1,0:T(8,128)(2,1)S(1)} %collective-permute-done.11.refs_10_), channel_id=1, source_target_pairs={{0,2},{2,4},{4,6},{6,8},{8,10},{10,12},{12,14},{14,0},{1,3},{3,5},... | collective-permute-start | bytes 196616 | tf_op jit(solution)/shard_map/gather_features/ppermute | solution.py:263
  32.5 6.2 %collective-permute-start.12 = (bf16[128,256]{1,0:T(8,128)(2,1)S(1)}, bf16[128,256]{1,0:T(8,128)(2,1)S(1)}, u32[]{:S(2)}, u32[]{:S(2)}) collective-permute-start(bf16[128,256]{1,0:T(8,128)(2,1)S(1)} %collective-permute-done.11.refs_10_), channel_id=1, source_target_pairs={{0,16},{16,0},{1,17},{17,1},{2,18},{18,2},{3,19},{19,3},{4,20},{20... | collective-permute-start | bytes 196616 | tf_op jit(solution)/shard_map/gather_features/ppermute | solution.py:258
  33.3 5.4 %collective-permute-start.16 = (bf16[128,256]{1,0:T(8,128)(2,1)S(1)}, bf16[128,256]{1,0:T(8,128)(2,1)S(1)}, u32[]{:S(2)}, u32[]{:S(2)}) collective-permute-start(bf16[128,256]{1,0:T(8,128)(2,1)S(1)} %collective-permute-done.14.refs_13_), channel_id=1, source_target_pairs={{0,14},{2,0},{4,2},{6,4},{8,6},{10,8},{12,10},{14,12},{1,15},{3,1}... | collective-permute-start | bytes 196616 | tf_op jit(solution)/shard_map/gather_features/ppermute | solution.py:263
  97.8 27.8 %copy-start = (f32[2048]{0:T(1024)S(1)}, f32[2048]{0:T(1024)}, u32[]{:S(2)}) copy-start(f32[2048]{0:T(1024)} %param.9) | copy-start | bytes 24580

commit v6 on v5

--- a/solution.py
+++ b/solution.py
@@ -37,7 +37,7 @@
 
 
 def prepare_kernel(slots, own_hbm, tgt_hbm, *refs):
-    lists_hbm, whole_ref, held_ref, tgt_ref, info_ref, refs, sems = refs[:4], *refs[4:8], refs[8:-1], refs[-1]
+    lists_hbm, whole_ref, held_ref, near_ref, tgt_ref, info_ref, refs, sems = refs[:4], *refs[4:9], refs[9:-1], refs[-1]
     pairs = ((tgt_hbm, tgt_ref), (own_hbm, held_ref)) + tuple(zip(lists_hbm, refs))
     moves = [pltpu.make_async_copy(source, target, sems.at[n]) for n, (source, target) in enumerate(pairs)]
     for move in moves:
@@ -52,24 +52,27 @@
         info_ref[8 * flip + slots : 8 * flip + slots + 1, :blocks] = counts_ref[...].astype(jnp.float32)
     size = tgt_ref.shape[0]
     info = info_ref[...].astype(whole_ref.dtype)
+    near_ref[...] = info_ref[...]
     for part in range(whole_ref.shape[0]):
         whole_ref[part, :size, :] = tgt_ref[...]
         whole_ref[part, size:, :] = info
 
 
-def plan_kernel(stages, slots, room, rows_ref, src_hbm, tgt_hbm, plan_ref, src_log_ref, tgt_log_ref, src_ref,
-                tgt_ref, lists_ref, info_ref, sems):
-    moves = (pltpu.make_async_copy(src_hbm, src_ref, sems.at[0]), pltpu.make_async_copy(tgt_hbm, tgt_ref, sems.at[1]))
-    for move in moves:
-        move.start()
+def plan_kernel(stages, slots, room, flip, rows_ref, *refs):
     deep, side, core = lax.axis_index("z"), lax.axis_index("h"), lax.axis_index("c")
-    pair = (lax.axis_index("x") * 2 + lax.axis_index("l")) * 2
+    plan_ref, lists_ref, info_ref, sem = (refs[0], *refs[-3:]) if flip else (refs[2], *refs[-3:])
     lanes = lists_ref.shape[1]
-    size = rows_ref.shape[1] - 16
-    for flip in range(2):
-        rows = rows_ref[pair + (side + flip) % 2, size:, :lanes].astype(jnp.float32)
-        lists_ref[16 * flip : 16 * flip + 16, :] = rows.astype(jnp.int32)
-    fetch = pltpu.make_async_copy(lists_ref, info_ref, sems.at[2])
+    if flip:
+        pair = (lax.axis_index("x") * 2 + lax.axis_index("l")) * 2 + 1 - side
+        rows = rows_ref[pair, rows_ref.shape[1] - 16 :, :lanes].astype(jnp.float32)
+    else:
+        rows = rows_ref[:, :lanes]
+        for weight, out in zip(refs[:2], refs[3:5]):
+            place = core if out is refs[4] else side
+            for row in range(stages):
+                out[row : row + 1, :] = jnp.log2(weight[pl.ds(row * 2 + place, 1), :])
+    lists_ref[...] = rows.astype(jnp.int32)
+    fetch = pltpu.make_async_copy(lists_ref, info_ref, sem)
     fetch.start()
     fetch.wait()
     blocks = 2 * stages
@@ -89,25 +92,25 @@
             first = 8 * (place % 2)
             block = depth * 2 + (core + place % 2) % 2
             row = depth * 2 + side
-            for flip in range(2):
-
-                def add(slot, at, first=first, flip=flip, row=row, block=block, place=place):
-                    local = info_ref[16 * flip + first + slot, row]
-                    target = local - local % 2 + (side + flip) % 2
-                    put(at, block, target, target * blocks + block, block * blocks + target, place)
-                    return at + jnp.where(local % 2 == core, 1, 0)
-
-                total = lax.fori_loop(0, info_ref[16 * flip + first + slots, row], add, total)
+
+            def add(slot, at, first=first, row=row, block=block, place=place):
+                local = info_ref[first + slot, row]
+                target = local - local % 2 + (side + flip) % 2
+                put(at, block, target, target * blocks + block, block * blocks + target, place)
+                return at + jnp.where(local % 2 == core, 1, 0)
+
+            total = lax.fori_loop(0, info_ref[first + slots, row], add, total)
         for extra in range(UNROLL - 1):
             put(total + extra, 0, 0, spare, spare, 0)
         total = (total + UNROLL - 1) // UNROLL * UNROLL
         chunk += length
     plan_ref[FIELDS * room + len(PIECES)] = total // UNROLL
-    for move in moves:
-        move.wait()
-    for row in range(stages):
-        src_log_ref[row : row + 1, :] = jnp.log2(src_ref[pl.ds(row * 2 + side, 1), :])
-        tgt_log_ref[row : row + 1, :] = jnp.log2(tgt_ref[pl.ds(row * 2 + core, 1), :])
+
+
+def both(near_ref, far_ref, end, group):
+    count = near_ref[end]
+    lax.fori_loop(0, count, functools.partial(group, near_ref, 0), 0)
+    lax.fori_loop(0, far_ref[end], functools.partial(group, far_ref, count * UNROLL), 0)
 
 
 def clear(high_ref, total_ref):
@@ -151,7 +154,7 @@
         left, right, (((1,), (1,)), ((), ())), preferred_element_type=jnp.float32)
 
 
-def first_kernel(room, scale, piece, plan_ref, tgt_ref, *refs):
+def first_kernel(room, scale, piece, near_ref, far_ref, tgt_ref, *refs):
     count = 2 * PIECES[piece]
     features, refs = refs[:count], refs[count:]
     log_ref = earlier_ref = None
@@ -164,18 +167,18 @@
         held_ref[place] = ref[...]
     clear(high_ref, total_ref)
 
-    def group(step, carry):
+    def group(plan_ref, base, step, carry):
         for lane in range(UNROLL):
             at = step * UNROLL + lane
+            tile = base + at
             left, right = held_ref[plan_ref[4 * room + at]], tgt_ref[plan_ref[room + at], : held_ref.shape[1], :]
             flipped = matmul(right, left, scale)
-            flipped_ref[at] = flipped
-            scores_ref[at] = flipped.T
+            flipped_ref[tile] = flipped
+            scores_ref[tile] = flipped.T
             keep_stats(flipped, plan_ref[2 * room + at], high_ref, total_ref)
         return carry
 
-    bounds = FIELDS * room + piece
-    lax.fori_loop(plan_ref[bounds], plan_ref[bounds + 1], group, 0)
+    both(near_ref, far_ref, FIELDS * room + len(PIECES), group)
     local = local_lse(high_ref, total_ref, out_ref.shape[0])
     if piece:
         local = jnp.maximum(local, earlier_ref[...])
@@ -185,7 +188,7 @@
         copies(local, log_ref, out_ref)
 
 
-def pass_kernel(room, own, row, fresh, first, emit, plan_ref, parts_ref, weight_ref, scores_ref, *refs):
+def pass_kernel(room, own, row, fresh, first, emit, near_ref, far_ref, parts_ref, weight_ref, scores_ref, *refs):
     log_ref = weight_ref if first else None
     out_ref, refs = refs[0], refs[1:]
     if fresh:
@@ -209,14 +212,15 @@
         column_ref[block] = jnp.broadcast_to(turned[:, block : block + 1], column_ref.shape[1:])
     clear(high_ref, total_ref)
 
-    def group(step, carry):
+    def group(plan_ref, base, step, carry):
         for lane in range(UNROLL):
             at = step * UNROLL + lane
-            shifted = scores_ref[at] + column_ref[plan_ref[own * room + at]]
+            tile = base + at
+            shifted = scores_ref[tile] + column_ref[plan_ref[own * room + at]]
             keep_stats(shifted, plan_ref[row * room + at], high_ref, total_ref)
         return carry
 
-    lax.fori_loop(0, plan_ref[FIELDS * room + len(PIECES)], group, 0)
+    both(near_ref, far_ref, FIELDS * room + len(PIECES), group)
     local = local_lse(high_ref, total_ref, blocks)
     if not emit:
         copies(local, log_ref, out_ref)
@@ -268,20 +272,21 @@
     size, features = src_feat.shape
     stages = lax.axis_size("z")
     blocks = 2 * stages
-    held = -(-2 * blocks * slots // UNROLL) * UNROLL + len(PIECES) * UNROLL
+    held = -(-2 * blocks * slots // UNROLL) * UNROLL + 2 * UNROLL
     room = -(-held // 128) * 128
     scale = LOG2E / math.sqrt(features)
 
     lists = (cand.transpose(2, 1, 0), counts.T)
     across = tuple(swap(part, "c") for part in lists)
-    whole, own = pl.pallas_call(
+    whole, own, near = pl.pallas_call(
         functools.partial(prepare_kernel, slots),
         out_shape=(
             jax.ShapeDtypeStruct((blocks, size + 16, features), tgt_feat.dtype),
             pltpu.VMEM(src_feat.shape, src_feat.dtype),
+            pltpu.VMEM((16, features), jnp.float32),
         ),
         in_specs=[ANY] * 6,
-        out_specs=(VMEM, VMEM),
+        out_specs=(VMEM, VMEM, VMEM),
         scratch_shapes=[pltpu.VMEM(tgt_feat.shape, tgt_feat.dtype), pltpu.VMEM((16, features), jnp.float32)]
         + [pltpu.VMEM((slots, 1, blocks), jnp.int32), pltpu.VMEM((1, blocks), jnp.int32)] * 2
         + [pltpu.SemaphoreType.DMA((6,))],
@@ -300,17 +305,27 @@
         pairs += [along_z(up, 1), along_z(pairs[-1], -1)]
 
     half = jax.ShapeDtypeStruct((stages, size), jnp.float32)
+    listed = pltpu.SMEM(((FIELDS + 1) * room,), jnp.int32)
+    lists = [pltpu.VMEM((16, size), jnp.int32), pltpu.SMEM((16, size), jnp.int32), pltpu.SemaphoreType.DMA]
     plan, src_log, tgt_log = pl.pallas_call(
-        functools.partial(plan_kernel, stages, slots, room),
-        out_shape=(pltpu.SMEM(((FIELDS + 1) * room,), jnp.int32), half, half),
-        in_specs=[VMEM] + [ANY] * 2,
+        functools.partial(plan_kernel, stages, slots, room, 0),
+        out_shape=(listed, half, half),
+        in_specs=[VMEM] * 3,
         out_specs=(SMEM, VMEM, VMEM),
-        scratch_shapes=[pltpu.VMEM((blocks, size), jnp.float32)] * 2
-        + [pltpu.VMEM((32, size), jnp.int32), pltpu.SMEM((32, size), jnp.int32), pltpu.SemaphoreType.DMA((3,))],
+        scratch_shapes=lists,
         compiler_params=PARAMS,
-        name="plan",
-    )(target_rows, in_hbm(src_weight.reshape(blocks, size)), in_hbm(tgt_weight.reshape(blocks, size)))
-    plan = pltpu.with_memory_space_constraint(plan, pltpu.SMEM)
+        name="plan_near",
+    )(near, src_weight.reshape(blocks, size), tgt_weight.reshape(blocks, size))
+    plan_far = pl.pallas_call(
+        functools.partial(plan_kernel, stages, slots, room, 1),
+        out_shape=listed,
+        in_specs=[VMEM],
+        out_specs=SMEM,
+        scratch_shapes=lists,
+        compiler_params=PARAMS,
+        name="plan_far",
+    )(target_rows)
+    plan, plan_far = (pltpu.with_memory_space_constraint(part, pltpu.SMEM) for part in (plan, plan_far))
 
     tables = [pltpu.VMEM((blocks * blocks + 8, size), jnp.float32)] * 2
     tiles = pltpu.VMEM((held, size, size), jnp.float32)
@@ -324,14 +339,14 @@
         *scored, local = pl.pallas_call(
             functools.partial(first_kernel, room, scale, piece),
             out_shape=(tiles, tiles, out),
-            in_specs=[SMEM] + [VMEM] * (1 + len(some) + len(more)),
+            in_specs=[SMEM] * 2 + [VMEM] * (1 + len(some) + len(more)),
             out_specs=(VMEM, VMEM, VMEM),
             scratch_shapes=[pltpu.VMEM((len(some), size, features), src_feat.dtype)] + tables,
             input_output_aliases={given + 1: 0, given + 2: 1} if scored else {},
             compiler_params=PARAMS,
             cost_estimate=cost(5 * PIECES[piece]),
             name=name,
-        )(plan, target_rows, *some, *more)
+        )(plan, plan_far, target_rows, *some, *more)
         return scored, local
 
     (flipped, scores), parts = first_rows(0, pairs, None, (), parts_of(blocks + stages), [src_log], "scores_and_rows")
@@ -346,13 +361,13 @@
         return pl.pallas_call(
             functools.partial(pass_kernel, room, own, row, fresh, first, emit),
             out_shape=shapes,
-            in_specs=[SMEM, VMEM, VMEM, VMEM],
+            in_specs=[SMEM, SMEM, VMEM, VMEM, VMEM],
             out_specs=(VMEM,) * len(shapes),
             scratch_shapes=[pltpu.VMEM((blocks, size, size), jnp.float32)] + tables
             + [pltpu.VMEM((stages, size), jnp.float32)] * emit,
             compiler_params=PARAMS,
             name=name,
-        )(plan, parts, weights, pltpu.with_memory_space_constraint(tiles, pltpu.VMEM))
+        )(plan, plan_far, parts, weights, pltpu.with_memory_space_constraint(tiles, pltpu.VMEM))
 
     src_kept = tgt_kept = None
     for step in range(ITERS):

time: 127 us -> 128 us (level)
  local copies, waits for them, and re-layouts: 0.01 us -> 1.4 us
    all_to_all x3, blocking collectives: 48.7 us -> 45.4 us  [on_device(): parts = lax.all_to_all(parts, ROW_GROUP, 0, 0)]
    all_to_all x3, blocking collectives: 31.9 us -> 34.4 us  [on_device(): parts = lax.all_to_all(parts, LAST_GROUP if last else COLUMN_GROUP, 0, 0)]
    unnamed x2 -> x6, local copies, waits for them, and re-layouts: 0.01 us -> 1.4 us
    pallas_call x1 -> x2, Pallas kernels: 2.43 us -> 2.92 us  [the longest x1 1.5 us: on_device(): pl.pallas_call(functools.partial(plan_kernel, stages, slots, room, 0), ou...]
where the time goes in v6:
time: 128 us; the launch traced here: 127 us
  blocking collectives  79.7 us (62%)
  starting transfers between devices  27.8 us (22%)
  Pallas kernels  11.8 us (9%)
  waiting for transfers between devices  5.79 us (5%)
  local copies, waits for them, and re-layouts  1.4 us (1%)
    all_to_all x3, blocking collectives, on_device(): parts = lax.all_to_all(parts, ROW_GROUP, 0, 0)  45.4 us
    all_to_all x3, blocking collectives, on_device(): parts = lax.all_to_all(parts, LAST_GROUP if last else COLUMN_GROUP, 0, 0)  34.4 us
    ppermute x8, starting transfers between devices, along_z(): lax.ppermute(value, 'z', [(k, (k + by) % stages) for k in range(stages)])  12.1 us
    ppermute x9, starting transfers between devices, swap(): return lax.ppermute(value, axis, [(0, 1), (1, 0)])  8.97 us
    all_to_all x1, starting transfers between devices, on_device(): target_rows = lax.all_to_all(whole, COLUMN_GROUP, 0, 0)  6.76 us
    pallas_call x5, Pallas kernels, sweep(): pl.pallas_call(functools.partial(pass_kernel, room, own, row, fresh, firs...  4.87 us
    ppermute x8, waiting for transfers between devices, along_z(): lax.ppermute(value, 'z', [(k, (k + by) % stages) for k in range(stages)])  4.67 us
  transfers between devices with their start and end apart: 18, of which 4 were waited for; matrix products, arithmetic and copies ran while one was open for 0% of the time, Pallas kernels for 4%

profile of v6, /device:TPU:1, one launch (start us, length us, event | category | flops | bytes accessed | tf_op | source)
XLA Modules:
  0.0 127.3 jit_solution(16552827667554331572)
XLA Ops:
  0.6 3.3 %collective-permute-start.2 = (bf16[128,256]{1,0:T(8,128)(2,1)}, bf16[128,256]{1,0:T(8,128)(2,1)S(1)}, u32[]{:S(2)}, u32[]{:S(2)}) collective-permute-start(bf16[128,256]{1,0:T(8,128)(2,1)} %own_hbm.1), channel_id=1, source_target_pairs={{0,16},{16,0},{1,17},{17,1},{2,18},{18,2},{3,19},{19,3},{4,20},{20... | collective-permute-start | bytes 196616 | tf_op jit(solution)/shard_map/gather_features/ppermute | solution.py:262
  4.0 3.9 %collective-permute-start.4 = (bf16[128,256]{1,0:T(8,128)(2,1)}, bf16[128,256]{1,0:T(8,128)(2,1)S(1)}, u32[]{:S(2)}, u32[]{:S(2)}) collective-permute-start(bf16[128,256]{1,0:T(8,128)(2,1)} %own_hbm.1), channel_id=1, source_target_pairs={{0,14},{2,0},{4,2},{6,4},{8,6},{10,8},{12,10},{14,12},{1,15},{3,1}... | collective-permute-start | bytes 196616 | tf_op jit(solution)/shard_map/gather_features/ppermute | solution.py:267
  8.3 1.1 collective-permute-done.1.refs_3_
  9.4 2.1 %prepare.1 = (bf16[16,144,256]{2,1,0:T(8,128)(2,1)}, bf16[128,256]{1,0:T(8,128)(2,1)S(1)}, f32[16,256]{1,0:T(8,128)S(1)}) custom-call(bf16[128,256]{1,0:T(8,128)(2,1)} %own_hbm.1, bf16[128,256]{1,0:T(8,128)(2,1)} %tgt_hbm.1, s32[6,1,16]{2,1,0:T(1,128)} %bitcast.10, s32[1,16]{1,0:T(1,128)} %bitcast.12, s32[6,1,16]{2,1,0:T(1,128)S(1)} %collective-permute-done.refs_2_, ...), custom_call_target="tpu_custom_call" | custom-call | tf_op jit(solution)/shard_map/prepare/pallas_call | solution.py:281
  12.4 6.8 %all-to-all-start = ((bf16[16,144,256]{2,1,0:T(8,128)(2,1)}), bf16[16,144,256]{2,1,0:T(8,128)(2,1)S(1)}, u32[]{:S(2)}, u32[]{:S(2)}) async-start(bf16[16,144,256]{2,1,0:T(8,128)(2,1)} %get-tuple-element.24), calls=%async_computation | async-start | bytes 2359296 | tf_op jit(solution)/shard_map/gather_features/all_to_all | solution.py:299
  19.1 2.2 %collective-permute-start.9 = (bf16[128,256]{1,0:T(8,128)(2,1)S(1)}, bf16[128,256]{1,0:T(8,128)(2,1)S(1)}, u32[]{:S(2)}, u32[]{:S(2)}) collective-permute-start(bf16[128,256]{1,0:T(8,128)(2,1)S(1)} %collective-permute-done.4.refs_4_), channel_id=1, source_target_pairs={{0,14},{2,0},{4,2},{6,4},{8,6},{10,8},{12,10},{14,12},{1,15},{3,1}... | collective-permute-start | bytes 196616 | tf_op jit(solution)/shard_map/gather_features/ppermute | solution.py:267
  21.3 1.3 %collective-permute-done.9.refs_8_ = bf16[128,256]{1,0:T(8,128)(2,1)S(1)} collective-permute-done((bf16[128,256]{1,0:T(8,128)(2,1)S(1)}, bf16[128,256]{1,0:T(8,128)(2,1)S(1)}, u32[]{:S(2)}, u32[]{:S(2)}) %collective-permute-start.9) | collective-permute-done | bytes 65568 | tf_op jit(solution)/shard_map/gather_features/ppermute | solution.py:267
  22.7 3.0 %collective-permute-start.13 = (bf16[128,256]{1,0:T(8,128)(2,1)S(1)}, bf16[128,256]{1,0:T(8,128)(2,1)S(1)}, u32[]{:S(2)}, u32[]{:S(2)}) collective-permute-start(bf16[128,256]{1,0:T(8,128)(2,1)S(1)} %collective-permute-done.9.refs_8_), channel_id=1, source_target_pairs={{0,14},{2,0},{4,2},{6,4},{8,6},{10,8},{12,10},{14,12},{1,15},{3,1}... | collective-permute-start | bytes 196616 | tf_op jit(solution)/shard_map/gather_features/ppermute | solution.py:267
  25.7 1.9 %collective-permute-start.5 = (bf16[128,256]{1,0:T(8,128)(2,1)S(1)}, bf16[128,256]{1,0:T(8,128)(2,1)S(1)}, u32[]{:S(2)}, u32[]{:S(2)}) collective-permute-start(bf16[128,256]{1,0:T(8,128)(2,1)S(1)} %collective-permute-done.3.refs_2_), channel_id=1, source_target_pairs={{0,16},{16,0},{1,17},{17,1},{2,18},{18,2},{3,19},{19,3},{4,20},{20... | collective-permute-start | bytes 196616 | tf_op jit(solution)/shard_map/gather_features/ppermute | solution.py:262
  27.7 1.8 %collective-permute-start.14 = (bf16[128,256]{1,0:T(8,128)(2,1)S(1)}, bf16[128,256]{1,0:T(8,128)(2,1)S(1)}, u32[]{:S(2)}, u32[]{:S(2)}) collective-permute-start(bf16[128,256]{1,0:T(8,128)(2,1)S(1)} %collective-permute-done.13.refs_12_), channel_id=1, source_target_pairs={{0,16},{16,0},{1,17},{17,1},{2,18},{18,2},{3,19},{19,3},{4,20},{20... | collective-permute-start | bytes 196616 | tf_op jit(solution)/shard_map/gather_features/ppermute | solution.py:262
  30.0 2.5 %collective-permute-done.11.refs_10_ = bf16[128,256]{1,0:T(8,128)(2,1)S(1)} collective-permute-done((bf16[128,256]{1,0:T(8,128)(2,1)S(1)}, bf16[128,256]{1,0:T(8,128)(2,1)S(1)}, u32[]{:S(2)}, u32[]{:S(2)}) %collective-permute-start.11) | collective-permute-done | bytes 65568 | tf_op jit(solution)/shard_map/gather_features/ppermute | solution.py:267
  33.3 3.0 %collective-permute-start.16 = (bf16[128,256]{1,0:T(8,128)(2,1)S(1)}, bf16[128,256]{1,0:T(8,128)(2,1)S(1)}, u32[]{:S(2)}, u32[]{:S(2)}) collective-permute-start(bf16[128,256]{1,0:T(8,128)(2,1)S(1)} %collective-permute-done.14.refs_13_), channel_id=1, source_target_pairs={{0,14},{2,0},{4,2},{6,4},{8,6},{10,8},{12,10},{14,12},{1,15},{3,1}... | collective-permute-start | bytes 196616 | tf_op jit(solution)/shard_map/gather_features/ppermute | solution.py:267
  37.7 1.5 %plan_near.1 = (s32[1536]{0:T(1024)S(4)}, f32[8,128]{1,0:T(8,128)S(1)}, f32[8,128]{1,0:T(8,128)S(1)}) custom-call(f32[16,256]{1,0:T(8,128)S(1)} %get-tuple-element.21.rows_ref, f32[16,128]{1,0:T(8,128)S(1)} %bitcast.8, f32[16,128]{1,0:T(8,128)S(1)} %bitcast.6), custom_call_target="tpu_custom_call" | custom-call | tf_op jit(solution)/shard_map/plan_near/pallas_call | solution.py:310
  39.2 1.4 %plan_far.1.far_ref = s32[1536]{0:T(1024)S(4)} custom-call(bf16[16,144,256]{2,1,0:T(8,128)(2,1)S(1)} %all-to-all-done.rows_ref.tgt_ref), custom_call_target="tpu_custom_call" | custom-call | tf_op jit(solution)/shard_map/plan_far/pallas_call | solution.py:319
  40.7 1.3 %scores_and_rows.1 = (f32[208,128,128]{2,1,0:T(8,128)S(1)}, f32[208,128,128]{2,1,0:T(8,128)S(1)}, f32[16,24,128]{2,1,0:T(8,128)S(1)}) custom-call(s32[1536]{0:T(1024)S(4)} %get-tuple-element.22.near_ref, s32[1536]{0:T(1024)S(4)} %plan_far.1.far_ref, bf16[16,144,256]{2,1,0:T(8,128)(2,1)S(1)} %all-to-all-done.rows_ref.tgt_ref, ...), custom_call_target="tpu_custom_call" | custom-call | flops 335544320 | bytes 2621440 | tf_op jit(solution)/shard_map/scores_and_rows/pallas_call | solution.py:339
  42.0 18.6 %all_to_all.35.parts_ref = f32[16,24,128]{2,1,0:T(8,128)S(1)} all-to-all(f32[16,24,128]{2,1,0:T(8,128)S(1)} %get-tuple-element.30), channel_id=1, replica_groups=mesh['x'=4,'l'=2,'c'=2,'z'=8,'h'=2] {'z','c'}, dimensions={0} | all-to-all | bytes 393216 | tf_op jit(solution)/shard_map/exchange_rows/all_to_all | solution.py:378
  61.6 12.0 %all_to_all.36.parts_ref = f32[16,24,128]{2,1,0:T(8,128)S(1)} all-to-all(f32[16,24,128]{2,1,0:T(8,128)S(1)} %get-tuple-element.33), channel_id=1, replica_groups=mesh['x'=4,'l'=2,'c'=2,'z'=8,'h'=2] {'x','l','h'}, dimensions={0} | all-to-all | bytes 393216 | tf_op jit(solution)/shard_map/exchange_columns/all_to_all | solution.py:383
  73.5 1.0 rows.2
  74.5 13.0 %all_to_all.37.parts_ref = f32[16,16,128]{2,1,0:T(8,128)S(1)} all-to-all(f32[16,16,128]{2,1,0:T(8,128)S(1)} %get-tuple-element.35), channel_id=1, replica_groups=mesh['x'=4,'l'=2,'c'=2,'z'=8,'h'=2] {'z','c'}, dimensions={0} | all-to-all | bytes 262144 | tf_op jit(solution)/shard_map/exchange_rows/all_to_all | solution.py:378
  88.5 10.4 %all_to_all.38.parts_ref = f32[16,16,128]{2,1,0:T(8,128)S(1)} all-to-all(f32[16,16,128]{2,1,0:T(8,128)S(1)} %columns.4), channel_id=1, replica_groups=mesh['x'=4,'l'=2,'c'=2,'z'=8,'h'=2] {'x','l','h'}, dimensions={0} | all-to-all | bytes 262144 | tf_op jit(solution)/shard_map/exchange_columns/all_to_all | solution.py:383
  98.9 1.0 rows.3
  99.9 13.8 %all_to_all.39.parts_ref = f32[16,16,128]{2,1,0:T(8,128)S(1)} all-to-all(f32[16,16,128]{2,1,0:T(8,128)S(1)} %rows.3), channel_id=1, replica_groups=mesh['x'=4,'l'=2,'c'=2,'z'=8,'h'=2] {'z','c'}, dimensions={0} | all-to-all | bytes 262144 | tf_op jit(solution)/shard_map/exchange_rows/all_to_all | solution.py:378
  113.7 1.0 columns.5
  114.6 12.0 %all_to_all.40.parts_ref = f32[32,16,128]{2,1,0:T(8,128)S(1)} all-to-all(f32[32,16,128]{2,1,0:T(8,128)S(1)} %columns.5), channel_id=1, replica_groups=mesh['x'=4,'l'=2,'c'=2,'z'=8,'h'=2] {'x','l','c','h'}, dimensions={0} | all-to-all | bytes 524288 | tf_op jit(solution)/shard_map/exchange_columns/all_to_all | solution.py:383
  (34 shorter events, 6.8 us)
Async XLA Ops:
  0.6 10.9 %collective-permute-start.2 = (bf16[128,256]{1,0:T(8,128)(2,1)}, bf16[128,256]{1,0:T(8,128)(2,1)S(1)}, u32[]{:S(2)}, u32[]{:S(2)}) collective-permute-start(bf16[128,256]{1,0:T(8,128)(2,1)} %own_hbm.1), channel_id=1, source_target_pairs={{0,16},{16,0},{1,17},{17,1},{2,18},{18,2},{3,19},{19,3},{4,20},{20... | collective-permute-start | bytes 196616 | tf_op jit(solution)/shard_map/gather_features/ppermute | solution.py:262
  4.0 7.6 %collective-permute-start.4 = (bf16[128,256]{1,0:T(8,128)(2,1)}, bf16[128,256]{1,0:T(8,128)(2,1)S(1)}, u32[]{:S(2)}, u32[]{:S(2)}) collective-permute-start(bf16[128,256]{1,0:T(8,128)(2,1)} %own_hbm.1), channel_id=1, source_target_pairs={{0,14},{2,0},{4,2},{6,4},{8,6},{10,8},{12,10},{14,12},{1,15},{3,1}... | collective-permute-start | bytes 196616 | tf_op jit(solution)/shard_map/gather_features/ppermute | solution.py:267
  7.8 4.5 %collective-permute-start.3 = (bf16[128,256]{1,0:T(8,128)(2,1)}, bf16[128,256]{1,0:T(8,128)(2,1)S(1)}, u32[]{:S(2)}, u32[]{:S(2)}) collective-permute-start(bf16[128,256]{1,0:T(8,128)(2,1)} %own_hbm.1), channel_id=1, source_target_pairs={{0,2},{2,4},{4,6},{6,8},{8,10},{10,12},{12,14},{14,0},{1,3},{3,5},... | collective-permute-start | bytes 196616 | tf_op jit(solution)/shard_map/gather_features/ppermute | solution.py:267
  7.8 1.6 %collective-permute-start = (s32[6,1,16]{2,1,0:T(1,128)}, s32[6,1,16]{2,1,0:T(1,128)S(1)}, u32[]{:S(2)}, u32[]{:S(2)}) collective-permute-start(s32[6,1,16]{2,1,0:T(1,128)} %bitcast.9), channel_id=1, source_target_pairs={{0,16},{16,0},{1,17},{17,1},{2,18},{18,2},{3,19},{19,3},{4,20},{20... | collective-permute-start | bytes 1160 | tf_op jit(solution)/shard_map/ppermute | solution.py:262
  8.2 1.3 collective-permute-start.1
  12.4 26.8 %all-to-all-start = ((bf16[16,144,256]{2,1,0:T(8,128)(2,1)}), bf16[16,144,256]{2,1,0:T(8,128)(2,1)S(1)}, u32[]{:S(2)}, u32[]{:S(2)}) async-start(bf16[16,144,256]{2,1,0:T(8,128)(2,1)} %get-tuple-element.24), calls=%async_computation | async-start | bytes 2359296 | tf_op jit(solution)/shard_map/gather_features/all_to_all | solution.py:299
  19.1 3.6 %collective-permute-start.9 = (bf16[128,256]{1,0:T(8,128)(2,1)S(1)}, bf16[128,256]{1,0:T(8,128)(2,1)S(1)}, u32[]{:S(2)}, u32[]{:S(2)}) collective-permute-start(bf16[128,256]{1,0:T(8,128)(2,1)S(1)} %collective-permute-done.4.refs_4_), channel_id=1, source_target_pairs={{0,14},{2,0},{4,2},{6,4},{8,6},{10,8},{12,10},{14,12},{1,15},{3,1}... | collective-permute-start | bytes 196616 | tf_op jit(solution)/shard_map/gather_features/ppermute | solution.py:267
  21.3 6.2 %collective-permute-start.7 = (bf16[128,256]{1,0:T(8,128)(2,1)S(1)}, bf16[128,256]{1,0:T(8,128)(2,1)S(1)}, u32[]{:S(2)}, u32[]{:S(2)}) collective-permute-start(bf16[128,256]{1,0:T(8,128)(2,1)S(1)} %collective-permute-done.3.refs_2_), channel_id=1, source_target_pairs={{0,2},{2,4},{4,6},{6,8},{8,10},{10,12},{12,14},{14,0},{1,3},{3,5},... | collective-permute-start | bytes 196616 | tf_op jit(solution)/shard_map/gather_features/ppermute | solution.py:267
  22.7 5.0 %collective-permute-start.13 = (bf16[128,256]{1,0:T(8,128)(2,1)S(1)}, bf16[128,256]{1,0:T(8,128)(2,1)S(1)}, u32[]{:S(2)}, u32[]{:S(2)}) collective-permute-start(bf16[128,256]{1,0:T(8,128)(2,1)S(1)} %collective-permute-done.9.refs_8_), channel_id=1, source_target_pairs={{0,14},{2,0},{4,2},{6,4},{8,6},{10,8},{12,10},{14,12},{1,15},{3,1}... | collective-permute-start | bytes 196616 | tf_op jit(solution)/shard_map/gather_features/ppermute | solution.py:267
  25.7 3.9 %collective-permute-start.5 = (bf16[128,256]{1,0:T(8,128)(2,1)S(1)}, bf16[128,256]{1,0:T(8,128)(2,1)S(1)}, u32[]{:S(2)}, u32[]{:S(2)}) collective-permute-start(bf16[128,256]{1,0:T(8,128)(2,1)S(1)} %collective-permute-done.3.refs_2_), channel_id=1, source_target_pairs={{0,16},{16,0},{1,17},{17,1},{2,18},{18,2},{3,19},{19,3},{4,20},{20... | collective-permute-start | bytes 196616 | tf_op jit(solution)/shard_map/gather_features/ppermute | solution.py:262
  27.6 4.9 %collective-permute-start.11 = (bf16[128,256]{1,0:T(8,128)(2,1)S(1)}, bf16[128,256]{1,0:T(8,128)(2,1)S(1)}, u32[]{:S(2)}, u32[]{:S(2)}) collective-permute-start(bf16[128,256]{1,0:T(8,128)(2,1)S(1)} %collective-permute-done.7.refs_6_), channel_id=1, source_target_pairs={{0,2},{2,4},{4,6},{6,8},{8,10},{10,12},{12,14},{14,0},{1,3},{3,5},... | collective-permute-start | bytes 196616 | tf_op jit(solution)/shard_map/gather_features/ppermute | solution.py:267
  27.6 4.9 %collective-permute-start.6 = (bf16[128,256]{1,0:T(8,128)(2,1)S(1)}, bf16[128,256]{1,0:T(8,128)(2,1)S(1)}, u32[]{:S(2)}, u32[]{:S(2)}) collective-permute-start(bf16[128,256]{1,0:T(8,128)(2,1)S(1)} %collective-permute-done.4.refs_4_), channel_id=1, source_target_pairs={{0,16},{16,0},{1,17},{17,1},{2,18},{18,2},{3,19},{19,3},{4,20},{20... | collective-permute-start | bytes 196616 | tf_op jit(solution)/shard_map/gather_features/ppermute | solution.py:262
  27.7 5.6 %collective-permute-start.14 = (bf16[128,256]{1,0:T(8,128)(2,1)S(1)}, bf16[128,256]{1,0:T(8,128)(2,1)S(1)}, u32[]{:S(2)}, u32[]{:S(2)}) collective-permute-start(bf16[128,256]{1,0:T(8,128)(2,1)S(1)} %collective-permute-done.13.refs_12_), channel_id=1, source_target_pairs={{0,16},{16,0},{1,17},{17,1},{2,18},{18,2},{3,19},{19,3},{4,20},{20... | collective-permute-start | bytes 196616 | tf_op jit(solution)/shard_map/gather_features/ppermute | solution.py:262
  29.5 11.1 %collective-permute-start.8 = (bf16[128,256]{1,0:T(8,128)(2,1)S(1)}, bf16[128,256]{1,0:T(8,128)(2,1)S(1)}, u32[]{:S(2)}, u32[]{:S(2)}) collective-permute-start(bf16[128,256]{1,0:T(8,128)(2,1)S(1)} %collective-permute-done.7.refs_6_), channel_id=1, source_target_pairs={{0,16},{16,0},{1,17},{17,1},{2,18},{18,2},{3,19},{19,3},{4,20},{20... | collective-permute-start | bytes 196616 | tf_op jit(solution)/shard_map/gather_features/ppermute | solution.py:262
  29.5 11.1 %collective-permute-start.10 = (bf16[128,256]{1,0:T(8,128)(2,1)S(1)}, bf16[128,256]{1,0:T(8,128)(2,1)S(1)}, u32[]{:S(2)}, u32[]{:S(2)}) collective-permute-start(bf16[128,256]{1,0:T(8,128)(2,1)S(1)} %collective-permute-done.9.refs_8_), channel_id=1, source_target_pairs={{0,16},{16,0},{1,17},{17,1},{2,18},{18,2},{3,19},{19,3},{4,20},{20... | collective-permute-start | bytes 196616 | tf_op jit(solution)/shard_map/gather_features/ppermute | solution.py:262
  32.5 8.1 %collective-permute-start.15 = (bf16[128,256]{1,0:T(8,128)(2,1)S(1)}, bf16[128,256]{1,0:T(8,128)(2,1)S(1)}, u32[]{:S(2)}, u32[]{:S(2)}) collective-permute-start(bf16[128,256]{1,0:T(8,128)(2,1)S(1)} %collective-permute-done.11.refs_10_), channel_id=1, source_target_pairs={{0,2},{2,4},{4,6},{6,8},{8,10},{10,12},{12,14},{14,0},{1,3},{3,5},... | collective-permute-start | bytes 196616 | tf_op jit(solution)/shard_map/gather_features/ppermute | solution.py:267
  32.5 8.1 %collective-permute-start.12 = (bf16[128,256]{1,0:T(8,128)(2,1)S(1)}, bf16[128,256]{1,0:T(8,128)(2,1)S(1)}, u32[]{:S(2)}, u32[]{:S(2)}) collective-permute-start(bf16[128,256]{1,0:T(8,128)(2,1)S(1)} %collective-permute-done.11.refs_10_), channel_id=1, source_target_pairs={{0,16},{16,0},{1,17},{17,1},{2,18},{18,2},{3,19},{19,3},{4,20},{20... | collective-permute-start | bytes 196616 | tf_op jit(solution)/shard_map/gather_features/ppermute | solution.py:262
  33.3 7.4 %collective-permute-start.16 = (bf16[128,256]{1,0:T(8,128)(2,1)S(1)}, bf16[128,256]{1,0:T(8,128)(2,1)S(1)}, u32[]{:S(2)}, u32[]{:S(2)}) collective-permute-start(bf16[128,256]{1,0:T(8,128)(2,1)S(1)} %collective-permute-done.14.refs_13_), channel_id=1, source_target_pairs={{0,14},{2,0},{4,2},{6,4},{8,6},{10,8},{12,10},{14,12},{1,15},{3,1}... | collective-permute-start | bytes 196616 | tf_op jit(solution)/shard_map/gather_features/ppermute | solution.py:267
  36.3 0.7 copy-start
  37.0 0.7 copy-start.2
  98.9 27.7 %copy-start.1 = (f32[2048]{0:T(1024)S(1)}, f32[2048]{0:T(1024)}, u32[]{:S(2)}) copy-start(f32[2048]{0:T(1024)} %param.9) | copy-start | bytes 24580

commit v7 on v5

--- a/solution.py
+++ b/solution.py
@@ -10,7 +10,7 @@
 from jax.sharding import PartitionSpec as P
 
 ITERS = 3
-UNROLL = 8
+UNROLL = 16
 FIELDS = 5
 LOW = -1e30
 LN2 = math.log(2.0)

time: 127 us -> 126 us (level)
  blocking collectives: 80.7 us -> 79.4 us
    all_to_all x3, blocking collectives: 48.7 us -> 46.3 us  [on_device(): parts = lax.all_to_all(parts, ROW_GROUP, 0, 0)]
where the time goes in v7:
time: 126 us
  blocking collectives  79.4 us (63%)
  starting transfers between devices  27.8 us (22%)
  Pallas kernels  11.8 us (9%)
  waiting for transfers between devices  5.79 us (5%)
    all_to_all x3, blocking collectives, on_device(): parts = lax.all_to_all(parts, ROW_GROUP, 0, 0)  46.3 us
    all_to_all x3, blocking collectives, on_device(): parts = lax.all_to_all(parts, LAST_GROUP if last else COLUMN_GROUP, 0, 0)  33.2 us
    ppermute x8, starting transfers between devices, along_z(): lax.ppermute(value, 'z', [(k, (k + by) % stages) for k in range(stages)])  12 us
    ppermute x9, starting transfers between devices, swap(): return lax.ppermute(value, axis, [(0, 1), (1, 0)])  8.98 us
    all_to_all x1, starting transfers between devices, on_device(): target_rows = lax.all_to_all(whole, COLUMN_GROUP, 0, 0)  6.76 us
    pallas_call x5, Pallas kernels, sweep(): pl.pallas_call(functools.partial(pass_kernel, room, own, row, fresh, firs...  5.36 us
    ppermute x8, waiting for transfers between devices, along_z(): lax.ppermute(value, 'z', [(k, (k + by) % stages) for k in range(stages)])  4.67 us
    pallas_call x1, Pallas kernels, on_device(): pl.pallas_call(functools.partial(plan_kernel, stages, slots, room), out_s...  2.55 us
  transfers between devices with their start and end apart: 18, of which 4 were waited for; matrix products, arithmetic and copies ran while one was open for 0% of the time, Pallas kernels for 4%

profile of v7, /device:TPU:1, one launch (start us, length us, event | category | flops | bytes accessed | tf_op | source)
XLA Modules:
  0.0 125.6 jit_solution(14285794686843042899)
XLA Ops:
  0.6 3.3 %collective-permute-start.2 = (bf16[128,256]{1,0:T(8,128)(2,1)}, bf16[128,256]{1,0:T(8,128)(2,1)S(1)}, u32[]{:S(2)}, u32[]{:S(2)}) collective-permute-start(bf16[128,256]{1,0:T(8,128)(2,1)} %own_hbm.1), channel_id=1, source_target_pairs={{0,16},{16,0},{1,17},{17,1},{2,18},{18,2},{3,19},{19,3},{4,20},{20... | collective-permute-start | bytes 196616 | tf_op jit(solution)/shard_map/gather_features/ppermute | solution.py:258
  4.0 3.9 %collective-permute-start.4 = (bf16[128,256]{1,0:T(8,128)(2,1)}, bf16[128,256]{1,0:T(8,128)(2,1)S(1)}, u32[]{:S(2)}, u32[]{:S(2)}) collective-permute-start(bf16[128,256]{1,0:T(8,128)(2,1)} %own_hbm.1), channel_id=1, source_target_pairs={{0,14},{2,0},{4,2},{6,4},{8,6},{10,8},{12,10},{14,12},{1,15},{3,1}... | collective-permute-start | bytes 196616 | tf_op jit(solution)/shard_map/gather_features/ppermute | solution.py:263
  8.3 1.1 collective-permute-done.1.refs_3_
  9.4 2.1 %prepare.1 = (bf16[16,144,256]{2,1,0:T(8,128)(2,1)}, bf16[128,256]{1,0:T(8,128)(2,1)S(1)}) custom-call(bf16[128,256]{1,0:T(8,128)(2,1)} %own_hbm.1, bf16[128,256]{1,0:T(8,128)(2,1)} %tgt_hbm.1, s32[6,1,16]{2,1,0:T(1,128)} %bitcast.10, s32[1,16]{1,0:T(1,128)} %bitcast.12, s32[6,1,16]{2,1,0:T(1,128)S(1)} %collective-permute-done.refs_2_, ...), custom_call_target="tpu_custom_call" | custom-call | tf_op jit(solution)/shard_map/prepare/pallas_call | solution.py:277
  12.4 6.8 %all-to-all-start = ((bf16[16,144,256]{2,1,0:T(8,128)(2,1)}), bf16[16,144,256]{2,1,0:T(8,128)(2,1)S(1)}, u32[]{:S(2)}, u32[]{:S(2)}) async-start(bf16[16,144,256]{2,1,0:T(8,128)(2,1)} %get-tuple-element.21), calls=%async_computation | async-start | bytes 2359296 | tf_op jit(solution)/shard_map/gather_features/all_to_all | solution.py:294
  19.1 2.2 %collective-permute-start.9 = (bf16[128,256]{1,0:T(8,128)(2,1)S(1)}, bf16[128,256]{1,0:T(8,128)(2,1)S(1)}, u32[]{:S(2)}, u32[]{:S(2)}) collective-permute-start(bf16[128,256]{1,0:T(8,128)(2,1)S(1)} %collective-permute-done.4.refs_4_), channel_id=1, source_target_pairs={{0,14},{2,0},{4,2},{6,4},{8,6},{10,8},{12,10},{14,12},{1,15},{3,1}... | collective-permute-start | bytes 196616 | tf_op jit(solution)/shard_map/gather_features/ppermute | solution.py:263
  21.3 1.3 %collective-permute-done.9.refs_8_ = bf16[128,256]{1,0:T(8,128)(2,1)S(1)} collective-permute-done((bf16[128,256]{1,0:T(8,128)(2,1)S(1)}, bf16[128,256]{1,0:T(8,128)(2,1)S(1)}, u32[]{:S(2)}, u32[]{:S(2)}) %collective-permute-start.9) | collective-permute-done | bytes 65568 | tf_op jit(solution)/shard_map/gather_features/ppermute | solution.py:263
  22.7 3.0 %collective-permute-start.13 = (bf16[128,256]{1,0:T(8,128)(2,1)S(1)}, bf16[128,256]{1,0:T(8,128)(2,1)S(1)}, u32[]{:S(2)}, u32[]{:S(2)}) collective-permute-start(bf16[128,256]{1,0:T(8,128)(2,1)S(1)} %collective-permute-done.9.refs_8_), channel_id=1, source_target_pairs={{0,14},{2,0},{4,2},{6,4},{8,6},{10,8},{12,10},{14,12},{1,15},{3,1}... | collective-permute-start | bytes 196616 | tf_op jit(solution)/shard_map/gather_features/ppermute | solution.py:263
  25.7 1.9 %collective-permute-start.5 = (bf16[128,256]{1,0:T(8,128)(2,1)S(1)}, bf16[128,256]{1,0:T(8,128)(2,1)S(1)}, u32[]{:S(2)}, u32[]{:S(2)}) collective-permute-start(bf16[128,256]{1,0:T(8,128)(2,1)S(1)} %collective-permute-done.3.refs_2_), channel_id=1, source_target_pairs={{0,16},{16,0},{1,17},{17,1},{2,18},{18,2},{3,19},{19,3},{4,20},{20... | collective-permute-start | bytes 196616 | tf_op jit(solution)/shard_map/gather_features/ppermute | solution.py:258
  27.7 1.8 %collective-permute-start.14 = (bf16[128,256]{1,0:T(8,128)(2,1)S(1)}, bf16[128,256]{1,0:T(8,128)(2,1)S(1)}, u32[]{:S(2)}, u32[]{:S(2)}) collective-permute-start(bf16[128,256]{1,0:T(8,128)(2,1)S(1)} %collective-permute-done.13.refs_12_), channel_id=1, source_target_pairs={{0,16},{16,0},{1,17},{17,1},{2,18},{18,2},{3,19},{19,3},{4,20},{20... | collective-permute-start | bytes 196616 | tf_op jit(solution)/shard_map/gather_features/ppermute | solution.py:258
  30.0 2.5 %collective-permute-done.11.refs_10_ = bf16[128,256]{1,0:T(8,128)(2,1)S(1)} collective-permute-done((bf16[128,256]{1,0:T(8,128)(2,1)S(1)}, bf16[128,256]{1,0:T(8,128)(2,1)S(1)}, u32[]{:S(2)}, u32[]{:S(2)}) %collective-permute-start.11) | collective-permute-done | bytes 65568 | tf_op jit(solution)/shard_map/gather_features/ppermute | solution.py:263
  33.3 3.0 %collective-permute-start.16 = (bf16[128,256]{1,0:T(8,128)(2,1)S(1)}, bf16[128,256]{1,0:T(8,128)(2,1)S(1)}, u32[]{:S(2)}, u32[]{:S(2)}) collective-permute-start(bf16[128,256]{1,0:T(8,128)(2,1)S(1)} %collective-permute-done.14.refs_13_), channel_id=1, source_target_pairs={{0,14},{2,0},{4,2},{6,4},{8,6},{10,8},{12,10},{14,12},{1,15},{3,1}... | collective-permute-start | bytes 196616 | tf_op jit(solution)/shard_map/gather_features/ppermute | solution.py:263
  36.3 2.6 %plan.1 = (s32[1536]{0:T(1024)S(4)}, f32[8,128]{1,0:T(8,128)S(1)}, f32[8,128]{1,0:T(8,128)S(1)}) custom-call(bf16[16,144,256]{2,1,0:T(8,128)(2,1)S(1)} %all-to-all-done.rows_ref.tgt_ref, f32[16,128]{1,0:T(8,128)} %bitcast.8, f32[16,128]{1,0:T(8,128)} %bitcast.6), custom_call_target="tpu_custom_call" | custom-call | tf_op jit(solution)/shard_map/plan/pallas_call | solution.py:303
  38.9 1.2 scores_and_rows.1
  40.1 19.4 %all_to_all.35.parts_ref = f32[16,24,128]{2,1,0:T(8,128)S(1)} all-to-all(f32[16,24,128]{2,1,0:T(8,128)S(1)} %get-tuple-element.28), channel_id=1, replica_groups=mesh['x'=4,'l'=2,'c'=2,'z'=8,'h'=2] {'z','c'}, dimensions={0} | all-to-all | bytes 393216 | tf_op jit(solution)/shard_map/exchange_rows/all_to_all | solution.py:363
  59.5 1.1 columns.3
  60.6 10.9 %all_to_all.36.parts_ref = f32[16,24,128]{2,1,0:T(8,128)S(1)} all-to-all(f32[16,24,128]{2,1,0:T(8,128)S(1)} %get-tuple-element.31), channel_id=1, replica_groups=mesh['x'=4,'l'=2,'c'=2,'z'=8,'h'=2] {'x','l','h'}, dimensions={0} | all-to-all | bytes 393216 | tf_op jit(solution)/shard_map/exchange_columns/all_to_all | solution.py:368
  71.4 1.1 rows.2
  72.5 13.7 %all_to_all.37.parts_ref = f32[16,16,128]{2,1,0:T(8,128)S(1)} all-to-all(f32[16,16,128]{2,1,0:T(8,128)S(1)} %get-tuple-element.33), channel_id=1, replica_groups=mesh['x'=4,'l'=2,'c'=2,'z'=8,'h'=2] {'z','c'}, dimensions={0} | all-to-all | bytes 262144 | tf_op jit(solution)/shard_map/exchange_rows/all_to_all | solution.py:363
  86.3 1.1 columns.4
  87.3 10.2 %all_to_all.38.parts_ref = f32[16,16,128]{2,1,0:T(8,128)S(1)} all-to-all(f32[16,16,128]{2,1,0:T(8,128)S(1)} %columns.4), channel_id=1, replica_groups=mesh['x'=4,'l'=2,'c'=2,'z'=8,'h'=2] {'x','l','h'}, dimensions={0} | all-to-all | bytes 262144 | tf_op jit(solution)/shard_map/exchange_columns/all_to_all | solution.py:368
  98.6 13.1 %all_to_all.39.parts_ref = f32[16,16,128]{2,1,0:T(8,128)S(1)} all-to-all(f32[16,16,128]{2,1,0:T(8,128)S(1)} %rows.3), channel_id=1, replica_groups=mesh['x'=4,'l'=2,'c'=2,'z'=8,'h'=2] {'z','c'}, dimensions={0} | all-to-all | bytes 262144 | tf_op jit(solution)/shard_map/exchange_rows/all_to_all | solution.py:363
  111.8 1.1 columns.5
  112.9 12.1 %all_to_all.40.parts_ref = f32[32,16,128]{2,1,0:T(8,128)S(1)} all-to-all(f32[32,16,128]{2,1,0:T(8,128)S(1)} %columns.5), channel_id=1, replica_groups=mesh['x'=4,'l'=2,'c'=2,'z'=8,'h'=2] {'x','l','c','h'}, dimensions={0} | all-to-all | bytes 524288 | tf_op jit(solution)/shard_map/exchange_columns/all_to_all | solution.py:368
  (29 shorter events, 4.5 us)
Async XLA Ops:
  0.6 10.9 %collective-permute-start.2 = (bf16[128,256]{1,0:T(8,128)(2,1)}, bf16[128,256]{1,0:T(8,128)(2,1)S(1)}, u32[]{:S(2)}, u32[]{:S(2)}) collective-permute-start(bf16[128,256]{1,0:T(8,128)(2,1)} %own_hbm.1), channel_id=1, source_target_pairs={{0,16},{16,0},{1,17},{17,1},{2,18},{18,2},{3,19},{19,3},{4,20},{20... | collective-permute-start | bytes 196616 | tf_op jit(solution)/shard_map/gather_features/ppermute | solution.py:258
  4.0 7.5 %collective-permute-start.4 = (bf16[128,256]{1,0:T(8,128)(2,1)}, bf16[128,256]{1,0:T(8,128)(2,1)S(1)}, u32[]{:S(2)}, u32[]{:S(2)}) collective-permute-start(bf16[128,256]{1,0:T(8,128)(2,1)} %own_hbm.1), channel_id=1, source_target_pairs={{0,14},{2,0},{4,2},{6,4},{8,6},{10,8},{12,10},{14,12},{1,15},{3,1}... | collective-permute-start | bytes 196616 | tf_op jit(solution)/shard_map/gather_features/ppermute | solution.py:263
  7.8 4.5 %collective-permute-start.3 = (bf16[128,256]{1,0:T(8,128)(2,1)}, bf16[128,256]{1,0:T(8,128)(2,1)S(1)}, u32[]{:S(2)}, u32[]{:S(2)}) collective-permute-start(bf16[128,256]{1,0:T(8,128)(2,1)} %own_hbm.1), channel_id=1, source_target_pairs={{0,2},{2,4},{4,6},{6,8},{8,10},{10,12},{12,14},{14,0},{1,3},{3,5},... | collective-permute-start | bytes 196616 | tf_op jit(solution)/shard_map/gather_features/ppermute | solution.py:263
  7.8 1.6 %collective-permute-start = (s32[6,1,16]{2,1,0:T(1,128)}, s32[6,1,16]{2,1,0:T(1,128)S(1)}, u32[]{:S(2)}, u32[]{:S(2)}) collective-permute-start(s32[6,1,16]{2,1,0:T(1,128)} %bitcast.9), channel_id=1, source_target_pairs={{0,16},{16,0},{1,17},{17,1},{2,18},{18,2},{3,19},{19,3},{4,20},{20... | collective-permute-start | bytes 1160 | tf_op jit(solution)/shard_map/ppermute | solution.py:258
  8.2 1.3 collective-permute-start.1
  12.4 23.9 %all-to-all-start = ((bf16[16,144,256]{2,1,0:T(8,128)(2,1)}), bf16[16,144,256]{2,1,0:T(8,128)(2,1)S(1)}, u32[]{:S(2)}, u32[]{:S(2)}) async-start(bf16[16,144,256]{2,1,0:T(8,128)(2,1)} %get-tuple-element.21), calls=%async_computation | async-start | bytes 2359296 | tf_op jit(solution)/shard_map/gather_features/all_to_all | solution.py:294
  19.1 3.5 %collective-permute-start.9 = (bf16[128,256]{1,0:T(8,128)(2,1)S(1)}, bf16[128,256]{1,0:T(8,128)(2,1)S(1)}, u32[]{:S(2)}, u32[]{:S(2)}) collective-permute-start(bf16[128,256]{1,0:T(8,128)(2,1)S(1)} %collective-permute-done.4.refs_4_), channel_id=1, source_target_pairs={{0,14},{2,0},{4,2},{6,4},{8,6},{10,8},{12,10},{14,12},{1,15},{3,1}... | collective-permute-start | bytes 196616 | tf_op jit(solution)/shard_map/gather_features/ppermute | solution.py:263
  21.3 6.2 %collective-permute-start.7 = (bf16[128,256]{1,0:T(8,128)(2,1)S(1)}, bf16[128,256]{1,0:T(8,128)(2,1)S(1)}, u32[]{:S(2)}, u32[]{:S(2)}) collective-permute-start(bf16[128,256]{1,0:T(8,128)(2,1)S(1)} %collective-permute-done.3.refs_2_), channel_id=1, source_target_pairs={{0,2},{2,4},{4,6},{6,8},{8,10},{10,12},{12,14},{14,0},{1,3},{3,5},... | collective-permute-start | bytes 196616 | tf_op jit(solution)/shard_map/gather_features/ppermute | solution.py:263
  22.7 5.0 %collective-permute-start.13 = (bf16[128,256]{1,0:T(8,128)(2,1)S(1)}, bf16[128,256]{1,0:T(8,128)(2,1)S(1)}, u32[]{:S(2)}, u32[]{:S(2)}) collective-permute-start(bf16[128,256]{1,0:T(8,128)(2,1)S(1)} %collective-permute-done.9.refs_8_), channel_id=1, source_target_pairs={{0,14},{2,0},{4,2},{6,4},{8,6},{10,8},{12,10},{14,12},{1,15},{3,1}... | collective-permute-start | bytes 196616 | tf_op jit(solution)/shard_map/gather_features/ppermute | solution.py:263
  25.7 3.9 %collective-permute-start.5 = (bf16[128,256]{1,0:T(8,128)(2,1)S(1)}, bf16[128,256]{1,0:T(8,128)(2,1)S(1)}, u32[]{:S(2)}, u32[]{:S(2)}) collective-permute-start(bf16[128,256]{1,0:T(8,128)(2,1)S(1)} %collective-permute-done.3.refs_2_), channel_id=1, source_target_pairs={{0,16},{16,0},{1,17},{17,1},{2,18},{18,2},{3,19},{19,3},{4,20},{20... | collective-permute-start | bytes 196616 | tf_op jit(solution)/shard_map/gather_features/ppermute | solution.py:258
  27.6 4.9 %collective-permute-start.11 = (bf16[128,256]{1,0:T(8,128)(2,1)S(1)}, bf16[128,256]{1,0:T(8,128)(2,1)S(1)}, u32[]{:S(2)}, u32[]{:S(2)}) collective-permute-start(bf16[128,256]{1,0:T(8,128)(2,1)S(1)} %collective-permute-done.7.refs_6_), channel_id=1, source_target_pairs={{0,2},{2,4},{4,6},{6,8},{8,10},{10,12},{12,14},{14,0},{1,3},{3,5},... | collective-permute-start | bytes 196616 | tf_op jit(solution)/shard_map/gather_features/ppermute | solution.py:263
  27.6 4.9 %collective-permute-start.6 = (bf16[128,256]{1,0:T(8,128)(2,1)S(1)}, bf16[128,256]{1,0:T(8,128)(2,1)S(1)}, u32[]{:S(2)}, u32[]{:S(2)}) collective-permute-start(bf16[128,256]{1,0:T(8,128)(2,1)S(1)} %collective-permute-done.4.refs_4_), channel_id=1, source_target_pairs={{0,16},{16,0},{1,17},{17,1},{2,18},{18,2},{3,19},{19,3},{4,20},{20... | collective-permute-start | bytes 196616 | tf_op jit(solution)/shard_map/gather_features/ppermute | solution.py:258
  27.7 5.6 %collective-permute-start.14 = (bf16[128,256]{1,0:T(8,128)(2,1)S(1)}, bf16[128,256]{1,0:T(8,128)(2,1)S(1)}, u32[]{:S(2)}, u32[]{:S(2)}) collective-permute-start(bf16[128,256]{1,0:T(8,128)(2,1)S(1)} %collective-permute-done.13.refs_12_), channel_id=1, source_target_pairs={{0,16},{16,0},{1,17},{17,1},{2,18},{18,2},{3,19},{19,3},{4,20},{20... | collective-permute-start | bytes 196616 | tf_op jit(solution)/shard_map/gather_features/ppermute | solution.py:258
  29.5 9.3 %collective-permute-start.8 = (bf16[128,256]{1,0:T(8,128)(2,1)S(1)}, bf16[128,256]{1,0:T(8,128)(2,1)S(1)}, u32[]{:S(2)}, u32[]{:S(2)}) collective-permute-start(bf16[128,256]{1,0:T(8,128)(2,1)S(1)} %collective-permute-done.7.refs_6_), channel_id=1, source_target_pairs={{0,16},{16,0},{1,17},{17,1},{2,18},{18,2},{3,19},{19,3},{4,20},{20... | collective-permute-start | bytes 196616 | tf_op jit(solution)/shard_map/gather_features/ppermute | solution.py:258
  29.5 9.3 %collective-permute-start.10 = (bf16[128,256]{1,0:T(8,128)(2,1)S(1)}, bf16[128,256]{1,0:T(8,128)(2,1)S(1)}, u32[]{:S(2)}, u32[]{:S(2)}) collective-permute-start(bf16[128,256]{1,0:T(8,128)(2,1)S(1)} %collective-permute-done.9.refs_8_), channel_id=1, source_target_pairs={{0,16},{16,0},{1,17},{17,1},{2,18},{18,2},{3,19},{19,3},{4,20},{20... | collective-permute-start | bytes 196616 | tf_op jit(solution)/shard_map/gather_features/ppermute | solution.py:258
  32.5 6.3 %collective-permute-start.15 = (bf16[128,256]{1,0:T(8,128)(2,1)S(1)}, bf16[128,256]{1,0:T(8,128)(2,1)S(1)}, u32[]{:S(2)}, u32[]{:S(2)}) collective-permute-start(bf16[128,256]{1,0:T(8,128)(2,1)S(1)} %collective-permute-done.11.refs_10_), channel_id=1, source_target_pairs={{0,2},{2,4},{4,6},{6,8},{8,10},{10,12},{12,14},{14,0},{1,3},{3,5},... | collective-permute-start | bytes 196616 | tf_op jit(solution)/shard_map/gather_features/ppermute | solution.py:263
  32.5 6.4 %collective-permute-start.12 = (bf16[128,256]{1,0:T(8,128)(2,1)S(1)}, bf16[128,256]{1,0:T(8,128)(2,1)S(1)}, u32[]{:S(2)}, u32[]{:S(2)}) collective-permute-start(bf16[128,256]{1,0:T(8,128)(2,1)S(1)} %collective-permute-done.11.refs_10_), channel_id=1, source_target_pairs={{0,16},{16,0},{1,17},{17,1},{2,18},{18,2},{3,19},{19,3},{4,20},{20... | collective-permute-start | bytes 196616 | tf_op jit(solution)/shard_map/gather_features/ppermute | solution.py:258
  33.3 5.6 %collective-permute-start.16 = (bf16[128,256]{1,0:T(8,128)(2,1)S(1)}, bf16[128,256]{1,0:T(8,128)(2,1)S(1)}, u32[]{:S(2)}, u32[]{:S(2)}) collective-permute-start(bf16[128,256]{1,0:T(8,128)(2,1)S(1)} %collective-permute-done.14.refs_13_), channel_id=1, source_target_pairs={{0,14},{2,0},{4,2},{6,4},{8,6},{10,8},{12,10},{14,12},{1,15},{3,1}... | collective-permute-start | bytes 196616 | tf_op jit(solution)/shard_map/gather_features/ppermute | solution.py:263
  97.6 27.4 %copy-start = (f32[2048]{0:T(1024)S(1)}, f32[2048]{0:T(1024)}, u32[]{:S(2)}) copy-start(f32[2048]{0:T(1024)} %param.9) | copy-start | bytes 24580
